TPU v7x, 768 devices: a whole 4x8x12 slice. The times are simulated.
768 devices in a mesh: row: 32 (over z_lo, x, core), col: 24 (over y, z_hi).
Axes of the slice: x: 4, y: 8, z: 12 (z_hi: 3, z_lo: 4; z = z_hi * 4 + z_lo), core: 2. Of those that a mesh axis runs over, the one named last changes fastest.
Arguments:
- node_latents: bfloat16 [24576, 512], P(('row', 'col')), may hold values from -6 to 6
- edge_latents: bfloat16 [196608, 512], P(('row', 'col')), may hold values from -6 to 6
- edge_sender: int32 [196608], P(('row', 'col')), may hold values from 0 to 767
- edge_receiver: int32 [196608], P(('row', 'col')), may hold values from 0 to 1023, as said below
- edge_count: int32 [768, 32], P(('row', 'col')), may hold values from 1 to 8, as said below
- w_in: bfloat16 [1536, 512], replicated, may hold values from -0.15625 to 0.15625
- b_in: float32 [512], replicated, may hold values from -4 to 4
- w_out: bfloat16 [512, 512], replicated, may hold values from -0.25 to 0.25
- b_out: float32 [512], replicated, may hold values from -4 to 4
- ln_gain: float32 [512], replicated, may hold values from 0.5 to 1.5
- ln_bias: float32 [512], replicated, may hold values from -3 to 3
- agg_cotangent: bfloat16 [24576, 512], P(('row', 'col')), may hold values from -6 to 6
- edge_cotangent: bfloat16 [196608, 512], P(('row', 'col')), may hold values from -6 to 6
Outputs:
- new_edges: bfloat16 [196608, 512], P(('row', 'col'))
- aggregated: bfloat16 [24576, 512], P(('row', 'col'))
- grad_nodes: bfloat16 [24576, 512], P(('row', 'col'))
- grad_edges: bfloat16 [196608, 512], P(('row', 'col'))
Inputs may be any that keep to these rules, and one draw needn't show every extreme that they name: `edge_receiver`: on every device, slots of receiver block b name receivers in b * 32 to (b + 1) * 32 - 1, non-decreasing within the block. `edge_count`: every device has a receiver block with exactly 8 live slots.
All inputs are finite; a program needn't handle non-finite values.
Results may differ from a plain program's by a relative error of at most 0.009.
Values may be sent and summed in bfloat16 or wider, within the bound.
No kernel may reach another device: no remote copies, remote signals or barrier semaphores. Data moves between devices by JAX's collectives and lax.ppermute only.
A program may use at most 32 MiB of HBM per device.

v0:
```python
import jax
import jax.numpy as jnp
from jax import lax
from jax.sharding import PartitionSpec as P


def edge_pass(
    edges, send_feat, recv_feat, live, cotangent, w_in, b_in, w_out, b_out, ln_gain, ln_bias
):
    joined = jnp.concatenate([edges, send_feat, recv_feat], axis=1)
    pre_act = jnp.dot(joined, w_in, preferred_element_type=jnp.float32) + b_in
    hidden = jax.nn.silu(pre_act).astype(jnp.bfloat16)
    outer = jnp.dot(hidden, w_out, preferred_element_type=jnp.float32) + b_out
    center = outer - jnp.mean(outer, axis=1, keepdims=True)
    inv_std = lax.rsqrt(jnp.mean(center * center, axis=1, keepdims=True) + 1e-05)
    normed = center * inv_std
    message = jnp.where(live[:, None], normed * ln_gain + ln_bias, 0.0).astype(jnp.bfloat16)
    new_edges = (edges.astype(jnp.float32) + message.astype(jnp.float32)).astype(jnp.bfloat16)
    cot = jnp.where(live[:, None], cotangent, 0.0)
    scaled = cot * ln_gain
    d_outer = inv_std * (
        scaled
        - jnp.mean(scaled, axis=1, keepdims=True)
        - normed * jnp.mean(scaled * normed, axis=1, keepdims=True)
    )
    d_outer = d_outer.astype(jnp.bfloat16)
    d_hidden = lax.dot_general(
        d_outer, w_out, (((1,), (1,)), ((), ())), preferred_element_type=jnp.float32
    )
    sigma = jax.nn.sigmoid(pre_act)
    d_pre = (d_hidden * sigma * (1.0 + pre_act * (1.0 - sigma))).astype(jnp.bfloat16)
    d_in = lax.dot_general(
        d_pre, w_in, (((1,), (1,)), ((), ())), preferred_element_type=jnp.float32
    )
    width = edges.shape[1]
    d_edge = d_in[:, :width]
    d_send = d_in[:, width : 2 * width].astype(jnp.bfloat16)
    d_recv = d_in[:, 2 * width :].astype(jnp.bfloat16)
    return (message, new_edges, d_edge, d_send, d_recv)


def on_device(
    node_latents,
    edge_latents,
    edge_sender,
    edge_receiver,
    edge_count,
    w_in,
    b_in,
    w_out,
    b_out,
    ln_gain,
    ln_bias,
    agg_cotangent,
    edge_cotangent,
):
    owned = node_latents.shape[0]
    width = node_latents.shape[1]
    slots = edge_latents.shape[0]
    blocks = lax.axis_size("row")
    per_block = slots // blocks
    sender_group = lax.all_gather(node_latents, "col", axis=0, tiled=True)
    receiver_group, receiver_cot = (
        lax.all_gather(node_latents, "row", axis=0, tiled=True),
        lax.all_gather(agg_cotangent, "row", axis=0, tiled=True),
    )
    slot_ids = jnp.arange(slots, dtype=jnp.int32)
    block_ids = slot_ids // per_block
    counts = edge_count[0]
    limit = jnp.sum(
        jnp.where(
            block_ids[:, None] == jnp.arange(blocks, dtype=jnp.int32)[None, :], counts[None, :], 0
        ),
        axis=1,
    )
    live = slot_ids % per_block < limit
    send_feat = jnp.take(sender_group, edge_sender, axis=0)
    recv_feat = jnp.take(receiver_group, edge_receiver, axis=0)
    cotangent = edge_cotangent.astype(jnp.float32) + jnp.take(
        receiver_cot, edge_receiver, axis=0
    ).astype(jnp.float32)
    message, new_edges, d_edge, d_send, d_recv = edge_pass(
        edge_latents,
        send_feat,
        recv_feat,
        live,
        cotangent,
        w_in,
        b_in,
        w_out,
        b_out,
        ln_gain,
        ln_bias,
    )
    grad_edges = (edge_cotangent.astype(jnp.float32) + d_edge).astype(jnp.bfloat16)
    stacked = jnp.concatenate([message, d_recv], axis=1)
    targets = jnp.arange(owned * lax.axis_size("row"), dtype=jnp.int32)
    selector = (targets[:, None] == edge_receiver[None, :]).astype(jnp.bfloat16)
    summed = lax.psum_scatter(
        jnp.dot(selector, stacked, preferred_element_type=jnp.float32),
        "row",
        scatter_dimension=0,
        tiled=True,
    )
    agg_sum = summed[:, :width]
    recv_sum = summed[:, width:]
    targets = jnp.arange(owned * lax.axis_size("col"), dtype=jnp.int32)
    selector = (targets[:, None] == edge_sender[None, :]).astype(jnp.bfloat16)
    send_sum = lax.psum_scatter(
        jnp.dot(selector, d_send, preferred_element_type=jnp.float32).astype(jnp.bfloat16),
        "col",
        scatter_dimension=0,
        tiled=True,
    ).astype(jnp.float32)
    aggregated = agg_sum.astype(jnp.bfloat16)
    grad_nodes = (recv_sum + send_sum).astype(jnp.bfloat16)
    return (new_edges, aggregated, grad_nodes, grad_edges)


def solution(mesh):
    return jax.shard_map(
        on_device,
        mesh=mesh,
        in_specs=(
            P(("row", "col"), None),
            P(("row", "col"), None),
            P(("row", "col")),
            P(("row", "col")),
            P(("row", "col"), None),
            P(),
            P(),
            P(),
            P(),
            P(),
            P(),
            P(("row", "col"), None),
            P(("row", "col"), None),
        ),
        out_specs=(
            P(("row", "col"), None),
            P(("row", "col"), None),
            P(("row", "col"), None),
            P(("row", "col"), None),
        ),
        check_vma=False,
    )
```

profile of v0, /device:TPU:1, one launch (start us, length us, event | category | flops | bytes accessed | tf_op | source)
XLA Modules:
  0.0 825.7 jit_solution(15211871183966718271)
XLA Ops:
  7.2 0.0 copy-start
  7.2 0.0 all-gather.3.cloned.1.call-start
  7.2 0.7 all-gather.3.cloned.1.call-update
  7.9 0.0 all-gather.5.cloned.1.call-start
  8.0 0.7 all-gather.5.cloned.1.call-update
  8.7 0.0 reduce-scatter.3.cloned.1.call-start
  8.7 0.7 compare_and_fusion
  9.4 0.7 compare_select_fusion
  10.1 82.8 %all_gather.9 = bf16[768,512]{1,0:T(8,128)(2,1)S(1)} all-gather(bf16[32,512]{1,0:T(8,128)(2,1)} %param.15), channel_id=1, replica_groups=mesh['row'=32,'col'=24] {'col'}, dimensions={0}, use_global_device_ids=true | all-gather | bytes 819200 | tf_op jit(solution)/shard_map/all_gather | solution.py:62
  92.9 0.7 compare_select_fusion.1
  93.6 0.7 select_reduce_fusion
  94.3 1.2 gather_fusion
  95.5 0.0 copy-done.4
  95.5 0.1 broadcast_select_fusion.2
  95.6 0.0 copy-start.2
  95.6 0.0 copy-start.8
  95.6 0.0 all-gather.3.cloned.1.call-done
  95.7 2.6 gather_fusion.1
  98.3 0.1 broadcast_select_fusion.1
  98.4 0.0 copy-done
  98.4 0.0 copy-done.2
  98.4 0.0 copy-done.8
  98.4 0.0 copy-start.7
  98.4 0.0 copy-start.9
  98.4 0.6 convolution_add_fusion
  99.0 0.4 copy-done.7
  99.5 0.0 copy-done.9
  99.5 0.4 fusion.47
  99.9 0.4 copy-done.10
  100.3 0.2 multiply_reduce_fusion.1
  100.5 51.7 %all-gather.5.cloned.1.call-done = bf16[1024,512]{1,0:T(8,128)(2,1)} async-done(((bf16[32,512]{1,0:T(8,128)(2,1)}), bf16[1024,512]{1,0:T(8,128)(2,1)}) %all-gather.5.cloned.1.call-update) | async-done | bytes 1048592 | tf_op jit(solution)/shard_map/all_gather | solution.py:65
  152.2 2.6 gather_fusion.2
  154.8 0.0 copy-done.1
  154.8 0.0 copy-done.5
  154.8 0.0 copy-done.6
  154.8 1.1 fusion.20
  155.9 3.7 fusion.48
  159.6 1.0 slice.29
  160.5 2.7 fusion.3
  163.2 0.0 reduce-scatter.3.cloned.1.call-update
  163.2 0.0 reduce-scatter.5.cloned.1.call-start
  163.3 2.2 convolution_convert_fusion
  165.5 0.0 reduce-scatter.5.cloned.1.call-update
  165.5 1.8 fusion.11
  167.3 146.7 %reduce-scatter.3.cloned.1.call-done = f32[32,1024]{1,0:T(8,128)} async-done(((f32[1024,1024]{1,0:T(8,128)}), f32[32,1024]{1,0:T(8,128)}) %reduce-scatter.3.cloned.1.call-update) | async-done | bytes 131088 | tf_op jit(solution)/shard_map/reduce_scatter | solution.py:99
  314.1 1.5 slice.41
  315.5 502.2 %reduce-scatter.5.cloned.1.call-done = bf16[32,512]{1,0:T(8,128)(2,1)} async-done(((bf16[768,512]{1,0:T(8,128)(2,1)}), bf16[32,512]{1,0:T(8,128)(2,1)}) %reduce-scatter.5.cloned.1.call-update) | async-done | bytes 32784 | tf_op jit(solution)/shard_map/reduce_scatter | solution.py:109
  817.7 1.5 fusion.38
  (15 shorter events, 0.1 us)
Async XLA Ops:
  7.2 91.2 %copy-start = (bf16[1536,512]{1,0:T(8,128)(2,1)S(1)}, bf16[1536,512]{1,0:T(8,128)(2,1)}, u32[]{:S(2)}) copy-start(bf16[1536,512]{1,0:T(8,128)(2,1)} %param.20) | copy-start | bytes 4718596
  7.2 88.5 %all-gather.3.cloned.1.call-start = ((), (), s32[]{:S(2)}) async-start(), calls=%async_computation.2 | async-start | bytes 1081344 | tf_op jit(solution)/shard_map/all_gather | solution.py:64
  7.9 144.3 %all-gather.5.cloned.1.call-start = ((), (), s32[]{:S(2)}) async-start(), calls=%async_computation.3 | async-start | bytes 1081344 | tf_op jit(solution)/shard_map/all_gather | solution.py:65
  8.7 305.4 %reduce-scatter.3.cloned.1.call-start = ((), (), s32[]{:S(2)}) async-start(), calls=%async_computation.4 | async-start | bytes 4325376 | tf_op jit(solution)/shard_map/reduce_scatter | solution.py:99
  10.1 85.4 %copy-start.4 = (s32[256]{0:T(256)S(1)}, s32[256]{0:T(256)}, u32[]{:S(2)}) copy-start(s32[256]{0:T(256)} %param.17) | copy-start | bytes 3076
  95.6 2.8 copy-start.2
  95.6 2.8 copy-start.8
  98.4 1.0 copy-start.7
  98.4 1.0 copy-start.9
  99.5 0.8 copy-start.10
  100.3 54.5 %copy-start.1 = (bf16[256,512]{1,0:T(8,128)(2,1)S(1)}, bf16[256,512]{1,0:T(8,128)(2,1)}, u32[]{:S(2)}) copy-start(bf16[256,512]{1,0:T(8,128)(2,1)} %param.27) | copy-start | bytes 786436
  100.3 54.5 %copy-start.5 = (f32[512]{0:T(512)S(1)}, f32[512]{0:T(512)}, u32[]{:S(2)}) copy-start(f32[512]{0:T(512)} %param.25) | copy-start | bytes 6148
  100.3 54.5 %copy-start.6 = (f32[512]{0:T(512)S(1)}, f32[512]{0:T(512)}, u32[]{:S(2)}) copy-start(f32[512]{0:T(512)} %param.24) | copy-start | bytes 6148
  155.9 4.7 copy-start.3
  163.2 654.5 %reduce-scatter.5.cloned.1.call-start = ((), (), s32[]{:S(2)}) async-start(), calls=%async_computation.5 | async-start | bytes 819200 | tf_op jit(solution)/shard_map/reduce_scatter | solution.py:109
Sparse Core Ops, SparseCore 0:
  10.5 77.4 all-gather.2
  90.4 61.7 all-gather.4
  163.3 150.6 reduce-scatter.2
  319.1 498.5 reduce-scatter.4
where the time goes:
time: 826 us
  waiting for transfers between devices  702 us (85%)
  blocking collectives  82.8 us (10%)
  between operations  13.9 us (2%)
  local copies, waits for them, and re-layouts  9.63 us (1%)
  matrix products  9.56 us (1%)
    reduce_scatter x1, waiting for transfers between devices, on_device(): lax.psum_scatter(jnp.dot(selector, d_send, preferred_element_type=jnp.flo...  502 us
    reduce_scatter x1, waiting for transfers between devices, on_device(): lax.psum_scatter(jnp.dot(selector, stacked, preferred_element_type=jnp.fl...  147 us
    all_gather x1, blocking collectives, on_device(): sender_group = lax.all_gather(node_latents, 'col', axis=0, tiled=True)  82.8 us
    all_gather x1, waiting for transfers between devices, on_device(): lax.all_gather(agg_cotangent, 'row', axis=0, tiled=True)  51.7 us
  transfers between devices with their start and end apart: 4, of which 3 were waited for; matrix products, arithmetic and copies ran while one was open for 2% of the time, Pallas kernels for 0%

commit v1 on v0

v1 whole, which is shorter than its diff:
```python
import functools

import jax
import jax.numpy as jnp
from jax import lax
from jax.experimental import pallas as pl
from jax.experimental.pallas import tpu as pltpu
from jax.sharding import PartitionSpec as P

Z_HI = 3


def dot(a, b):
    return jnp.dot(a, b, preferred_element_type=jnp.float32)


def dot_t(a, b):
    return lax.dot_general(a, b, (((1,), (1,)), ((), ())), preferred_element_type=jnp.float32)


def edge_kernel(
    edges, table, pick, spread, recv, live, edge_cot,
    w_in, b_in, w_out, b_out, gain, bias,
    new_edges, packed, partial,
):
    slots, width = edges.shape
    group = table.shape[0]
    lane = lax.broadcasted_iota(jnp.int32, (slots, group), 1)
    chosen = jnp.where(pick[...] == lane, 1.0, 0.0).astype(jnp.bfloat16)
    send_feat = dot(chosen, table[...]).astype(jnp.bfloat16)
    pre = dot(edges[...], w_in[:width, :])
    pre += dot(recv[:, :width], w_in[2 * width :, :])
    pre += dot(send_feat, w_in[width : 2 * width, :])
    pre += b_in[...]
    sigma = jax.nn.sigmoid(pre)
    hidden = (pre * sigma).astype(jnp.bfloat16)
    outer = dot(hidden, w_out[...]) + b_out[...]
    center = outer - jnp.mean(outer, axis=1, keepdims=True)
    inv_std = lax.rsqrt(jnp.mean(center * center, axis=1, keepdims=True) + 1e-05)
    normed = center * inv_std
    alive = live[...] > 0
    message = jnp.where(alive, normed * gain[...] + bias[...], 0.0).astype(jnp.bfloat16)
    packed[:, :width] = message
    new_edges[...] = (edges[...].astype(jnp.float32) + message.astype(jnp.float32)).astype(jnp.bfloat16)
    cot = edge_cot[...].astype(jnp.float32) + recv[:, width:].astype(jnp.float32)
    scaled = jnp.where(alive, cot, 0.0) * gain[...]
    d_outer = inv_std * (
        scaled
        - jnp.mean(scaled, axis=1, keepdims=True)
        - normed * jnp.mean(scaled * normed, axis=1, keepdims=True)
    )
    d_hidden = dot_t(d_outer.astype(jnp.bfloat16), w_out[...])
    d_pre = (d_hidden * sigma * (1.0 + pre * (1.0 - sigma))).astype(jnp.bfloat16)
    packed[:, width:] = d_pre
    row = lax.broadcasted_iota(jnp.int32, (group, slots), 0)
    placed = jnp.where(spread[...] == row, 1.0, 0.0).astype(jnp.bfloat16)
    partial[...] = dot(placed, d_pre).astype(jnp.bfloat16)


def on_device(
    node_latents,
    edge_latents,
    edge_sender,
    edge_receiver,
    edge_count,
    w_in,
    b_in,
    w_out,
    b_out,
    ln_gain,
    ln_bias,
    agg_cotangent,
    edge_cotangent,
):
    owned, width = node_latents.shape
    slots = edge_latents.shape[0]
    rows = lax.axis_size("row")
    cols = lax.axis_size("col")
    per_block = slots // rows
    tall = cols // Z_HI
    along_y = [[y * Z_HI + h for y in range(tall)] for h in range(Z_HI)]
    up = [(y * Z_HI + h, y * Z_HI + (h + 1) % Z_HI) for y in range(tall) for h in range(Z_HI)]
    down = [(b, a) for a, b in up]
    my_h = lax.axis_index("col") % Z_HI

    block_of = jnp.arange(slots, dtype=jnp.int32) // per_block
    wanted = (edge_receiver - block_of * owned).reshape(rows, per_block)
    asked = lax.all_to_all(wanted, "row", 0, 0, tiled=True).reshape(slots)
    onehot = (asked[:, None] == jnp.arange(owned, dtype=jnp.int32)[None, :]).astype(jnp.bfloat16)
    own = jnp.concatenate([node_latents, agg_cotangent], axis=1)
    answer = dot(onehot, own).astype(jnp.bfloat16)
    recv = lax.all_to_all(answer, "row", 0, 0, tiled=True)

    from_below = lax.ppermute(node_latents, "col", up)
    from_above = lax.ppermute(node_latents, "col", down)
    column = jnp.concatenate([node_latents, from_below, from_above], axis=0)
    table = lax.all_gather(column, "col", axis=0, tiled=True, axis_index_groups=along_y)

    device = edge_sender // owned
    turn = (my_h - device % Z_HI + Z_HI) % Z_HI
    place = ((device // Z_HI) * Z_HI + turn) * owned + edge_sender % owned
    live = (
        jnp.arange(per_block, dtype=jnp.int32)[None, :] < edge_count[0][:, None]
    ).astype(jnp.int32).reshape(slots, 1)

    vmem = pl.BlockSpec(memory_space=pltpu.VMEM)
    new_edges, packed, partial = pl.pallas_call(
        edge_kernel,
        in_specs=[vmem] * 13,
        out_specs=[vmem] * 3,
        out_shape=[
            jax.ShapeDtypeStruct((slots, width), jnp.bfloat16),
            jax.ShapeDtypeStruct((slots, 2 * width), jnp.bfloat16),
            jax.ShapeDtypeStruct((cols * owned, width), jnp.bfloat16),
        ],
        compiler_params=pltpu.CompilerParams(vmem_limit_bytes=40 * 1024 * 1024),
        cost_estimate=pl.CostEstimate(
            flops=2 * slots * width * (5 * width + 2 * cols * owned),
            bytes_accessed=6 * 1024 * 1024,
            transcendentals=slots * width,
        ),
    )(
        edge_latents, table, place.reshape(slots, 1), place.reshape(1, slots), recv, live,
        edge_cotangent, w_in, b_in.reshape(1, -1), w_out, b_out.reshape(1, -1),
        ln_gain.reshape(1, -1), ln_bias.reshape(1, -1),
    )

    parts = lax.all_to_all(partial, "col", 0, 0, tiled=True, axis_index_groups=along_y)
    column_sum = jnp.sum(parts.reshape(tall, Z_HI * owned, width).astype(jnp.float32), axis=0)
    away = column_sum.astype(jnp.bfloat16)
    to_below = lax.ppermute(away[owned : 2 * owned], "col", down)
    to_above = lax.ppermute(away[2 * owned :], "col", up)

    returned = lax.all_to_all(packed, "row", 0, 0, tiled=True)
    summed = lax.dot_general(
        onehot, returned, (((0,), (0,)), ((), ())), preferred_element_type=jnp.float32
    )
    send_sum = column_sum[:owned] + to_below.astype(jnp.float32) + to_above.astype(jnp.float32)
    grad_nodes = dot_t(summed[:, width:].astype(jnp.bfloat16), w_in[2 * width :]) + dot_t(
        send_sum.astype(jnp.bfloat16), w_in[width : 2 * width]
    )
    d_edge = dot_t(packed[:, width:], w_in[:width])
    grad_edges = (edge_cotangent.astype(jnp.float32) + d_edge).astype(jnp.bfloat16)
    return (
        new_edges,
        summed[:, :width].astype(jnp.bfloat16),
        grad_nodes.astype(jnp.bfloat16),
        grad_edges,
    )


def solution(mesh):
    split = P(("row", "col"), None)
    return jax.shard_map(
        on_device,
        mesh=mesh,
        in_specs=(
            split, split, P(("row", "col")), P(("row", "col")), split,
            P(), P(), P(), P(), P(), P(), split, split,
        ),
        out_specs=(split, split, split, split),
        check_vma=False,
    )
```

time: 826 us -> 136 us (0.16)
  waiting for transfers between devices: 702 us -> 12.8 us
  starting transfers between devices: 0.16 us -> 42.9 us
  blocking collectives: 82.8 us -> 63.6 us
  between operations: 13.9 us -> 0.9 us
    reduce_scatter x2 -> x0, waiting for transfers between devices: 649 us -> none  [the longest x1 502 us: on_device(): lax.psum_scatter(jnp.dot(selector, d_send, preferred_element_type=jnp.flo...]
    all_gather x1, blocking collectives: 82.8 us -> 22.4 us  [on_device(): lax.all_gather(column, 'col', axis=0, tiled=True, axis_index_groups=along_y)]
    all_gather x2 -> x0, waiting for transfers between devices: 51.7 us -> none  [the longest x1 51.7 us: on_device(): lax.all_gather(agg_cotangent, 'row', axis=0, tiled=True)]
    all_to_all x0 -> x2, blocking collectives: none -> 41.2 us  [the longest x1 20.7 us: on_device(): asked = lax.all_to_all(wanted, 'row', 0, 0, tiled=True).reshape(slots)]
    all_to_all x0 -> x2, starting transfers between devices: none -> 22.2 us  [the longest x1 18.1 us: on_device(): returned = lax.all_to_all(packed, 'row', 0, 0, tiled=True)]
    ppermute x0 -> x4, starting transfers between devices: none -> 20.6 us  [the longest x1 9.51 us: on_device(): from_above = lax.ppermute(node_latents, 'col', down)]
  transfers between devices with their start and end apart: 4 -> 6, of which waited for: 3 -> 2; matrix products, arithmetic and copies ran while one was open for 2% -> 3% of each run, Pallas kernels for 0% -> 0%
where the time goes in v1:
time: 136 us
  blocking collectives  63.6 us (47%)
  starting transfers between devices  42.9 us (32%)
  waiting for transfers between devices  12.8 us (9%)
  local copies, waits for them, and re-layouts  5.76 us (4%)
  matrix products  5.37 us (4%)
  Pallas kernels  2.58 us (2%)
  other arithmetic  1.62 us (1%)
    all_gather x1, blocking collectives, on_device(): lax.all_gather(column, 'col', axis=0, tiled=True, axis_index_groups=along_y)  22.4 us
    all_to_all x1, blocking collectives, on_device(): asked = lax.all_to_all(wanted, 'row', 0, 0, tiled=True).reshape(slots)  20.7 us
    all_to_all x1, blocking collectives, on_device(): lax.all_to_all(partial, 'col', 0, 0, tiled=True, axis_index_groups=along_y)  20.5 us
    all_to_all x1, starting transfers between devices, on_device(): returned = lax.all_to_all(packed, 'row', 0, 0, tiled=True)  18.1 us
    ppermute x1, starting transfers between devices, on_device(): from_above = lax.ppermute(node_latents, 'col', down)  9.51 us
    all_to_all x1, waiting for transfers between devices, on_device(): returned = lax.all_to_all(packed, 'row', 0, 0, tiled=True)  7.1 us
    ppermute x1, starting transfers between devices, on_device(): to_above = lax.ppermute(away[2 * owned:], 'col', up)  5.84 us
    ppermute x1, waiting for transfers between devices, on_device(): from_below = lax.ppermute(node_latents, 'col', up)  5.69 us
  transfers between devices with their start and end apart: 6, of which 2 were waited for; matrix products, arithmetic and copies ran while one was open for 3% of the time, Pallas kernels for 0%

profile of v1, /device:TPU:1, one launch (start us, length us, event | category | flops | bytes accessed | tf_op | source)
XLA Modules:
  0.0 135.5 jit_solution(13528749418086703494)
XLA Ops:
  0.6 0.0 copy-start.11
  0.6 0.0 copy-start.15
  0.7 0.0 copy-start.14
  0.7 0.7 fusion.23
  1.4 0.1 all_to_all.27
  1.5 0.0 copy-start.1
  1.5 0.0 copy-start.7
  1.5 0.0 copy-start.8
  1.5 0.0 copy-start.9
  1.5 20.7 %all_to_all.41 = s32[32,1,8]{2,1,0:T(1,128)S(1)} all-to-all(s32[32,1,8]{2,1,0:T(1,128)S(1)} %bitcast.25), channel_id=1, replica_groups=mesh['row'=32,'col'=24] {'row'}, dimensions={0} | all-to-all | bytes 2048 | tf_op jit(solution)/shard_map/all_to_all | solution.py:88
  22.2 0.5 broadcast.33
  22.7 0.7 reduce.3
  23.4 0.1 eq.21
  23.5 0.0 copy-start.12
  23.5 1.9 %fusion = bf16[32,8,1024]{2,1,0:T(8,128)(2,1)} fusion(bf16[32,512]{1,0:T(8,128)(2,1)} %param.24, bf16[32,512]{1,0:T(8,128)(2,1)} %param.13, s32[256]{0:T(256)S(1)} %eq.21), kind=kOutput, calls=%fused_computation.2 | convolution fusion | flops 17178624 | bytes 590848 | tf_op jit(solution)/shard_map/dot_general | solution.py:14
  25.4 0.0 copy-done.12
  25.4 4.2 %all-to-all-start.1 = ((bf16[32,8,1024]{2,1,0:T(8,128)(2,1)}), bf16[32,8,1024]{2,1,0:T(8,128)(2,1)S(1)}, u32[]{:S(2)}, u32[]{:S(2)}) async-start(bf16[32,8,1024]{2,1,0:T(8,128)(2,1)} %fusion), calls=%async_computation.1 | async-start | bytes 1048576 | tf_op jit(solution)/shard_map/all_to_all | solution.py:92
  29.6 0.0 copy-done.11
  29.6 9.5 %collective-permute-start.1 = (bf16[32,512]{1,0:T(8,128)(2,1)S(1)}, bf16[32,512]{1,0:T(8,128)(2,1)S(1)}, u32[]{:S(2)}, u32[]{:S(2)}) collective-permute-start(bf16[32,512]{1,0:T(8,128)(2,1)S(1)} %copy-done.11), channel_id=1, source_target_pairs={{1,0},{2,1},{0,2},{4,3},{5,4},{3,5},{7,6},{8,7},{6,8},{10,9},{11,1... | collective-permute-start | bytes 98312 | tf_op jit(solution)/shard_map/ppermute | solution.py:95
  39.1 1.9 %collective-permute-start = (bf16[32,512]{1,0:T(8,128)(2,1)S(1)}, bf16[32,512]{1,0:T(8,128)(2,1)S(1)}, u32[]{:S(2)}, u32[]{:S(2)}) collective-permute-start(bf16[32,512]{1,0:T(8,128)(2,1)S(1)} %copy-done.11), channel_id=1, source_target_pairs={{0,1},{1,2},{2,0},{3,4},{4,5},{5,3},{6,7},{7,8},{8,6},{9,10},{10,1... | collective-permute-start | bytes 98312 | tf_op jit(solution)/shard_map/ppermute | solution.py:94
  41.1 0.1 fusion.18
  41.2 0.0 copy-done.14
  41.2 0.1 reshape.76.live
  41.3 0.8 copy.20.pick
  42.1 0.0 collective-permute-done.1
  42.1 5.7 %collective-permute-done = bf16[32,512]{1,0:T(8,128)(2,1)S(1)} collective-permute-done((bf16[32,512]{1,0:T(8,128)(2,1)S(1)}, bf16[32,512]{1,0:T(8,128)(2,1)S(1)}, u32[]{:S(2)}, u32[]{:S(2)}) %collective-permute-start) | collective-permute-done | bytes 32800 | tf_op jit(solution)/shard_map/ppermute | solution.py:94
  47.8 22.4 %all_gather.3.table = bf16[768,512]{1,0:T(8,128)(2,1)S(1)} all-gather(bf16[96,512]{1,0:T(8,128)(2,1)S(1)} %pad_maximum_fusion), channel_id=1, replica_groups={{0,3,6,9,12,15,18,21},{1,4,7,10,13,16,19,22},{2,5,8,11,14,17,20,23},{24..., dimensions={0}, use_global_device_ids=true | all-gather | bytes 884736 | tf_op jit(solution)/shard_map/all_gather | solution.py:97
  70.2 0.0 all-to-all-done.1
  70.3 0.0 copy-start.2
  70.3 0.9 copy-done.2
  71.2 0.9 copy-done.4
  72.1 0.9 copy-done.5
  73.1 0.7 copy-done.10
  73.8 2.6 %shard_map.156 = (bf16[256,512]{1,0:T(8,128)(2,1)}, bf16[256,1024]{1,0:T(8,128)(2,1)S(1)}, bf16[768,512]{1,0:T(8,128)(2,1)S(1)}) custom-call(bf16[256,512]{1,0:T(8,128)(2,1)S(1)} %copy-done.4, bf16[768,512]{1,0:T(8,128)(2,1)S(1)} %all_gather.3.table, s32[256,1]{1,0:T(8,128)S(1)} %copy-done.2, s32[1,256]{1,0:T(1,128)S(1)} %bitcast.20, ...), custom_call_target="tpu_custom_call" | custom-call | flops 1073741824 | bytes 6291456 | tf_op jit(solution)/shard_map/pallas_call | solution.py:107
  76.3 20.5 %all_to_all.42 = bf16[8,96,512]{2,1,0:T(8,128)(2,1)S(1)} all-to-all(bf16[8,96,512]{2,1,0:T(8,128)(2,1)S(1)} %bitcast.17), channel_id=1, replica_groups={{0,3,6,9,12,15,18,21},{1,4,7,10,13,16,19,22},{2,5,8,11,14,17,20,23},{24..., dimensions={0} | all-to-all | bytes 1572864 | tf_op jit(solution)/shard_map/all_to_all | solution.py:128
  96.9 18.1 %all-to-all-start.2 = ((bf16[32,8,1024]{2,1,0:T(8,128)(2,1)}), bf16[32,8,1024]{2,1,0:T(8,128)(2,1)S(1)}, u32[]{:S(2)}, u32[]{:S(2)}) async-start(bf16[32,8,1024]{2,1,0:T(8,128)(2,1)} %bitcast.18), calls=%async_computation.2 | async-start | bytes 1048576 | tf_op jit(solution)/shard_map/all_to_all | solution.py:134
  114.9 0.0 copy-start.13
  115.0 2.0 %fusion.1 = bf16[256,512]{1,0:T(8,128)(2,1)} fusion(bf16[1536,512]{1,0:T(8,128)(2,1)S(1)} %copy-done, bf16[256,512]{1,0:T(8,128)(2,1)S(1)} %copy-done.6, bf16[256,1024]{1,0:T(8,128)(2,1)} %copy-done.3), kind=kOutput, calls=%fused_computation.4 | convolution fusion | flops 134610944 | bytes 1310720 | tf_op jit(solution)/shard_map/dot_general | solution.py:18
  117.0 0.1 convert_reduce_fusion
  117.1 3.4 %collective-permute-start.2 = (bf16[32,512]{1,0:T(8,128)(2,1)S(1)}, bf16[32,512]{1,0:T(8,128)(2,1)S(1)}, u32[]{:S(2)}, u32[]{:S(2)}) collective-permute-start(bf16[32,512]{1,0:T(8,128)(2,1)S(1)} %get-tuple-element.10), channel_id=1, source_target_pairs={{1,0},{2,1},{0,2},{4,3},{5,4},{3,5},{7,6},{8,7},{6,8},{10,9},{11,1... | collective-permute-start | bytes 98312 | tf_op jit(solution)/shard_map/ppermute | solution.py:131
  120.5 5.8 %collective-permute-start.3 = (bf16[32,512]{1,0:T(8,128)(2,1)S(1)}, bf16[32,512]{1,0:T(8,128)(2,1)S(1)}, u32[]{:S(2)}, u32[]{:S(2)}) collective-permute-start(bf16[32,512]{1,0:T(8,128)(2,1)S(1)} %get-tuple-element.11), channel_id=1, source_target_pairs={{0,1},{1,2},{2,0},{3,4},{4,5},{5,3},{6,7},{7,8},{8,6},{9,10},{10,1... | collective-permute-start | bytes 98312 | tf_op jit(solution)/shard_map/ppermute | solution.py:132
  126.3 7.1 %all-to-all-done.2 = bf16[32,8,1024]{2,1,0:T(8,128)(2,1)S(1)} async-done(((bf16[32,8,1024]{2,1,0:T(8,128)(2,1)}), bf16[32,8,1024]{2,1,0:T(8,128)(2,1)S(1)}, u32[]{:S(2)}, u32[]{:S(2)}) %all-to-all-start.2) | async-done | bytes 524320 | tf_op jit(solution)/shard_map/all_to_all | solution.py:134
  133.4 0.3 convolution_convert_fusion.1
  133.7 0.3 fusion.6
  134.0 0.6 slice.38
  134.6 0.0 collective-permute-done.2
  134.6 0.0 collective-permute-done.3
  134.6 0.9 fusion.2
  (19 shorter events, 0.1 us)
Async XLA Ops:
  0.6 29.0 %copy-start.11 = (bf16[32,512]{1,0:T(8,128)(2,1)S(1)}, bf16[32,512]{1,0:T(8,128)(2,1)}, u32[]{:S(2)}) copy-start(bf16[32,512]{1,0:T(8,128)(2,1)} %param.13) | copy-start | bytes 98308
  0.6 40.4 %copy-start.15 = (s32[1,32]{1,0:T(1,128)S(1)}, s32[1,32]{1,0:T(1,128)}, u32[]{:S(2)}) copy-start(s32[1,32]{1,0:T(1,128)} %param.17) | copy-start | bytes 388
  0.7 40.5 %copy-start.14 = (s32[256]{0:T(256)S(1)}, s32[256]{0:T(256)}, u32[]{:S(2)}) copy-start(s32[256]{0:T(256)} %param.15) | copy-start | bytes 3076
  1.4 68.8 %copy-start = (bf16[1536,512]{1,0:T(8,128)(2,1)S(1)}, bf16[1536,512]{1,0:T(8,128)(2,1)}, u32[]{:S(2)}) copy-start(bf16[1536,512]{1,0:T(8,128)(2,1)} %w_in.1) | copy-start | bytes 4718596
  1.5 68.8 %copy-start.1 = (bf16[512,512]{1,0:T(8,128)(2,1)S(1)}, bf16[512,512]{1,0:T(8,128)(2,1)}, u32[]{:S(2)}) copy-start(bf16[512,512]{1,0:T(8,128)(2,1)} %w_out.1) | copy-start | bytes 1572868
  1.5 68.8 %copy-start.7 = (f32[512]{0:T(512)S(1)}, f32[512]{0:T(512)}, u32[]{:S(2)}) copy-start(f32[512]{0:T(512)} %param.19) | copy-start | bytes 6148
  1.5 68.8 %copy-start.8 = (f32[512]{0:T(512)S(1)}, f32[512]{0:T(512)}, u32[]{:S(2)}) copy-start(f32[512]{0:T(512)} %param.21) | copy-start | bytes 6148
  1.5 68.8 %copy-start.9 = (f32[512]{0:T(512)S(1)}, f32[512]{0:T(512)}, u32[]{:S(2)}) copy-start(f32[512]{0:T(512)} %param.22) | copy-start | bytes 6148
  23.5 1.9 %copy-start.12 = (s32[256]{0:T(256)}, s32[256]{0:T(256)S(1)}, u32[]{:S(2)}) copy-start(s32[256]{0:T(256)S(1)} %eq.21) | copy-start | bytes 3076
  25.4 44.8 %all-to-all-start.1 = ((bf16[32,8,1024]{2,1,0:T(8,128)(2,1)}), bf16[32,8,1024]{2,1,0:T(8,128)(2,1)S(1)}, u32[]{:S(2)}, u32[]{:S(2)}) async-start(bf16[32,8,1024]{2,1,0:T(8,128)(2,1)} %fusion), calls=%async_computation.1 | async-start | bytes 1048576 | tf_op jit(solution)/shard_map/all_to_all | solution.py:92
  29.6 12.5 %collective-permute-start.1 = (bf16[32,512]{1,0:T(8,128)(2,1)S(1)}, bf16[32,512]{1,0:T(8,128)(2,1)S(1)}, u32[]{:S(2)}, u32[]{:S(2)}) collective-permute-start(bf16[32,512]{1,0:T(8,128)(2,1)S(1)} %copy-done.11), channel_id=1, source_target_pairs={{1,0},{2,1},{0,2},{4,3},{5,4},{3,5},{7,6},{8,7},{6,8},{10,9},{11,1... | collective-permute-start | bytes 98312 | tf_op jit(solution)/shard_map/ppermute | solution.py:95
  39.1 8.7 %collective-permute-start = (bf16[32,512]{1,0:T(8,128)(2,1)S(1)}, bf16[32,512]{1,0:T(8,128)(2,1)S(1)}, u32[]{:S(2)}, u32[]{:S(2)}) collective-permute-start(bf16[32,512]{1,0:T(8,128)(2,1)S(1)} %copy-done.11), channel_id=1, source_target_pairs={{0,1},{1,2},{2,0},{3,4},{4,5},{5,3},{6,7},{7,8},{8,6},{9,10},{10,1... | collective-permute-start | bytes 98312 | tf_op jit(solution)/shard_map/ppermute | solution.py:94
  70.3 0.9 copy-start.2
  71.2 0.9 copy-start.4
  72.1 0.9 copy-start.5
  73.1 0.7 copy-start.10
  76.3 20.5 %copy-start.3 = (bf16[256,1024]{1,0:T(8,128)(2,1)}, bf16[256,1024]{1,0:T(8,128)(2,1)S(1)}, u32[]{:S(2)}) copy-start(bf16[256,1024]{1,0:T(8,128)(2,1)S(1)} %get-tuple-element.8) | copy-start | bytes 1572868
  76.3 38.6 %copy-start.6 = (bf16[256,512]{1,0:T(8,128)(2,1)S(1)}, bf16[256,512]{1,0:T(8,128)(2,1)}, u32[]{:S(2)}) copy-start(bf16[256,512]{1,0:T(8,128)(2,1)} %edge_cot.1) | copy-start | bytes 786436
  96.9 36.6 %all-to-all-start.2 = ((bf16[32,8,1024]{2,1,0:T(8,128)(2,1)}), bf16[32,8,1024]{2,1,0:T(8,128)(2,1)S(1)}, u32[]{:S(2)}, u32[]{:S(2)}) async-start(bf16[32,8,1024]{2,1,0:T(8,128)(2,1)} %bitcast.18), calls=%async_computation.2 | async-start | bytes 1048576 | tf_op jit(solution)/shard_map/all_to_all | solution.py:134
  114.9 18.5 %copy-start.13 = (s32[256]{0:T(256)S(1)}, s32[256]{0:T(256)}, u32[]{:S(2)}) copy-start(s32[256]{0:T(256)} %copy-done.12) | copy-start | bytes 3076
  117.1 17.5 %collective-permute-start.2 = (bf16[32,512]{1,0:T(8,128)(2,1)S(1)}, bf16[32,512]{1,0:T(8,128)(2,1)S(1)}, u32[]{:S(2)}, u32[]{:S(2)}) collective-permute-start(bf16[32,512]{1,0:T(8,128)(2,1)S(1)} %get-tuple-element.10), channel_id=1, source_target_pairs={{1,0},{2,1},{0,2},{4,3},{5,4},{3,5},{7,6},{8,7},{6,8},{10,9},{11,1... | collective-permute-start | bytes 98312 | tf_op jit(solution)/shard_map/ppermute | solution.py:131
  120.5 14.1 %collective-permute-start.3 = (bf16[32,512]{1,0:T(8,128)(2,1)S(1)}, bf16[32,512]{1,0:T(8,128)(2,1)S(1)}, u32[]{:S(2)}, u32[]{:S(2)}) collective-permute-start(bf16[32,512]{1,0:T(8,128)(2,1)S(1)} %get-tuple-element.11), channel_id=1, source_target_pairs={{0,1},{1,2},{2,0},{3,4},{4,5},{5,3},{6,7},{7,8},{8,6},{9,10},{10,1... | collective-permute-start | bytes 98312 | tf_op jit(solution)/shard_map/ppermute | solution.py:132

commit v2 on v1

v2 whole, which is shorter than its diff:
```python
import functools

import jax
import jax.numpy as jnp
from jax import lax
from jax.experimental import pallas as pl
from jax.experimental.pallas import tpu as pltpu
from jax.sharding import PartitionSpec as P

Z_HI = 3


def dot(a, b):
    return jnp.dot(a, b, preferred_element_type=jnp.float32)


def dot_t(a, b):
    return lax.dot_general(a, b, (((1,), (1,)), ((), ())), preferred_element_type=jnp.float32)


def onehot_of(asked, owned):
    rows, _, per_block = asked.shape
    spread = jnp.broadcast_to(asked[...], (rows, per_block, per_block)).reshape(rows * per_block, per_block)
    slot = lax.broadcasted_iota(jnp.int32, spread.shape, 0) % per_block
    lane = lax.broadcasted_iota(jnp.int32, spread.shape, 1)
    index = jnp.sum(jnp.where(slot == lane, spread, 0), axis=1, keepdims=True)
    node = lax.broadcasted_iota(jnp.int32, (rows * per_block, owned), 1)
    return jnp.where(index % owned == node, 1.0, 0.0).astype(jnp.bfloat16)


def answer_kernel(asked, nodes, cots, answer):
    owned, width = nodes.shape
    onehot = onehot_of(asked, owned)
    answer[:, :width] = dot(onehot, nodes[...]).astype(jnp.bfloat16)
    answer[:, width:] = dot(onehot, cots[...]).astype(jnp.bfloat16)


def edge_kernel(
    table, spread, recv, counts, w_in, w_out, vectors, edges_hbm, cot_hbm,
    new_edges, packed, partial,
    edges, edge_cot, sems,
):
    slots, width = edges.shape
    group = table.shape[0]
    per_block = slots // counts.shape[1]
    edges_copy = pltpu.make_async_copy(edges_hbm, edges, sems.at[0])
    cot_copy = pltpu.make_async_copy(cot_hbm, edge_cot, sems.at[1])
    edges_copy.start()
    cot_copy.start()
    b_in, b_out = vectors[0:1, :], vectors[1:2, :]
    gain, bias = vectors[2:3, :], vectors[3:4, :]
    diagonal = lax.broadcasted_iota(jnp.int32, (slots, slots), 0) == lax.broadcasted_iota(
        jnp.int32, (slots, slots), 1
    )
    pick = jnp.sum(jnp.where(diagonal, spread[...], 0), axis=1, keepdims=True)
    slot = lax.broadcasted_iota(jnp.int32, (slots, counts.shape[1]), 0)
    block = lax.broadcasted_iota(jnp.int32, (slots, counts.shape[1]), 1)
    count = jnp.sum(jnp.where(slot // per_block == block, counts[...], 0), axis=1, keepdims=True)
    alive = slot[:, :1] % per_block < count
    lane = lax.broadcasted_iota(jnp.int32, (slots, group), 1)
    chosen = jnp.where(pick == lane, 1.0, 0.0).astype(jnp.bfloat16)
    send_feat = dot(chosen, table[...]).astype(jnp.bfloat16)
    pre = dot(recv[:, :width], w_in[2 * width :, :])
    pre += dot(send_feat, w_in[width : 2 * width, :])
    edges_copy.wait()
    pre += dot(edges[...], w_in[:width, :])
    pre += b_in
    sigma = jax.nn.sigmoid(pre)
    hidden = (pre * sigma).astype(jnp.bfloat16)
    outer = dot(hidden, w_out[...]) + b_out
    center = outer - jnp.mean(outer, axis=1, keepdims=True)
    inv_std = lax.rsqrt(jnp.mean(center * center, axis=1, keepdims=True) + 1e-05)
    normed = center * inv_std
    message = jnp.where(alive, normed * gain + bias, 0.0).astype(jnp.bfloat16)
    packed[:, :width] = message
    new_edges[...] = (edges[...].astype(jnp.float32) + message.astype(jnp.float32)).astype(jnp.bfloat16)
    cot_copy.wait()
    cot = edge_cot[...].astype(jnp.float32) + recv[:, width:].astype(jnp.float32)
    scaled = jnp.where(alive, cot, 0.0) * gain
    d_outer = inv_std * (
        scaled
        - jnp.mean(scaled, axis=1, keepdims=True)
        - normed * jnp.mean(scaled * normed, axis=1, keepdims=True)
    )
    d_hidden = dot_t(d_outer.astype(jnp.bfloat16), w_out[...])
    d_pre = (d_hidden * sigma * (1.0 + pre * (1.0 - sigma))).astype(jnp.bfloat16)
    packed[:, width:] = d_pre
    row = lax.broadcasted_iota(jnp.int32, (group, slots), 0)
    placed = jnp.where(spread[...] == row, 1.0, 0.0).astype(jnp.bfloat16)
    partial[...] = dot(placed, d_pre).astype(jnp.bfloat16)


def owner_kernel(asked, returned, column_sum, to_below, to_above, w_back, aggregated, grad_nodes):
    owned, width = aggregated.shape
    onehot = onehot_of(asked, owned)
    summed = lax.dot_general(
        onehot, returned[...], (((0,), (0,)), ((), ())), preferred_element_type=jnp.float32
    )
    aggregated[...] = summed[:, :width].astype(jnp.bfloat16)
    sent = column_sum[...] + to_below[...].astype(jnp.float32) + to_above[...].astype(jnp.float32)
    grad = dot_t(sent.astype(jnp.bfloat16), w_back[:width, :])
    grad += dot_t(summed[:, width:].astype(jnp.bfloat16), w_back[width:, :])
    grad_nodes[...] = grad.astype(jnp.bfloat16)


VMEM = pl.BlockSpec(memory_space=pltpu.VMEM)
ANY = pl.BlockSpec(memory_space=pl.ANY)


def on_device(
    node_latents,
    edge_latents,
    edge_sender,
    edge_receiver,
    edge_count,
    w_in,
    b_in,
    w_out,
    b_out,
    ln_gain,
    ln_bias,
    agg_cotangent,
    edge_cotangent,
):
    owned, width = node_latents.shape
    slots = edge_latents.shape[0]
    rows = lax.axis_size("row")
    cols = lax.axis_size("col")
    per_block = slots // rows
    tall = cols // Z_HI
    along_y = [[y * Z_HI + h for y in range(tall)] for h in range(Z_HI)]
    up = [(y * Z_HI + h, y * Z_HI + (h + 1) % Z_HI) for y in range(tall) for h in range(Z_HI)]
    down = [(b, a) for a, b in up]
    my_h = lax.axis_index("col") % Z_HI

    from_below = lax.ppermute(node_latents, "col", up)
    from_above = lax.ppermute(node_latents, "col", down)
    asked = lax.all_to_all(edge_receiver.reshape(rows, 1, per_block), "row", 0, 0, tiled=True)
    answer = pl.pallas_call(
        answer_kernel,
        in_specs=[VMEM] * 3,
        out_specs=VMEM,
        out_shape=jax.ShapeDtypeStruct((slots, 2 * width), jnp.bfloat16),
        cost_estimate=pl.CostEstimate(
            flops=2 * slots * owned * 2 * width, bytes_accessed=640 * 1024, transcendentals=0
        ),
    )(asked, node_latents, agg_cotangent)
    answer, from_below, from_above = lax.optimization_barrier((answer, from_below, from_above))
    recv = lax.all_to_all(answer, "row", 0, 0, tiled=True)
    column = jnp.concatenate([node_latents, from_below, from_above], axis=0)
    table = lax.all_gather(column, "col", axis=0, tiled=True, axis_index_groups=along_y)

    device = edge_sender // owned
    turn = (my_h - device % Z_HI + Z_HI) % Z_HI
    place = ((device // Z_HI) * Z_HI + turn) * owned + edge_sender % owned
    vectors = jnp.stack([b_in, b_out, ln_gain, ln_bias])

    new_edges, packed, partial = pl.pallas_call(
        edge_kernel,
        in_specs=[VMEM] * 7 + [ANY] * 2,
        out_specs=[VMEM] * 3,
        out_shape=[
            jax.ShapeDtypeStruct((slots, width), jnp.bfloat16),
            jax.ShapeDtypeStruct((slots, 2 * width), jnp.bfloat16),
            jax.ShapeDtypeStruct((cols * owned, width), jnp.bfloat16),
        ],
        scratch_shapes=[
            pltpu.VMEM((slots, width), jnp.bfloat16),
            pltpu.VMEM((slots, width), jnp.bfloat16),
            pltpu.SemaphoreType.DMA((2,)),
        ],
        compiler_params=pltpu.CompilerParams(vmem_limit_bytes=40 * 1024 * 1024),
        cost_estimate=pl.CostEstimate(
            flops=2 * slots * width * (5 * width + 2 * cols * owned),
            bytes_accessed=6 * 1024 * 1024,
            transcendentals=slots * width,
        ),
    )(
        table, place.reshape(1, slots), recv, edge_count, w_in, w_out, vectors,
        edge_latents, edge_cotangent,
    )

    parts = lax.all_to_all(partial, "col", 0, 0, tiled=True, axis_index_groups=along_y)
    column_sum = jnp.sum(parts.reshape(tall, Z_HI * owned, width).astype(jnp.float32), axis=0)
    away = column_sum.astype(jnp.bfloat16)
    to_below = lax.ppermute(away[owned : 2 * owned], "col", down)
    to_above = lax.ppermute(away[2 * owned :], "col", up)

    returned = lax.all_to_all(packed, "row", 0, 0, tiled=True)
    aggregated, grad_nodes = pl.pallas_call(
        owner_kernel,
        in_specs=[VMEM] * 6,
        out_specs=[VMEM] * 2,
        out_shape=[jax.ShapeDtypeStruct((owned, width), jnp.bfloat16)] * 2,
        cost_estimate=pl.CostEstimate(
            flops=2 * owned * width * (2 * slots + 2 * width), bytes_accessed=2 * 1024 * 1024, transcendentals=0
        ),
    )(asked, returned, column_sum[:owned], to_below, to_above, w_in[width:])
    d_edge = dot_t(packed[:, width:], w_in[:width])
    grad_edges = (edge_cotangent.astype(jnp.float32) + d_edge).astype(jnp.bfloat16)
    return (new_edges, aggregated, grad_nodes, grad_edges)


def solution(mesh):
    split = P(("row", "col"), None)
    return jax.shard_map(
        on_device,
        mesh=mesh,
        in_specs=(
            split, split, P(("row", "col")), P(("row", "col")), split,
            P(), P(), P(), P(), P(), P(), split, split,
        ),
        out_specs=(split, split, split, split),
        check_vma=False,
    )
```

time: 136 us -> 128 us (0.941)
  the two profiles are of different devices: /device:TPU:1 before, /device:TPU:69 now
where the time goes in v2:
time: 128 us; the launch traced here: 127 us
  blocking collectives  56.9 us (44%)
  starting transfers between devices  46.5 us (36%)
  Pallas kernels  7.57 us (6%)
  waiting for transfers between devices  7.52 us (6%)
  local copies, waits for them, and re-layouts  5.21 us (4%)
  matrix products  1.99 us (2%)
    all_gather x1, blocking collectives, on_device(): lax.all_gather(column, 'col', axis=0, tiled=True, axis_index_groups=along_y)  23 us
    all_to_all x1, blocking collectives, on_device(): lax.all_to_all(partial, 'col', 0, 0, tiled=True, axis_index_groups=along_y)  21.3 us
    all_to_all x1, starting transfers between devices, on_device(): returned = lax.all_to_all(packed, 'row', 0, 0, tiled=True)  14.6 us
    all_to_all x1, blocking collectives, on_device(): lax.all_to_all(edge_receiver.reshape(rows, 1, per_block), 'row', 0, 0, ti...  12.6 us
    ppermute x1, starting transfers between devices, on_device(): from_below = lax.ppermute(node_latents, 'col', up)  10.8 us
    ppermute x1, waiting for transfers between devices, on_device(): to_above = lax.ppermute(away[2 * owned:], 'col', up)  7.5 us
    all_to_all x1, starting transfers between devices, on_device(): recv = lax.all_to_all(answer, 'row', 0, 0, tiled=True)  7.01 us
    ppermute x1, starting transfers between devices, on_device(): to_above = lax.ppermute(away[2 * owned:], 'col', up)  6.29 us
  transfers between devices with their start and end apart: 6, of which 1 were waited for; matrix products, arithmetic and copies ran while one was open for 4% of the time, Pallas kernels for 2%

profile of v2, /device:TPU:69, one launch (start us, length us, event | category | flops | bytes accessed | tf_op | source)
XLA Modules:
  0.0 126.8 jit_solution(4111050379001501318)
XLA Ops:
  0.6 0.0 copy-start.7
  0.6 0.0 copy-start.10
  0.7 0.0 copy-start.11
  0.7 0.0 copy-start.12
  0.7 0.0 copy-start.13
  0.7 0.0 copy-start.14
  0.7 0.0 copy-start
  0.7 0.0 copy-start.1
  0.7 0.0 copy-start.5
  0.7 10.8 %collective-permute-start = (bf16[32,512]{1,0:T(8,128)(2,1)}, bf16[32,512]{1,0:T(8,128)(2,1)S(1)}, u32[]{:S(2)}, u32[]{:S(2)}) collective-permute-start(bf16[32,512]{1,0:T(8,128)(2,1)} %nodes.1), channel_id=1, source_target_pairs={{0,1},{1,2},{2,0},{3,4},{4,5},{5,3},{6,7},{7,8},{8,6},{9,10},{10,1... | collective-permute-start | bytes 98312 | tf_op jit(solution)/shard_map/ppermute | solution.py:136
  11.5 4.7 %collective-permute-start.1 = (bf16[32,512]{1,0:T(8,128)(2,1)}, bf16[32,512]{1,0:T(8,128)(2,1)S(1)}, u32[]{:S(2)}, u32[]{:S(2)}) collective-permute-start(bf16[32,512]{1,0:T(8,128)(2,1)} %nodes.1), channel_id=1, source_target_pairs={{1,0},{2,1},{0,2},{4,3},{5,4},{3,5},{7,6},{8,7},{6,8},{10,9},{11,1... | collective-permute-start | bytes 98312 | tf_op jit(solution)/shard_map/ppermute | solution.py:137
  16.2 0.8 reshape.22
  16.9 12.6 %all_to_all.36.asked = s32[32,1,8]{2,1,0:T(1,128)} all-to-all(s32[32,1,8]{2,1,0:T(1,128)S(1)} %bitcast.16), channel_id=1, replica_groups=mesh['row'=32,'col'=24] {'row'}, dimensions={0} | all-to-all | bytes 2048 | tf_op jit(solution)/shard_map/all_to_all | solution.py:138
  29.5 2.0 %shard_map.156 = bf16[256,1024]{1,0:T(8,128)(2,1)} custom-call(s32[32,1,8]{2,1,0:T(1,128)} %all_to_all.36.asked, bf16[32,512]{1,0:T(8,128)(2,1)} %nodes.1, bf16[32,512]{1,0:T(8,128)(2,1)} %cots.1), custom_call_target="tpu_custom_call" | custom-call | flops 16777216 | bytes 655360 | tf_op jit(solution)/shard_map/pallas_call | solution.py:139
  31.5 0.0 collective-permute-done
  31.5 0.0 collective-permute-done.1
  31.5 7.0 %all-to-all-start.1 = ((bf16[32,8,1024]{2,1,0:T(8,128)(2,1)}), bf16[32,8,1024]{2,1,0:T(8,128)(2,1)S(1)}, u32[]{:S(2)}, u32[]{:S(2)}) async-start(bf16[32,8,1024]{2,1,0:T(8,128)(2,1)} %bitcast.15), calls=%async_computation.1 | async-start | bytes 1048576 | tf_op jit(solution)/shard_map/all_to_all | solution.py:149
  38.5 0.0 copy-done.10
  38.5 0.0 copy-done.11
  38.6 0.0 copy-done.12
  38.6 0.0 copy-done.13
  38.6 0.0 copy-done.14
  38.6 0.0 copy-done.7
  38.7 23.0 %all_gather.3.table = bf16[768,512]{1,0:T(8,128)(2,1)S(1)} all-gather(bf16[96,512]{1,0:T(8,128)(2,1)S(1)} %pad_maximum_fusion), channel_id=1, replica_groups={{0,3,6,9,12,15,18,21},{1,4,7,10,13,16,19,22},{2,5,8,11,14,17,20,23},{24..., dimensions={0}, use_global_device_ids=true | all-gather | bytes 884736 | tf_op jit(solution)/shard_map/all_gather | solution.py:151
  61.7 0.0 all-to-all-done.1
  61.7 0.0 copy-done
  61.7 0.0 copy-done.1
  61.7 0.0 copy-done.5
  61.7 0.0 copy-start.2
  61.7 0.9 copy-done.2
  62.6 0.9 copy-done.3
  63.6 2.8 %shard_map.157 = (bf16[256,512]{1,0:T(8,128)(2,1)}, bf16[256,1024]{1,0:T(8,128)(2,1)}, bf16[768,512]{1,0:T(8,128)(2,1)S(1)}) custom-call(bf16[768,512]{1,0:T(8,128)(2,1)S(1)} %all_gather.3.table, s32[1,256]{1,0:T(1,128)S(1)} %bitcast.13, bf16[256,1024]{1,0:T(8,128)(2,1)S(1)} %bitcast.12, s32[1,32]{1,0:T(1,128)S(1)} %copy-done.5, ...), custom_call_target="tpu_custom_call" | custom-call | flops 1073741824 | bytes 6291456 | tf_op jit(solution)/shard_map/pallas_call | solution.py:158
  66.4 21.3 %all_to_all.37 = bf16[8,96,512]{2,1,0:T(8,128)(2,1)S(1)} all-to-all(bf16[8,96,512]{2,1,0:T(8,128)(2,1)S(1)} %bitcast.11), channel_id=1, replica_groups={{0,3,6,9,12,15,18,21},{1,4,7,10,13,16,19,22},{2,5,8,11,14,17,20,23},{24..., dimensions={0} | all-to-all | bytes 1572864 | tf_op jit(solution)/shard_map/all_to_all | solution.py:183
  87.8 14.6 %all-to-all-start.2 = ((bf16[32,8,1024]{2,1,0:T(8,128)(2,1)}), bf16[32,8,1024]{2,1,0:T(8,128)(2,1)S(1)}, u32[]{:S(2)}, u32[]{:S(2)}) async-start(bf16[32,8,1024]{2,1,0:T(8,128)(2,1)} %bitcast.8), calls=%async_computation.2 | async-start | bytes 1048576 | tf_op jit(solution)/shard_map/all_to_all | solution.py:189
  102.4 0.0 copy-start.4
  102.4 1.1 slice.21.w_back
  103.4 0.1 convert_reduce_fusion
  103.6 6.3 %collective-permute-start.3 = (bf16[32,512]{1,0:T(8,128)(2,1)S(1)}, bf16[32,512]{1,0:T(8,128)(2,1)S(1)}, u32[]{:S(2)}, u32[]{:S(2)}) collective-permute-start(bf16[32,512]{1,0:T(8,128)(2,1)S(1)} %get-tuple-element.20), channel_id=1, source_target_pairs={{0,1},{1,2},{2,0},{3,4},{4,5},{5,3},{6,7},{7,8},{8,6},{9,10},{10,1... | collective-permute-start | bytes 98312 | tf_op jit(solution)/shard_map/ppermute | solution.py:187
  109.9 3.2 %collective-permute-start.2 = (bf16[32,512]{1,0:T(8,128)(2,1)S(1)}, bf16[32,512]{1,0:T(8,128)(2,1)S(1)}, u32[]{:S(2)}, u32[]{:S(2)}) collective-permute-start(bf16[32,512]{1,0:T(8,128)(2,1)S(1)} %get-tuple-element.21), channel_id=1, source_target_pairs={{1,0},{2,1},{0,2},{4,3},{5,4},{3,5},{7,6},{8,7},{6,8},{10,9},{11,1... | collective-permute-start | bytes 98312 | tf_op jit(solution)/shard_map/ppermute | solution.py:186
  113.1 2.0 %fusion = bf16[256,512]{1,0:T(8,128)(2,1)} fusion(bf16[1536,512]{1,0:T(8,128)(2,1)S(1)} %copy-done, bf16[256,512]{1,0:T(8,128)(2,1)S(1)} %copy-done.4, bf16[256,1024]{1,0:T(8,128)(2,1)} %get-tuple-element.16), kind=kOutput, calls=%fused_computation.2 | convolution fusion | flops 134610944 | bytes 1310720 | tf_op jit(solution)/shard_map/dot_general | solution.py:18
  115.1 0.6 slice.24.column_sum
  115.7 7.5 %collective-permute-done.3.to_above = bf16[32,512]{1,0:T(8,128)(2,1)S(1)} collective-permute-done((bf16[32,512]{1,0:T(8,128)(2,1)S(1)}, bf16[32,512]{1,0:T(8,128)(2,1)S(1)}, u32[]{:S(2)}, u32[]{:S(2)}) %collective-permute-start.3) | collective-permute-done | bytes 32800 | tf_op jit(solution)/shard_map/ppermute | solution.py:187
  123.2 0.0 collective-permute-done.2.to_below
  123.2 0.0 all-to-all-done.2
  123.2 0.6 copy-done.8
  123.8 0.0 copy-done.9
  123.8 0.2 copy-done.6
  124.0 2.8 %shard_map.158 = (bf16[32,512]{1,0:T(8,128)(2,1)}, bf16[32,512]{1,0:T(8,128)(2,1)}) custom-call(s32[32,1,8]{2,1,0:T(1,128)} %all_to_all.36.asked, bf16[256,1024]{1,0:T(8,128)(2,1)} %bitcast.14, f32[32,512]{1,0:T(8,128)} %slice.24.column_sum, bf16[32,512]{1,0:T(8,128)(2,1)} %copy-done.9, bf16[32,512]{1,0:T(8,128)(2,1)} %copy-done.8, ...), custom_call_target="tpu_custom_call" | custom-call | flops 50331648 | bytes 2097152 | tf_op jit(solution)/shard_map/pallas_call | solution.py:190
  (10 shorter events, 0.1 us)
Async XLA Ops:
  0.6 38.0 %copy-start.7 = (bf16[32,512]{1,0:T(8,128)(2,1)S(1)}, bf16[32,512]{1,0:T(8,128)(2,1)}, u32[]{:S(2)}) copy-start(bf16[32,512]{1,0:T(8,128)(2,1)} %nodes.1) | copy-start | bytes 98308
  0.6 37.9 %copy-start.10 = (f32[512]{0:T(512)S(1)}, f32[512]{0:T(512)}, u32[]{:S(2)}) copy-start(f32[512]{0:T(512)} %param.23) | copy-start | bytes 6148
  0.7 37.9 %copy-start.11 = (f32[512]{0:T(512)S(1)}, f32[512]{0:T(512)}, u32[]{:S(2)}) copy-start(f32[512]{0:T(512)} %param.22) | copy-start | bytes 6148
  0.7 37.9 %copy-start.12 = (f32[512]{0:T(512)S(1)}, f32[512]{0:T(512)}, u32[]{:S(2)}) copy-start(f32[512]{0:T(512)} %param.21) | copy-start | bytes 6148
  0.7 37.9 %copy-start.13 = (f32[512]{0:T(512)S(1)}, f32[512]{0:T(512)}, u32[]{:S(2)}) copy-start(f32[512]{0:T(512)} %param.19) | copy-start | bytes 6148
  0.7 37.9 %copy-start.14 = (s32[256]{0:T(256)S(1)}, s32[256]{0:T(256)}, u32[]{:S(2)}) copy-start(s32[256]{0:T(256)} %param.15) | copy-start | bytes 3076
  0.7 61.0 %copy-start = (bf16[1536,512]{1,0:T(8,128)(2,1)S(1)}, bf16[1536,512]{1,0:T(8,128)(2,1)}, u32[]{:S(2)}) copy-start(bf16[1536,512]{1,0:T(8,128)(2,1)} %w_in.1) | copy-start | bytes 4718596
  0.7 61.0 %copy-start.1 = (bf16[512,512]{1,0:T(8,128)(2,1)S(1)}, bf16[512,512]{1,0:T(8,128)(2,1)}, u32[]{:S(2)}) copy-start(bf16[512,512]{1,0:T(8,128)(2,1)} %w_out.1) | copy-start | bytes 1572868
  0.7 61.0 %copy-start.5 = (s32[1,32]{1,0:T(1,128)S(1)}, s32[1,32]{1,0:T(1,128)}, u32[]{:S(2)}) copy-start(s32[1,32]{1,0:T(1,128)} %counts.1) | copy-start | bytes 388
  0.7 30.8 %collective-permute-start = (bf16[32,512]{1,0:T(8,128)(2,1)}, bf16[32,512]{1,0:T(8,128)(2,1)S(1)}, u32[]{:S(2)}, u32[]{:S(2)}) collective-permute-start(bf16[32,512]{1,0:T(8,128)(2,1)} %nodes.1), channel_id=1, source_target_pairs={{0,1},{1,2},{2,0},{3,4},{4,5},{5,3},{6,7},{7,8},{8,6},{9,10},{10,1... | collective-permute-start | bytes 98312 | tf_op jit(solution)/shard_map/ppermute | solution.py:136
  11.5 20.0 %collective-permute-start.1 = (bf16[32,512]{1,0:T(8,128)(2,1)}, bf16[32,512]{1,0:T(8,128)(2,1)S(1)}, u32[]{:S(2)}, u32[]{:S(2)}) collective-permute-start(bf16[32,512]{1,0:T(8,128)(2,1)} %nodes.1), channel_id=1, source_target_pairs={{1,0},{2,1},{0,2},{4,3},{5,4},{3,5},{7,6},{8,7},{6,8},{10,9},{11,1... | collective-permute-start | bytes 98312 | tf_op jit(solution)/shard_map/ppermute | solution.py:137
  31.5 30.2 %all-to-all-start.1 = ((bf16[32,8,1024]{2,1,0:T(8,128)(2,1)}), bf16[32,8,1024]{2,1,0:T(8,128)(2,1)S(1)}, u32[]{:S(2)}, u32[]{:S(2)}) async-start(bf16[32,8,1024]{2,1,0:T(8,128)(2,1)} %bitcast.15), calls=%async_computation.1 | async-start | bytes 1048576 | tf_op jit(solution)/shard_map/all_to_all | solution.py:149
  61.7 1.0 copy-start.2
  62.6 0.9 copy-start.3
  87.8 35.4 %all-to-all-start.2 = ((bf16[32,8,1024]{2,1,0:T(8,128)(2,1)}), bf16[32,8,1024]{2,1,0:T(8,128)(2,1)S(1)}, u32[]{:S(2)}, u32[]{:S(2)}) async-start(bf16[32,8,1024]{2,1,0:T(8,128)(2,1)} %bitcast.8), calls=%async_computation.2 | async-start | bytes 1048576 | tf_op jit(solution)/shard_map/all_to_all | solution.py:189
  102.4 10.7 %copy-start.4 = (bf16[256,512]{1,0:T(8,128)(2,1)S(1)}, bf16[256,512]{1,0:T(8,128)(2,1)}, u32[]{:S(2)}) copy-start(bf16[256,512]{1,0:T(8,128)(2,1)} %cot_hbm.1) | copy-start | bytes 786436
  103.6 19.6 %collective-permute-start.3 = (bf16[32,512]{1,0:T(8,128)(2,1)S(1)}, bf16[32,512]{1,0:T(8,128)(2,1)S(1)}, u32[]{:S(2)}, u32[]{:S(2)}) collective-permute-start(bf16[32,512]{1,0:T(8,128)(2,1)S(1)} %get-tuple-element.20), channel_id=1, source_target_pairs={{0,1},{1,2},{2,0},{3,4},{4,5},{5,3},{6,7},{7,8},{8,6},{9,10},{10,1... | collective-permute-start | bytes 98312 | tf_op jit(solution)/shard_map/ppermute | solution.py:187
  109.9 13.3 %collective-permute-start.2 = (bf16[32,512]{1,0:T(8,128)(2,1)S(1)}, bf16[32,512]{1,0:T(8,128)(2,1)S(1)}, u32[]{:S(2)}, u32[]{:S(2)}) collective-permute-start(bf16[32,512]{1,0:T(8,128)(2,1)S(1)} %get-tuple-element.21), channel_id=1, source_target_pairs={{1,0},{2,1},{0,2},{4,3},{5,4},{3,5},{7,6},{8,7},{6,8},{10,9},{11,1... | collective-permute-start | bytes 98312 | tf_op jit(solution)/shard_map/ppermute | solution.py:186
  123.2 0.6 copy-start.8
  123.2 0.6 copy-start.9
  123.2 0.8 copy-start.6

commit v3 on v2

v3 whole, which is shorter than its diff:
```python
import functools

import jax
import jax.numpy as jnp
from jax import lax
from jax.experimental import pallas as pl
from jax.experimental.pallas import tpu as pltpu
from jax.sharding import PartitionSpec as P

Z_HI = 3
Z_LO = 4


def dot(a, b):
    return jnp.dot(a, b, preferred_element_type=jnp.float32)


def dot_t(a, b):
    return lax.dot_general(a, b, (((1,), (1,)), ((), ())), preferred_element_type=jnp.float32)


def column_of(row):
    n = row.shape[1]
    diagonal = lax.broadcasted_iota(jnp.int32, (n, n), 0) == lax.broadcasted_iota(jnp.int32, (n, n), 1)
    return jnp.sum(jnp.where(diagonal, row, 0), axis=1, keepdims=True)


def selector(index, size):
    lane = lax.broadcasted_iota(jnp.int32, (index.shape[0], size), 1)
    return jnp.where(index == lane, 1.0, 0.0).astype(jnp.bfloat16)


def edge_kernel(
    senders, sender, spread, receiver, counts, w_in, w_out, vectors, owners_hbm, edges_hbm, cot_hbm,
    new_edges, packed, partial,
    owners, edges, edge_cot, sems,
):
    slots, width = edges.shape
    group = senders.shape[0]
    blocks = counts.shape[1]
    per_block = slots // blocks
    owned = owners.shape[0] // blocks
    near = blocks // Z_LO
    owners_copy = pltpu.make_async_copy(owners_hbm, owners, sems.at[0])
    edges_copy = pltpu.make_async_copy(edges_hbm, edges, sems.at[1])
    cot_copy = pltpu.make_async_copy(cot_hbm, edge_cot, sems.at[2])
    owners_copy.start()
    edges_copy.start()
    cot_copy.start()
    b_in, b_out = vectors[0:1, :], vectors[1:2, :]
    gain, bias = vectors[2:3, :], vectors[3:4, :]
    slot = lax.broadcasted_iota(jnp.int32, (slots, blocks), 0)
    block = lax.broadcasted_iota(jnp.int32, (slots, blocks), 1)
    count = jnp.sum(jnp.where(slot // per_block == block, counts[...], 0), axis=1, keepdims=True)
    alive = slot[:, :1] % per_block < count
    send_feat = dot(selector(column_of(sender[...]), group), senders[...]).astype(jnp.bfloat16)
    pre = dot(send_feat, w_in[width : 2 * width, :])
    edges_copy.wait()
    pre += dot(edges[...], w_in[:width, :])
    node = column_of(receiver[...])
    owner = node // owned
    where = ((owner % near) * Z_LO + owner // near) * owned + node % owned
    owners_copy.wait()
    recv = dot(selector(where, owners.shape[0]), owners[...]).astype(jnp.bfloat16)
    pre += dot(recv[:, :width], w_in[2 * width :, :])
    pre += b_in
    sigma = jax.nn.sigmoid(pre)
    hidden = (pre * sigma).astype(jnp.bfloat16)
    outer = dot(hidden, w_out[...]) + b_out
    center = outer - jnp.mean(outer, axis=1, keepdims=True)
    inv_std = lax.rsqrt(jnp.mean(center * center, axis=1, keepdims=True) + 1e-05)
    normed = center * inv_std
    message = jnp.where(alive, normed * gain + bias, 0.0).astype(jnp.bfloat16)
    packed[:, :width] = message
    new_edges[...] = (edges[...].astype(jnp.float32) + message.astype(jnp.float32)).astype(jnp.bfloat16)
    cot_copy.wait()
    cot = edge_cot[...].astype(jnp.float32) + recv[:, width:].astype(jnp.float32)
    scaled = jnp.where(alive, cot, 0.0) * gain
    d_outer = inv_std * (
        scaled
        - jnp.mean(scaled, axis=1, keepdims=True)
        - normed * jnp.mean(scaled * normed, axis=1, keepdims=True)
    )
    d_hidden = dot_t(d_outer.astype(jnp.bfloat16), w_out[...])
    d_pre = (d_hidden * sigma * (1.0 + pre * (1.0 - sigma))).astype(jnp.bfloat16)
    packed[:, width : 2 * width] = d_pre
    packed[:, 2 * width :] = jnp.broadcast_to(
        (node % owned).astype(jnp.float32), (slots, packed.shape[1] - 2 * width)
    ).astype(jnp.bfloat16)
    row = lax.broadcasted_iota(jnp.int32, (group, slots), 0)
    placed = jnp.where(spread[...] == row, 1.0, 0.0).astype(jnp.bfloat16)
    partial[...] = dot(placed, d_pre).astype(jnp.bfloat16)


def owner_kernel(returned, column_sum, to_below, to_above, w_in, aggregated, grad_nodes):
    owned, width = aggregated.shape
    index = returned[:, 2 * width :].astype(jnp.float32)
    lane = lax.broadcasted_iota(jnp.int32, index.shape, 1).astype(jnp.float32)
    onehot = jnp.where(index == lane, 1.0, 0.0).astype(jnp.bfloat16)
    summed = lax.dot_general(
        onehot, returned[:, : 2 * width], (((0,), (0,)), ((), ())), preferred_element_type=jnp.float32
    )[:owned]
    aggregated[...] = summed[:, :width].astype(jnp.bfloat16)
    sent = column_sum[:owned, :] + to_below[...].astype(jnp.float32) + to_above[...].astype(jnp.float32)
    grad = dot_t(sent.astype(jnp.bfloat16), w_in[width : 2 * width, :])
    grad += dot_t(summed[:, width:].astype(jnp.bfloat16), w_in[2 * width :, :])
    grad_nodes[...] = grad.astype(jnp.bfloat16)


VMEM = pl.BlockSpec(memory_space=pltpu.VMEM)
HBM = pl.BlockSpec(memory_space=pltpu.HBM)


def everywhere(block, axis, groups):
    peers = len(groups[0])
    copies = jnp.broadcast_to(block[None], (peers,) + block.shape).reshape(-1, block.shape[1])
    return lax.all_to_all(copies, axis, 0, 0, tiled=True, axis_index_groups=groups)


def on_device(
    node_latents,
    edge_latents,
    edge_sender,
    edge_receiver,
    edge_count,
    w_in,
    b_in,
    w_out,
    b_out,
    ln_gain,
    ln_bias,
    agg_cotangent,
    edge_cotangent,
):
    owned, width = node_latents.shape
    slots = edge_latents.shape[0]
    rows = lax.axis_size("row")
    cols = lax.axis_size("col")
    tall, near = cols // Z_HI, rows // Z_LO
    along_y = [[y * Z_HI + h for y in range(tall)] for h in range(Z_HI)]
    along_h = [[y * Z_HI + h for h in range(Z_HI)] for y in range(tall)]
    along_z = [[z * near + n for z in range(Z_LO)] for n in range(near)]
    along_x = [[z * near + n for n in range(near)] for z in range(Z_LO)]
    up = [(y * Z_HI + h, y * Z_HI + (h + 1) % Z_HI) for y in range(tall) for h in range(Z_HI)]
    down = [(b, a) for a, b in up]
    my_h = lax.axis_index("col") % Z_HI

    own = jnp.concatenate([node_latents, agg_cotangent], axis=1)
    quarter = everywhere(own, "row", along_z)
    owners = lax.all_gather(quarter, "row", axis=0, tiled=True, axis_index_groups=along_x)
    mine, quarter = lax.optimization_barrier((node_latents, quarter))
    senders = everywhere(everywhere(mine, "col", along_h), "col", along_y)

    device = edge_sender // owned
    turn = (my_h - device % Z_HI + Z_HI) % Z_HI
    place = ((device // Z_HI) * Z_HI + turn) * owned + edge_sender % owned
    vectors = jnp.stack([b_in, b_out, ln_gain, ln_bias])

    new_edges, packed, partial = pl.pallas_call(
        edge_kernel,
        in_specs=[VMEM] * 8 + [HBM] * 3,
        out_specs=[VMEM] * 3,
        out_shape=[
            jax.ShapeDtypeStruct((slots, width), jnp.bfloat16),
            jax.ShapeDtypeStruct((slots, 2 * width + 128), jnp.bfloat16),
            jax.ShapeDtypeStruct((cols * owned, width), jnp.bfloat16),
        ],
        scratch_shapes=[
            pltpu.VMEM((rows * owned, 2 * width), jnp.bfloat16),
            pltpu.VMEM((slots, width), jnp.bfloat16),
            pltpu.VMEM((slots, width), jnp.bfloat16),
            pltpu.SemaphoreType.DMA((3,)),
        ],
        compiler_params=pltpu.CompilerParams(vmem_limit_bytes=40 * 1024 * 1024),
        cost_estimate=pl.CostEstimate(
            flops=2 * slots * width * (5 * width + 2 * cols * owned + 2 * rows * owned),
            bytes_accessed=8 * 1024 * 1024,
            transcendentals=slots * width,
        ),
    )(
        senders, edge_sender.reshape(1, slots), place.reshape(1, slots), edge_receiver.reshape(1, slots),
        edge_count, w_in, w_out, vectors, owners, edge_latents, edge_cotangent,
    )

    parts = lax.all_to_all(partial, "col", 0, 0, tiled=True, axis_index_groups=along_y)
    column_sum = jnp.sum(parts.reshape(tall, Z_HI * owned, width).astype(jnp.float32), axis=0)
    away = column_sum.astype(jnp.bfloat16)
    to_below = lax.ppermute(away[owned : 2 * owned], "col", down)
    to_above = lax.ppermute(away[2 * owned :], "col", up)

    returned = lax.all_to_all(packed, "row", 0, 0, tiled=True)
    aggregated, grad_nodes = pl.pallas_call(
        owner_kernel,
        in_specs=[VMEM] * 5,
        out_specs=[VMEM] * 2,
        out_shape=[jax.ShapeDtypeStruct((owned, width), jnp.bfloat16)] * 2,
        cost_estimate=pl.CostEstimate(
            flops=2 * owned * width * (2 * slots + 2 * width), bytes_accessed=2 * 1024 * 1024, transcendentals=0
        ),
    )(returned, column_sum, to_below, to_above, w_in)
    d_edge = dot_t(packed[:, width : 2 * width], w_in[:width])
    grad_edges = (edge_cotangent.astype(jnp.float32) + d_edge).astype(jnp.bfloat16)
    return (new_edges, aggregated, grad_nodes, grad_edges)


def solution(mesh):
    split = P(("row", "col"), None)
    return jax.shard_map(
        on_device,
        mesh=mesh,
        in_specs=(
            split, split, P(("row", "col")), P(("row", "col")), split,
            P(), P(), P(), P(), P(), P(), split, split,
        ),
        out_specs=(split, split, split, split),
        check_vma=False,
    )
```

time: 128 us -> 141 us (1.10)
  the two profiles are of different devices: /device:TPU:69 before, /device:TPU:128 now
where the time goes in v3:
time: 141 us
  blocking collectives  54.4 us (39%)
  waiting for transfers between devices  31.5 us (22%)
  starting transfers between devices  26.1 us (19%)
  between operations  14.3 us (10%)
  Pallas kernels  6.99 us (5%)
  local copies, waits for them, and re-layouts  4.37 us (3%)
  matrix products  1.99 us (1%)
    all_to_all x2, blocking collectives, everywhere(): lax.all_to_all(copies, axis, 0, 0, tiled=True, axis_index_groups=groups)  31.3 us
    all_to_all x1, blocking collectives, on_device(): lax.all_to_all(partial, 'col', 0, 0, tiled=True, axis_index_groups=along_y)  23.1 us
    all_to_all x1, waiting for transfers between devices, everywhere(): lax.all_to_all(copies, axis, 0, 0, tiled=True, axis_index_groups=groups)  21 us
    ppermute x1, waiting for transfers between devices, on_device(): to_below = lax.ppermute(away[owned:2 * owned], 'col', down)  10.5 us
    all_to_all x1, starting transfers between devices, on_device(): returned = lax.all_to_all(packed, 'row', 0, 0, tiled=True)  9.05 us
    ppermute x1, starting transfers between devices, on_device(): to_above = lax.ppermute(away[2 * owned:], 'col', up)  8.01 us
    all_to_all x1, starting transfers between devices, everywhere(): lax.all_to_all(copies, axis, 0, 0, tiled=True, axis_index_groups=groups)  7.1 us
    pallas_call x1, Pallas kernels, on_device(): pl.pallas_call(edge_kernel, in_specs=[VMEM] * 8 + [HBM] * 3, out_specs=[V...  4.06 us
  transfers between devices with their start and end apart: 5, of which 2 were waited for; matrix products, arithmetic and copies ran while one was open for 3% of the time, Pallas kernels for 0%

profile of v3, /device:TPU:128, one launch (start us, length us, event | category | flops | bytes accessed | tf_op | source)
XLA Modules:
  0.0 140.6 jit_solution(14174507052780536906)
XLA Ops:
  7.2 0.0 all-gather.2.cloned.1.call-start
  7.2 0.8 pad_maximum_fusion
  8.0 15.8 %all_to_all.43 = bf16[4,32,1024]{2,1,0:T(8,128)(2,1)} all-to-all(bf16[4,32,1024]{2,1,0:T(8,128)(2,1)S(1)} %broadcast_in_dim.8), channel_id=1, replica_groups={{0,192,384,576},{24,216,408,600},{48,240,432,624},{72,264,456,648},{96,..., dimensions={0} | all-to-all | bytes 524288 | tf_op jit(solution)/shard_map/all_to_all | solution.py:117
  23.8 0.0 copy-start.12
  23.8 0.0 copy-start.13
  23.8 0.0 copy-start.14
  23.8 0.0 copy-start.1
  23.8 0.0 copy-start
  23.8 0.0 copy-start.3
  23.8 0.0 copy-start.4
  23.9 0.0 copy-start.5
  23.9 0.0 copy-start.6
  23.9 0.0 copy-start.7
  23.9 0.0 all-gather.2.cloned.1.call-update
  23.9 0.9 broadcast_in_dim.9
  24.8 15.5 %all_to_all.44 = bf16[3,32,512]{2,1,0:T(8,128)(2,1)S(1)} all-to-all(bf16[3,32,512]{2,1,0:T(8,128)(2,1)S(1)} %broadcast_in_dim.9), channel_id=1, replica_groups={{0,1,2},{3,4,5},{6,7,8},{9,10,11},{12,13,14},{15,16,17},{18,19,20},{21,..., dimensions={0} | all-to-all | bytes 196608 | tf_op jit(solution)/shard_map/all_to_all | solution.py:117
  40.3 0.9 broadcast_in_dim.11
  41.3 7.1 %all-to-all-start.2 = ((bf16[8,96,512]{2,1,0:T(8,128)(2,1)}), bf16[8,96,512]{2,1,0:T(8,128)(2,1)S(1)}, u32[]{:S(2)}, u32[]{:S(2)}) async-start(bf16[8,96,512]{2,1,0:T(8,128)(2,1)} %broadcast_in_dim.11), calls=%async_computation.2 | async-start | bytes 1572864 | tf_op jit(solution)/shard_map/all_to_all | solution.py:117
  48.4 0.0 copy-done.12
  48.4 0.0 copy-done.13
  48.4 0.0 copy-done.14
  48.4 0.0 copy-done.15
  48.5 0.0 copy-done.1
  48.5 21.0 %all-to-all-done.2 = bf16[8,96,512]{2,1,0:T(8,128)(2,1)S(1)} async-done(((bf16[8,96,512]{2,1,0:T(8,128)(2,1)}), bf16[8,96,512]{2,1,0:T(8,128)(2,1)S(1)}, u32[]{:S(2)}, u32[]{:S(2)}) %all-to-all-start.2) | async-done | bytes 786464 | tf_op jit(solution)/shard_map/all_to_all | solution.py:117
  69.5 0.0 copy-done
  69.5 0.0 copy-done.3
  69.5 0.0 copy-done.4
  69.5 0.0 copy-done.5
  69.5 0.0 copy-done.6
  69.5 0.0 copy-done.7
  69.5 0.0 copy-start.2
  69.5 1.6 %copy-done.2 = bf16[1024,1024]{1,0:T(8,128)(2,1)S(1)} copy-done((bf16[1024,1024]{1,0:T(8,128)(2,1)S(1)}, bf16[1024,1024]{1,0:T(8,128)(2,1)}, u32[]{:S(2)}) %copy-start.2) | copy-done | bytes 2097176
  71.1 4.1 %shard_map.156 = (bf16[256,512]{1,0:T(8,128)(2,1)}, bf16[256,1152]{1,0:T(8,128)(2,1)}, bf16[768,512]{1,0:T(8,128)(2,1)S(1)}) custom-call(bf16[768,512]{1,0:T(8,128)(2,1)S(1)} %bitcast.13, s32[1,256]{1,0:T(1,128)S(1)} %bitcast.15, s32[1,256]{1,0:T(1,128)S(1)} %bitcast.16, s32[1,256]{1,0:T(1,128)S(1)} %bitcast.17, s32[1,32]{1,0:T(1,128)S(1)} %copy-done.7, ...), custom_call_target="tpu_custom_call" | custom-call | flops 1610612736 | bytes 8388608 | tf_op jit(solution)/shard_map/pallas_call | solution.py:159
  75.2 23.1 %all_to_all.45 = bf16[8,96,512]{2,1,0:T(8,128)(2,1)S(1)} all-to-all(bf16[8,96,512]{2,1,0:T(8,128)(2,1)S(1)} %bitcast.14), channel_id=1, replica_groups={{0,3,6,9,12,15,18,21},{1,4,7,10,13,16,19,22},{2,5,8,11,14,17,20,23},{24..., dimensions={0} | all-to-all | bytes 1572864 | tf_op jit(solution)/shard_map/all_to_all | solution.py:185
  98.2 9.1 %all-to-all-start.3 = ((bf16[32,8,1152]{2,1,0:T(8,128)(2,1)}), bf16[32,8,1152]{2,1,0:T(8,128)(2,1)S(1)}, u32[]{:S(2)}, u32[]{:S(2)}) async-start(bf16[32,8,1152]{2,1,0:T(8,128)(2,1)} %bitcast.10), calls=%async_computation.3 | async-start | bytes 1179648 | tf_op jit(solution)/shard_map/all_to_all | solution.py:191
  107.3 0.1 convert_reduce_fusion.column_sum
  107.4 0.0 copy-start.9
  107.4 8.0 %collective-permute-start.1 = (bf16[32,512]{1,0:T(8,128)(2,1)S(1)}, bf16[32,512]{1,0:T(8,128)(2,1)S(1)}, u32[]{:S(2)}, u32[]{:S(2)}) collective-permute-start(bf16[32,512]{1,0:T(8,128)(2,1)S(1)} %get-tuple-element.16), channel_id=1, source_target_pairs={{0,1},{1,2},{2,0},{3,4},{4,5},{5,3},{6,7},{7,8},{8,6},{9,10},{10,1... | collective-permute-start | bytes 98312 | tf_op jit(solution)/shard_map/ppermute | solution.py:189
  115.5 1.9 %collective-permute-start = (bf16[32,512]{1,0:T(8,128)(2,1)S(1)}, bf16[32,512]{1,0:T(8,128)(2,1)S(1)}, u32[]{:S(2)}, u32[]{:S(2)}) collective-permute-start(bf16[32,512]{1,0:T(8,128)(2,1)S(1)} %get-tuple-element.17), channel_id=1, source_target_pairs={{1,0},{2,1},{0,2},{4,3},{5,4},{3,5},{7,6},{8,7},{6,8},{10,9},{11,1... | collective-permute-start | bytes 98312 | tf_op jit(solution)/shard_map/ppermute | solution.py:188
  117.4 2.0 %fusion = bf16[256,512]{1,0:T(8,128)(2,1)} fusion(bf16[1536,512]{1,0:T(8,128)(2,1)S(1)} %copy-done, bf16[256,512]{1,0:T(8,128)(2,1)S(1)} %copy-done.5, bf16[256,1152]{1,0:T(8,128)(2,1)} %get-tuple-element.12), kind=kOutput, calls=%fused_computation.2 | convolution fusion | flops 134610944 | bytes 1310720 | tf_op jit(solution)/shard_map/dot_general | solution.py:19
  119.4 0.0 collective-permute-done.1.to_above
  119.4 10.5 %collective-permute-done.to_below = bf16[32,512]{1,0:T(8,128)(2,1)S(1)} collective-permute-done((bf16[32,512]{1,0:T(8,128)(2,1)S(1)}, bf16[32,512]{1,0:T(8,128)(2,1)S(1)}, u32[]{:S(2)}, u32[]{:S(2)}) %collective-permute-start) | collective-permute-done | bytes 32800 | tf_op jit(solution)/shard_map/ppermute | solution.py:188
  129.9 0.0 all-to-all-done.3
  129.9 0.0 copy-done.9
  129.9 0.0 copy-done.10
  130.0 0.6 copy-done.11
  130.5 0.2 copy-done.8
  130.8 2.9 %shard_map.157 = (bf16[32,512]{1,0:T(8,128)(2,1)}, bf16[32,512]{1,0:T(8,128)(2,1)}) custom-call(bf16[256,1152]{1,0:T(8,128)(2,1)} %bitcast.18, f32[96,512]{1,0:T(8,128)} %copy-done.9, bf16[32,512]{1,0:T(8,128)(2,1)} %copy-done.11, bf16[32,512]{1,0:T(8,128)(2,1)} %copy-done.10, bf16[1536,512]{1,0:T(8,128)(2,1)} %w_in.3), custom_call_target="tpu_custom_call" | custom-call | flops 50331648 | bytes 2097152 | tf_op jit(solution)/shard_map/pallas_call | solution.py:192
  (10 shorter events, 0.1 us)
Async XLA Ops:
  7.2 62.3 %all-gather.2.cloned.1.call-start = ((), (), s32[]{:S(2)}) async-start(), calls=%async_computation.5 | async-start | bytes 2359296 | tf_op jit(solution)/shard_map/all_gather | solution.py:150
  23.8 24.6 %copy-start.12 = (f32[512]{0:T(512)S(1)}, f32[512]{0:T(512)}, u32[]{:S(2)}) copy-start(f32[512]{0:T(512)} %param.23) | copy-start | bytes 6148
  23.8 24.6 %copy-start.13 = (f32[512]{0:T(512)S(1)}, f32[512]{0:T(512)}, u32[]{:S(2)}) copy-start(f32[512]{0:T(512)} %param.22) | copy-start | bytes 6148
  23.8 24.6 %copy-start.14 = (f32[512]{0:T(512)S(1)}, f32[512]{0:T(512)}, u32[]{:S(2)}) copy-start(f32[512]{0:T(512)} %param.21) | copy-start | bytes 6148
  23.8 24.6 %copy-start.15 = (f32[512]{0:T(512)S(1)}, f32[512]{0:T(512)}, u32[]{:S(2)}) copy-start(f32[512]{0:T(512)} %param.19) | copy-start | bytes 6148
  23.8 24.7 %copy-start.1 = (s32[256]{0:T(256)S(1)}, s32[256]{0:T(256)}, u32[]{:S(2)}) copy-start(s32[256]{0:T(256)} %param.15) | copy-start | bytes 3076
  23.8 45.7 %copy-start = (bf16[1536,512]{1,0:T(8,128)(2,1)S(1)}, bf16[1536,512]{1,0:T(8,128)(2,1)}, u32[]{:S(2)}) copy-start(bf16[1536,512]{1,0:T(8,128)(2,1)} %w_in.3) | copy-start | bytes 4718596
  23.8 45.6 %copy-start.3 = (bf16[512,512]{1,0:T(8,128)(2,1)S(1)}, bf16[512,512]{1,0:T(8,128)(2,1)}, u32[]{:S(2)}) copy-start(bf16[512,512]{1,0:T(8,128)(2,1)} %w_out.1) | copy-start | bytes 1572868
  23.8 45.6 %copy-start.4 = (bf16[256,512]{1,0:T(8,128)(2,1)S(1)}, bf16[256,512]{1,0:T(8,128)(2,1)}, u32[]{:S(2)}) copy-start(bf16[256,512]{1,0:T(8,128)(2,1)} %edges_hbm.1) | copy-start | bytes 786436
  23.9 45.6 %copy-start.5 = (bf16[256,512]{1,0:T(8,128)(2,1)S(1)}, bf16[256,512]{1,0:T(8,128)(2,1)}, u32[]{:S(2)}) copy-start(bf16[256,512]{1,0:T(8,128)(2,1)} %cot_hbm.1) | copy-start | bytes 786436
  23.9 45.6 %copy-start.6 = (s32[256]{0:T(256)S(1)}, s32[256]{0:T(256)}, u32[]{:S(2)}) copy-start(s32[256]{0:T(256)} %param.16) | copy-start | bytes 3076
  23.9 45.6 %copy-start.7 = (s32[1,32]{1,0:T(1,128)S(1)}, s32[1,32]{1,0:T(1,128)}, u32[]{:S(2)}) copy-start(s32[1,32]{1,0:T(1,128)} %counts.1) | copy-start | bytes 388
  41.3 28.2 %all-to-all-start.2 = ((bf16[8,96,512]{2,1,0:T(8,128)(2,1)}), bf16[8,96,512]{2,1,0:T(8,128)(2,1)S(1)}, u32[]{:S(2)}, u32[]{:S(2)}) async-start(bf16[8,96,512]{2,1,0:T(8,128)(2,1)} %broadcast_in_dim.11), calls=%async_computation.2 | async-start | bytes 1572864 | tf_op jit(solution)/shard_map/all_to_all | solution.py:117
  69.5 1.6 %copy-start.2 = (bf16[1024,1024]{1,0:T(8,128)(2,1)S(1)}, bf16[1024,1024]{1,0:T(8,128)(2,1)}, u32[]{:S(2)}) copy-start(bf16[1024,1024]{1,0:T(8,128)(2,1)} %all-gather.2.cloned.1.call-done.owners_hbm) | copy-start | bytes 6291460
  98.2 31.7 %all-to-all-start.3 = ((bf16[32,8,1152]{2,1,0:T(8,128)(2,1)}), bf16[32,8,1152]{2,1,0:T(8,128)(2,1)S(1)}, u32[]{:S(2)}, u32[]{:S(2)}) async-start(bf16[32,8,1152]{2,1,0:T(8,128)(2,1)} %bitcast.10), calls=%async_computation.3 | async-start | bytes 1179648 | tf_op jit(solution)/shard_map/all_to_all | solution.py:191
  107.4 22.5 %copy-start.9 = (f32[96,512]{1,0:T(8,128)}, f32[96,512]{1,0:T(8,128)S(1)}, u32[]{:S(2)}) copy-start(f32[96,512]{1,0:T(8,128)S(1)} %convert_reduce_fusion.column_sum) | copy-start | bytes 589828
  107.4 11.9 %collective-permute-start.1 = (bf16[32,512]{1,0:T(8,128)(2,1)S(1)}, bf16[32,512]{1,0:T(8,128)(2,1)S(1)}, u32[]{:S(2)}, u32[]{:S(2)}) collective-permute-start(bf16[32,512]{1,0:T(8,128)(2,1)S(1)} %get-tuple-element.16), channel_id=1, source_target_pairs={{0,1},{1,2},{2,0},{3,4},{4,5},{5,3},{6,7},{7,8},{8,6},{9,10},{10,1... | collective-permute-start | bytes 98312 | tf_op jit(solution)/shard_map/ppermute | solution.py:189
  115.5 14.5 %collective-permute-start = (bf16[32,512]{1,0:T(8,128)(2,1)S(1)}, bf16[32,512]{1,0:T(8,128)(2,1)S(1)}, u32[]{:S(2)}, u32[]{:S(2)}) collective-permute-start(bf16[32,512]{1,0:T(8,128)(2,1)S(1)} %get-tuple-element.17), channel_id=1, source_target_pairs={{1,0},{2,1},{0,2},{4,3},{5,4},{3,5},{7,6},{8,7},{6,8},{10,9},{11,1... | collective-permute-start | bytes 98312 | tf_op jit(solution)/shard_map/ppermute | solution.py:188
  119.4 10.6 %copy-start.10 = (bf16[32,512]{1,0:T(8,128)(2,1)}, bf16[32,512]{1,0:T(8,128)(2,1)S(1)}, u32[]{:S(2)}) copy-start(bf16[32,512]{1,0:T(8,128)(2,1)S(1)} %collective-permute-done.1.to_above) | copy-start | bytes 98308
  129.9 0.6 copy-start.11
  129.9 0.8 copy-start.8
Sparse Core Ops, SparseCore 0:
  24.0 34.8 all-gather.1

commit v4 on v2

--- a/solution.py
+++ b/solution.py
@@ -28,11 +28,8 @@
     return jnp.where(index % owned == node, 1.0, 0.0).astype(jnp.bfloat16)
 
 
-def answer_kernel(asked, nodes, cots, answer):
-    owned, width = nodes.shape
-    onehot = onehot_of(asked, owned)
-    answer[:, :width] = dot(onehot, nodes[...]).astype(jnp.bfloat16)
-    answer[:, width:] = dot(onehot, cots[...]).astype(jnp.bfloat16)
+def answer_kernel(asked, own, answer):
+    answer[...] = dot(onehot_of(asked, own.shape[0]), own[...]).astype(jnp.bfloat16)
 
 
 def edge_kernel(
@@ -90,16 +87,16 @@
     partial[...] = dot(placed, d_pre).astype(jnp.bfloat16)
 
 
-def owner_kernel(asked, returned, column_sum, to_below, to_above, w_back, aggregated, grad_nodes):
+def owner_kernel(asked, returned, column_sum, to_below, to_above, w_in, aggregated, grad_nodes):
     owned, width = aggregated.shape
     onehot = onehot_of(asked, owned)
     summed = lax.dot_general(
         onehot, returned[...], (((0,), (0,)), ((), ())), preferred_element_type=jnp.float32
     )
     aggregated[...] = summed[:, :width].astype(jnp.bfloat16)
-    sent = column_sum[...] + to_below[...].astype(jnp.float32) + to_above[...].astype(jnp.float32)
-    grad = dot_t(sent.astype(jnp.bfloat16), w_back[:width, :])
-    grad += dot_t(summed[:, width:].astype(jnp.bfloat16), w_back[width:, :])
+    sent = column_sum[:owned, :] + to_below[...].astype(jnp.float32) + to_above[...].astype(jnp.float32)
+    grad = dot_t(sent.astype(jnp.bfloat16), w_in[width : 2 * width, :])
+    grad += dot_t(summed[:, width:].astype(jnp.bfloat16), w_in[2 * width :, :])
     grad_nodes[...] = grad.astype(jnp.bfloat16)
 
 
@@ -133,18 +130,21 @@
     down = [(b, a) for a, b in up]
     my_h = lax.axis_index("col") % Z_HI
 
-    from_below = lax.ppermute(node_latents, "col", up)
-    from_above = lax.ppermute(node_latents, "col", down)
+    own = jnp.concatenate([node_latents, agg_cotangent], axis=1)
+    latents, own = lax.optimization_barrier((node_latents, own))
+    from_below = lax.ppermute(latents, "col", up)
+    from_above = lax.ppermute(latents, "col", down)
     asked = lax.all_to_all(edge_receiver.reshape(rows, 1, per_block), "row", 0, 0, tiled=True)
     answer = pl.pallas_call(
         answer_kernel,
-        in_specs=[VMEM] * 3,
+        in_specs=[VMEM] * 2,
         out_specs=VMEM,
         out_shape=jax.ShapeDtypeStruct((slots, 2 * width), jnp.bfloat16),
         cost_estimate=pl.CostEstimate(
-            flops=2 * slots * owned * 2 * width, bytes_accessed=640 * 1024, transcendentals=0
-        ),
-    )(asked, node_latents, agg_cotangent)
+            flops=4_000_000_000, bytes_accessed=640 * 1024, transcendentals=0
+        ),
+        compiler_params=pltpu.CompilerParams(vmem_limit_bytes=16 * 1024 * 1024),
+    )(asked, own)
     answer, from_below, from_above = lax.optimization_barrier((answer, from_below, from_above))
     recv = lax.all_to_all(answer, "row", 0, 0, tiled=True)
     column = jnp.concatenate([node_latents, from_below, from_above], axis=0)
@@ -195,7 +195,8 @@
         cost_estimate=pl.CostEstimate(
             flops=2 * owned * width * (2 * slots + 2 * width), bytes_accessed=2 * 1024 * 1024, transcendentals=0
         ),
-    )(asked, returned, column_sum[:owned], to_below, to_above, w_in[width:])
+        compiler_params=pltpu.CompilerParams(vmem_limit_bytes=16 * 1024 * 1024),
+    )(asked, returned, column_sum, to_below, to_above, w_in)
     d_edge = dot_t(packed[:, width:], w_in[:width])
     grad_edges = (edge_cotangent.astype(jnp.float32) + d_edge).astype(jnp.bfloat16)
     return (new_edges, aggregated, grad_nodes, grad_edges)

time: 128 us -> 130 us (1.016)
  the two profiles are of different devices: /device:TPU:69 before, /device:TPU:1 now
where the time goes in v4:
time: 130 us; the launch traced here: 129 us
  starting transfers between devices  58.3 us (45%)
  blocking collectives  45.4 us (35%)
  waiting for transfers between devices  12.8 us (10%)
  Pallas kernels  5.33 us (4%)
  local copies, waits for them, and re-layouts  3.32 us (3%)
  matrix products  1.99 us (2%)
    all_gather x1, blocking collectives, on_device(): lax.all_gather(column, 'col', axis=0, tiled=True, axis_index_groups=along_y)  23 us
    all_to_all x1, blocking collectives, on_device(): lax.all_to_all(partial, 'col', 0, 0, tiled=True, axis_index_groups=along_y)  22.4 us
    all_to_all x1, starting transfers between devices, on_device(): lax.all_to_all(edge_receiver.reshape(rows, 1, per_block), 'row', 0, 0, ti...  14 us
    all_to_all x1, starting transfers between devices, on_device(): returned = lax.all_to_all(packed, 'row', 0, 0, tiled=True)  13.7 us
    all_to_all x1, starting transfers between devices, on_device(): recv = lax.all_to_all(answer, 'row', 0, 0, tiled=True)  10.4 us
    ppermute x1, starting transfers between devices, on_device(): from_above = lax.ppermute(latents, 'col', down)  9.1 us
    ppermute x1, starting transfers between devices, on_device(): to_below = lax.ppermute(away[owned:2 * owned], 'col', down)  7.27 us
    ppermute x1, waiting for transfers between devices, on_device(): from_below = lax.ppermute(latents, 'col', up)  5.67 us
  transfers between devices with their start and end apart: 7, of which 3 were waited for; matrix products, arithmetic and copies ran while one was open for 2% of the time, Pallas kernels for 1%

profile of v4, /device:TPU:1, one launch (start us, length us, event | category | flops | bytes accessed | tf_op | source)
XLA Modules:
  0.0 129.0 jit_solution(6239635757330020231)
XLA Ops:
  0.6 1.4 %reshape.22 = s32[32,1,8]{2,0,1:T(8,128)} reshape(s32[256]{0:T(256)} %param.16) | data formatting | bytes 2048 | tf_op jit(solution)/shard_map/reshape | solution.py:137
  2.0 14.0 %all-to-all-start = ((s32[32,1,8]{2,1,0:T(1,128)}), s32[32,1,8]{2,1,0:T(1,128)S(1)}, u32[]{:S(2)}, u32[]{:S(2)}) async-start(s32[32,1,8]{2,1,0:T(1,128)} %bitcast), calls=%async_computation | async-start | bytes 32768 | tf_op jit(solution)/shard_map/all_to_all | solution.py:137
  16.0 0.8 pad_maximum_fusion.1.own
  16.8 0.0 copy-start.7
  16.8 0.0 copy-start.8
  16.8 0.0 copy-start.9
  16.8 0.0 copy-start.10
  16.8 0.0 copy-start.11
  16.8 0.0 copy-start.6
  16.8 9.1 %collective-permute-start.1 = (bf16[32,512]{1,0:T(8,128)(2,1)}, bf16[32,512]{1,0:T(8,128)(2,1)S(1)}, u32[]{:S(2)}, u32[]{:S(2)}) collective-permute-start(bf16[32,512]{1,0:T(8,128)(2,1)} %param.13), channel_id=1, source_target_pairs={{1,0},{2,1},{0,2},{4,3},{5,4},{3,5},{7,6},{8,7},{6,8},{10,9},{11,1... | collective-permute-start | bytes 98312 | tf_op jit(solution)/shard_map/ppermute | solution.py:136
  25.9 1.9 %collective-permute-start = (bf16[32,512]{1,0:T(8,128)(2,1)}, bf16[32,512]{1,0:T(8,128)(2,1)S(1)}, u32[]{:S(2)}, u32[]{:S(2)}) collective-permute-start(bf16[32,512]{1,0:T(8,128)(2,1)} %param.13), channel_id=1, source_target_pairs={{0,1},{1,2},{2,0},{3,4},{4,5},{5,3},{6,7},{7,8},{8,6},{9,10},{10,1... | collective-permute-start | bytes 98312 | tf_op jit(solution)/shard_map/ppermute | solution.py:135
  27.9 0.0 all-to-all-done.asked
  27.9 1.2 shard_map.156
  29.1 0.0 copy-start
  29.1 0.0 copy-start.1
  29.1 0.0 copy-start.5
  29.1 0.0 collective-permute-done.1
  29.1 5.7 %collective-permute-done = bf16[32,512]{1,0:T(8,128)(2,1)S(1)} collective-permute-done((bf16[32,512]{1,0:T(8,128)(2,1)}, bf16[32,512]{1,0:T(8,128)(2,1)S(1)}, u32[]{:S(2)}, u32[]{:S(2)}) %collective-permute-start) | collective-permute-done | bytes 32800 | tf_op jit(solution)/shard_map/ppermute | solution.py:135
  34.8 10.4 %all-to-all-start.1 = ((bf16[32,8,1024]{2,1,0:T(8,128)(2,1)}), bf16[32,8,1024]{2,1,0:T(8,128)(2,1)S(1)}, u32[]{:S(2)}, u32[]{:S(2)}) async-start(bf16[32,8,1024]{2,1,0:T(8,128)(2,1)} %bitcast.2), calls=%async_computation.1 | async-start | bytes 1048576 | tf_op jit(solution)/shard_map/all_to_all | solution.py:149
  45.2 0.0 copy-done.7
  45.2 0.0 copy-done.8
  45.2 0.0 copy-done.9
  45.2 0.0 copy-done.10
  45.3 0.0 copy-done.11
  45.3 0.0 copy-done.6
  45.3 23.0 %all_gather.3.table = bf16[768,512]{1,0:T(8,128)(2,1)S(1)} all-gather(bf16[96,512]{1,0:T(8,128)(2,1)S(1)} %pad_maximum_fusion), channel_id=1, replica_groups={{0,3,6,9,12,15,18,21},{1,4,7,10,13,16,19,22},{2,5,8,11,14,17,20,23},{24..., dimensions={0}, use_global_device_ids=true | all-gather | bytes 884736 | tf_op jit(solution)/shard_map/all_gather | solution.py:151
  68.3 0.0 all-to-all-done.1
  68.3 0.0 copy-done
  68.3 0.0 copy-done.1
  68.3 0.0 copy-done.5
  68.3 0.0 copy-start.2
  68.3 0.9 copy-done.2
  69.3 0.0 copy-start.3
  69.3 0.9 copy-done.3
  70.2 2.8 %shard_map.157 = (bf16[256,512]{1,0:T(8,128)(2,1)}, bf16[256,1024]{1,0:T(8,128)(2,1)}, bf16[768,512]{1,0:T(8,128)(2,1)S(1)}) custom-call(bf16[768,512]{1,0:T(8,128)(2,1)S(1)} %all_gather.3.table, s32[1,256]{1,0:T(1,128)S(1)} %bitcast.14, bf16[256,1024]{1,0:T(8,128)(2,1)S(1)} %bitcast.13, s32[1,32]{1,0:T(1,128)S(1)} %copy-done.5, ...), custom_call_target="tpu_custom_call" | custom-call | flops 1073741824 | bytes 6291456 | tf_op jit(solution)/shard_map/pallas_call | solution.py:158
  73.1 22.4 %all_to_all.36 = bf16[8,96,512]{2,1,0:T(8,128)(2,1)S(1)} all-to-all(bf16[8,96,512]{2,1,0:T(8,128)(2,1)S(1)} %bitcast.12), channel_id=1, replica_groups={{0,3,6,9,12,15,18,21},{1,4,7,10,13,16,19,22},{2,5,8,11,14,17,20,23},{24..., dimensions={0} | all-to-all | bytes 1572864 | tf_op jit(solution)/shard_map/all_to_all | solution.py:183
  95.5 0.0 copy-start.4
  95.5 13.7 %all-to-all-start.2 = ((bf16[32,8,1024]{2,1,0:T(8,128)(2,1)}), bf16[32,8,1024]{2,1,0:T(8,128)(2,1)S(1)}, u32[]{:S(2)}, u32[]{:S(2)}) async-start(bf16[32,8,1024]{2,1,0:T(8,128)(2,1)} %bitcast.8), calls=%async_computation.2 | async-start | bytes 1048576 | tf_op jit(solution)/shard_map/all_to_all | solution.py:189
  109.2 0.1 convert_reduce_fusion.column_sum
  109.3 1.9 %collective-permute-start.3 = (bf16[32,512]{1,0:T(8,128)(2,1)S(1)}, bf16[32,512]{1,0:T(8,128)(2,1)S(1)}, u32[]{:S(2)}, u32[]{:S(2)}) collective-permute-start(bf16[32,512]{1,0:T(8,128)(2,1)S(1)} %get-tuple-element.24), channel_id=1, source_target_pairs={{0,1},{1,2},{2,0},{3,4},{4,5},{5,3},{6,7},{7,8},{8,6},{9,10},{10,1... | collective-permute-start | bytes 98312 | tf_op jit(solution)/shard_map/ppermute | solution.py:187
  111.3 7.3 %collective-permute-start.2 = (bf16[32,512]{1,0:T(8,128)(2,1)S(1)}, bf16[32,512]{1,0:T(8,128)(2,1)S(1)}, u32[]{:S(2)}, u32[]{:S(2)}) collective-permute-start(bf16[32,512]{1,0:T(8,128)(2,1)S(1)} %get-tuple-element.25), channel_id=1, source_target_pairs={{1,0},{2,1},{0,2},{4,3},{5,4},{3,5},{7,6},{8,7},{6,8},{10,9},{11,1... | collective-permute-start | bytes 98312 | tf_op jit(solution)/shard_map/ppermute | solution.py:186
  118.5 0.0 copy-done.4
  118.6 2.0 %fusion = bf16[256,512]{1,0:T(8,128)(2,1)} fusion(bf16[1536,512]{1,0:T(8,128)(2,1)S(1)} %copy-done, bf16[256,512]{1,0:T(8,128)(2,1)S(1)} %copy-done.4, bf16[256,1024]{1,0:T(8,128)(2,1)} %get-tuple-element.20), kind=kOutput, calls=%fused_computation.2 | convolution fusion | flops 134610944 | bytes 1310720 | tf_op jit(solution)/shard_map/dot_general | solution.py:18
  120.5 1.7 %collective-permute-done.3.to_above = bf16[32,512]{1,0:T(8,128)(2,1)S(1)} collective-permute-done((bf16[32,512]{1,0:T(8,128)(2,1)S(1)}, bf16[32,512]{1,0:T(8,128)(2,1)S(1)}, u32[]{:S(2)}, u32[]{:S(2)}) %collective-permute-start.3) | collective-permute-done | bytes 32800 | tf_op jit(solution)/shard_map/ppermute | solution.py:187
  122.2 0.0 collective-permute-done.2.to_below
  122.2 5.5 %all-to-all-done.2 = bf16[32,8,1024]{2,1,0:T(8,128)(2,1)S(1)} async-done(((bf16[32,8,1024]{2,1,0:T(8,128)(2,1)}), bf16[32,8,1024]{2,1,0:T(8,128)(2,1)S(1)}, u32[]{:S(2)}, u32[]{:S(2)}) %all-to-all-start.2) | async-done | bytes 524320 | tf_op jit(solution)/shard_map/all_to_all | solution.py:189
  127.7 1.3 %shard_map.158 = (bf16[32,512]{1,0:T(8,128)(2,1)}, bf16[32,512]{1,0:T(8,128)(2,1)}) custom-call(s32[32,1,8]{2,1,0:T(1,128)S(1)} %all-to-all-done.asked, bf16[256,1024]{1,0:T(8,128)(2,1)S(1)} %bitcast.11, f32[96,512]{1,0:T(8,128)S(1)} %convert_reduce_fusion.column_sum, bf16[32,512]{1,0:T(8,128)(2,1)S(1)} %collective-permute-done.2.to_below, ...), custom_call_target="tpu_custom_call" | custom-call | flops 50331648 | bytes 2097152 | tf_op jit(solution)/shard_map/pallas_call | solution.py:190
  (5 shorter events, 0.1 us)
Async XLA Ops:
  2.0 25.9 %all-to-all-start = ((s32[32,1,8]{2,1,0:T(1,128)}), s32[32,1,8]{2,1,0:T(1,128)S(1)}, u32[]{:S(2)}, u32[]{:S(2)}) async-start(s32[32,1,8]{2,1,0:T(1,128)} %bitcast), calls=%async_computation | async-start | bytes 32768 | tf_op jit(solution)/shard_map/all_to_all | solution.py:137
  16.8 28.4 %copy-start.7 = (f32[512]{0:T(512)S(1)}, f32[512]{0:T(512)}, u32[]{:S(2)}) copy-start(f32[512]{0:T(512)} %param.23) | copy-start | bytes 6148
  16.8 28.4 %copy-start.8 = (f32[512]{0:T(512)S(1)}, f32[512]{0:T(512)}, u32[]{:S(2)}) copy-start(f32[512]{0:T(512)} %param.22) | copy-start | bytes 6148
  16.8 28.4 %copy-start.9 = (f32[512]{0:T(512)S(1)}, f32[512]{0:T(512)}, u32[]{:S(2)}) copy-start(f32[512]{0:T(512)} %param.21) | copy-start | bytes 6148
  16.8 28.4 %copy-start.10 = (f32[512]{0:T(512)S(1)}, f32[512]{0:T(512)}, u32[]{:S(2)}) copy-start(f32[512]{0:T(512)} %param.19) | copy-start | bytes 6148
  16.8 28.5 %copy-start.11 = (s32[256]{0:T(256)S(1)}, s32[256]{0:T(256)}, u32[]{:S(2)}) copy-start(s32[256]{0:T(256)} %param.15) | copy-start | bytes 3076
  16.8 28.5 %copy-start.6 = (bf16[32,512]{1,0:T(8,128)(2,1)S(1)}, bf16[32,512]{1,0:T(8,128)(2,1)}, u32[]{:S(2)}) copy-start(bf16[32,512]{1,0:T(8,128)(2,1)} %param.13) | copy-start | bytes 98308
  16.8 12.2 %collective-permute-start.1 = (bf16[32,512]{1,0:T(8,128)(2,1)}, bf16[32,512]{1,0:T(8,128)(2,1)S(1)}, u32[]{:S(2)}, u32[]{:S(2)}) collective-permute-start(bf16[32,512]{1,0:T(8,128)(2,1)} %param.13), channel_id=1, source_target_pairs={{1,0},{2,1},{0,2},{4,3},{5,4},{3,5},{7,6},{8,7},{6,8},{10,9},{11,1... | collective-permute-start | bytes 98312 | tf_op jit(solution)/shard_map/ppermute | solution.py:136
  25.9 8.8 %collective-permute-start = (bf16[32,512]{1,0:T(8,128)(2,1)}, bf16[32,512]{1,0:T(8,128)(2,1)S(1)}, u32[]{:S(2)}, u32[]{:S(2)}) collective-permute-start(bf16[32,512]{1,0:T(8,128)(2,1)} %param.13), channel_id=1, source_target_pairs={{0,1},{1,2},{2,0},{3,4},{4,5},{5,3},{6,7},{7,8},{8,6},{9,10},{10,1... | collective-permute-start | bytes 98312 | tf_op jit(solution)/shard_map/ppermute | solution.py:135
  29.1 39.2 %copy-start = (bf16[1536,512]{1,0:T(8,128)(2,1)S(1)}, bf16[1536,512]{1,0:T(8,128)(2,1)}, u32[]{:S(2)}) copy-start(bf16[1536,512]{1,0:T(8,128)(2,1)} %w_in.3) | copy-start | bytes 4718596
  29.1 39.2 %copy-start.1 = (bf16[512,512]{1,0:T(8,128)(2,1)S(1)}, bf16[512,512]{1,0:T(8,128)(2,1)}, u32[]{:S(2)}) copy-start(bf16[512,512]{1,0:T(8,128)(2,1)} %w_out.1) | copy-start | bytes 1572868
  29.1 39.2 %copy-start.5 = (s32[1,32]{1,0:T(1,128)S(1)}, s32[1,32]{1,0:T(1,128)}, u32[]{:S(2)}) copy-start(s32[1,32]{1,0:T(1,128)} %counts.1) | copy-start | bytes 388
  34.8 33.5 %all-to-all-start.1 = ((bf16[32,8,1024]{2,1,0:T(8,128)(2,1)}), bf16[32,8,1024]{2,1,0:T(8,128)(2,1)S(1)}, u32[]{:S(2)}, u32[]{:S(2)}) async-start(bf16[32,8,1024]{2,1,0:T(8,128)(2,1)} %bitcast.2), calls=%async_computation.1 | async-start | bytes 1048576 | tf_op jit(solution)/shard_map/all_to_all | solution.py:149
  68.3 1.0 copy-start.2
  69.3 0.9 copy-start.3
  95.5 23.1 %copy-start.4 = (bf16[256,512]{1,0:T(8,128)(2,1)S(1)}, bf16[256,512]{1,0:T(8,128)(2,1)}, u32[]{:S(2)}) copy-start(bf16[256,512]{1,0:T(8,128)(2,1)} %cot_hbm.1) | copy-start | bytes 786436
  95.5 32.2 %all-to-all-start.2 = ((bf16[32,8,1024]{2,1,0:T(8,128)(2,1)}), bf16[32,8,1024]{2,1,0:T(8,128)(2,1)S(1)}, u32[]{:S(2)}, u32[]{:S(2)}) async-start(bf16[32,8,1024]{2,1,0:T(8,128)(2,1)} %bitcast.8), calls=%async_computation.2 | async-start | bytes 1048576 | tf_op jit(solution)/shard_map/all_to_all | solution.py:189
  109.3 12.9 %collective-permute-start.3 = (bf16[32,512]{1,0:T(8,128)(2,1)S(1)}, bf16[32,512]{1,0:T(8,128)(2,1)S(1)}, u32[]{:S(2)}, u32[]{:S(2)}) collective-permute-start(bf16[32,512]{1,0:T(8,128)(2,1)S(1)} %get-tuple-element.24), channel_id=1, source_target_pairs={{0,1},{1,2},{2,0},{3,4},{4,5},{5,3},{6,7},{7,8},{8,6},{9,10},{10,1... | collective-permute-start | bytes 98312 | tf_op jit(solution)/shard_map/ppermute | solution.py:187
  111.3 10.9 %collective-permute-start.2 = (bf16[32,512]{1,0:T(8,128)(2,1)S(1)}, bf16[32,512]{1,0:T(8,128)(2,1)S(1)}, u32[]{:S(2)}, u32[]{:S(2)}) collective-permute-start(bf16[32,512]{1,0:T(8,128)(2,1)S(1)} %get-tuple-element.25), channel_id=1, source_target_pairs={{1,0},{2,1},{0,2},{4,3},{5,4},{3,5},{7,6},{8,7},{6,8},{10,9},{11,1... | collective-permute-start | bytes 98312 | tf_op jit(solution)/shard_map/ppermute | solution.py:186

commit v5 on v4

--- a/solution.py
+++ b/solution.py
@@ -33,17 +33,23 @@
 
 
 def edge_kernel(
-    table, spread, recv, counts, w_in, w_out, vectors, edges_hbm, cot_hbm,
+    table, spread, recv, counts, w_out, vectors, w_hbm, edges_hbm, cot_hbm,
     new_edges, packed, partial,
-    edges, edge_cot, sems,
+    w_in, edges, edge_cot, sems,
 ):
     slots, width = edges.shape
     group = table.shape[0]
     per_block = slots // counts.shape[1]
     edges_copy = pltpu.make_async_copy(edges_hbm, edges, sems.at[0])
     cot_copy = pltpu.make_async_copy(cot_hbm, edge_cot, sems.at[1])
-    edges_copy.start()
-    cot_copy.start()
+    w_copies = [
+        pltpu.make_async_copy(
+            w_hbm.at[pl.ds(part * width, width), :], w_in.at[pl.ds(part * width, width), :], sems.at[2 + part]
+        )
+        for part in range(3)
+    ]
+    for copy in (w_copies[1], w_copies[2], edges_copy, w_copies[0], cot_copy):
+        copy.start()
     b_in, b_out = vectors[0:1, :], vectors[1:2, :]
     gain, bias = vectors[2:3, :], vectors[3:4, :]
     diagonal = lax.broadcasted_iota(jnp.int32, (slots, slots), 0) == lax.broadcasted_iota(
@@ -57,9 +63,12 @@
     lane = lax.broadcasted_iota(jnp.int32, (slots, group), 1)
     chosen = jnp.where(pick == lane, 1.0, 0.0).astype(jnp.bfloat16)
     send_feat = dot(chosen, table[...]).astype(jnp.bfloat16)
-    pre = dot(recv[:, :width], w_in[2 * width :, :])
-    pre += dot(send_feat, w_in[width : 2 * width, :])
+    w_copies[1].wait()
+    pre = dot(send_feat, w_in[width : 2 * width, :])
+    w_copies[2].wait()
+    pre += dot(recv[:, :width], w_in[2 * width :, :])
     edges_copy.wait()
+    w_copies[0].wait()
     pre += dot(edges[...], w_in[:width, :])
     pre += b_in
     sigma = jax.nn.sigmoid(pre)
@@ -131,9 +140,8 @@
     my_h = lax.axis_index("col") % Z_HI
 
     own = jnp.concatenate([node_latents, agg_cotangent], axis=1)
-    latents, own = lax.optimization_barrier((node_latents, own))
-    from_below = lax.ppermute(latents, "col", up)
-    from_above = lax.ppermute(latents, "col", down)
+    from_below = lax.ppermute(node_latents, "col", up)
+    from_above = lax.ppermute(node_latents, "col", down)
     asked = lax.all_to_all(edge_receiver.reshape(rows, 1, per_block), "row", 0, 0, tiled=True)
     answer = pl.pallas_call(
         answer_kernel,
@@ -157,7 +165,7 @@
 
     new_edges, packed, partial = pl.pallas_call(
         edge_kernel,
-        in_specs=[VMEM] * 7 + [ANY] * 2,
+        in_specs=[VMEM] * 6 + [ANY] * 3,
         out_specs=[VMEM] * 3,
         out_shape=[
             jax.ShapeDtypeStruct((slots, width), jnp.bfloat16),
@@ -165,19 +173,20 @@
             jax.ShapeDtypeStruct((cols * owned, width), jnp.bfloat16),
         ],
         scratch_shapes=[
+            pltpu.VMEM((3 * width, width), jnp.bfloat16),
             pltpu.VMEM((slots, width), jnp.bfloat16),
             pltpu.VMEM((slots, width), jnp.bfloat16),
-            pltpu.SemaphoreType.DMA((2,)),
+            pltpu.SemaphoreType.DMA((5,)),
         ],
-        compiler_params=pltpu.CompilerParams(vmem_limit_bytes=40 * 1024 * 1024),
+        compiler_params=pltpu.CompilerParams(vmem_limit_bytes=50 * 1024 * 1024),
         cost_estimate=pl.CostEstimate(
             flops=2 * slots * width * (5 * width + 2 * cols * owned),
             bytes_accessed=6 * 1024 * 1024,
             transcendentals=slots * width,
         ),
     )(
-        table, place.reshape(1, slots), recv, edge_count, w_in, w_out, vectors,
-        edge_latents, edge_cotangent,
+        table, place.reshape(1, slots), recv, edge_count, w_out, vectors,
+        w_in, edge_latents, edge_cotangent,
     )
 
     parts = lax.all_to_all(partial, "col", 0, 0, tiled=True, axis_index_groups=along_y)

time: 130 us -> 124 us (0.954)
  the two profiles are of different devices: /device:TPU:1 before, /device:TPU:69 now
where the time goes in v5:
time: 124 us
  starting transfers between devices  55 us (44%)
  blocking collectives  44.3 us (36%)
  waiting for transfers between devices  12.7 us (10%)
  Pallas kernels  6.18 us (5%)
  matrix products  1.99 us (2%)
  local copies, waits for them, and re-layouts  1.43 us (1%)
    all_gather x1, blocking collectives, on_device(): lax.all_gather(column, 'col', axis=0, tiled=True, axis_index_groups=along_y)  23 us
    all_to_all x1, blocking collectives, on_device(): lax.all_to_all(partial, 'col', 0, 0, tiled=True, axis_index_groups=along_y)  21.3 us
    all_to_all x1, starting transfers between devices, on_device(): returned = lax.all_to_all(packed, 'row', 0, 0, tiled=True)  14.7 us
    ppermute x1, starting transfers between devices, on_device(): from_below = lax.ppermute(node_latents, 'col', up)  10.6 us
    ppermute x1, waiting for transfers between devices, on_device(): to_above = lax.ppermute(away[2 * owned:], 'col', up)  9.2 us
    all_to_all x1, starting transfers between devices, on_device(): lax.all_to_all(edge_receiver.reshape(rows, 1, per_block), 'row', 0, 0, ti...  8.28 us
    all_to_all x1, starting transfers between devices, on_device(): recv = lax.all_to_all(answer, 'row', 0, 0, tiled=True)  7.3 us
    ppermute x1, starting transfers between devices, on_device(): to_above = lax.ppermute(away[2 * owned:], 'col', up)  6.31 us
  transfers between devices with their start and end apart: 7, of which 2 were waited for; matrix products, arithmetic and copies ran while one was open for 4% of the time, Pallas kernels for 1%

profile of v5, /device:TPU:69, one launch (start us, length us, event | category | flops | bytes accessed | tf_op | source)
XLA Modules:
  0.0 123.6 jit_solution(3819205593328501837)
XLA Ops:
  0.6 10.6 %collective-permute-start = (bf16[32,512]{1,0:T(8,128)(2,1)}, bf16[32,512]{1,0:T(8,128)(2,1)S(1)}, u32[]{:S(2)}, u32[]{:S(2)}) collective-permute-start(bf16[32,512]{1,0:T(8,128)(2,1)} %param.13), channel_id=1, source_target_pairs={{0,1},{1,2},{2,0},{3,4},{4,5},{5,3},{6,7},{7,8},{8,6},{9,10},{10,1... | collective-permute-start | bytes 98312 | tf_op jit(solution)/shard_map/ppermute | solution.py:143
  11.3 4.7 %collective-permute-start.1 = (bf16[32,512]{1,0:T(8,128)(2,1)}, bf16[32,512]{1,0:T(8,128)(2,1)S(1)}, u32[]{:S(2)}, u32[]{:S(2)}) collective-permute-start(bf16[32,512]{1,0:T(8,128)(2,1)} %param.13), channel_id=1, source_target_pairs={{1,0},{2,1},{0,2},{4,3},{5,4},{3,5},{7,6},{8,7},{6,8},{10,9},{11,1... | collective-permute-start | bytes 98312 | tf_op jit(solution)/shard_map/ppermute | solution.py:144
  15.9 1.4 %reshape.22 = s32[32,1,8]{2,0,1:T(8,128)} reshape(s32[256]{0:T(256)} %param.16) | data formatting | bytes 2048 | tf_op jit(solution)/shard_map/reshape | solution.py:145
  17.3 8.3 %all-to-all-start = ((s32[32,1,8]{2,1,0:T(1,128)}), s32[32,1,8]{2,1,0:T(1,128)S(1)}, u32[]{:S(2)}, u32[]{:S(2)}) async-start(s32[32,1,8]{2,1,0:T(1,128)} %bitcast), calls=%async_computation | async-start | bytes 32768 | tf_op jit(solution)/shard_map/all_to_all | solution.py:145
  25.6 0.8 pad_maximum_fusion.1.own
  26.4 0.0 copy-start.6
  26.4 0.0 copy-start.7
  26.4 0.0 copy-start.8
  26.4 0.0 copy-start.9
  26.4 0.0 copy-start.10
  26.4 0.0 copy-start.5
  26.4 3.5 %all-to-all-done.asked = s32[32,1,8]{2,1,0:T(1,128)S(1)} async-done(((s32[32,1,8]{2,1,0:T(1,128)}), s32[32,1,8]{2,1,0:T(1,128)S(1)}, u32[]{:S(2)}, u32[]{:S(2)}) %all-to-all-start) | async-done | bytes 1056 | tf_op jit(solution)/shard_map/all_to_all | solution.py:145
  29.9 1.2 shard_map.156
  31.1 0.0 copy-start.1
  31.1 0.0 copy-start.2
  31.1 0.0 copy-start.3
  31.1 0.0 copy-start.4
  31.1 0.0 collective-permute-done
  31.1 0.0 collective-permute-done.1
  31.1 7.3 %all-to-all-start.1 = ((bf16[32,8,1024]{2,1,0:T(8,128)(2,1)}), bf16[32,8,1024]{2,1,0:T(8,128)(2,1)S(1)}, u32[]{:S(2)}, u32[]{:S(2)}) async-start(bf16[32,8,1024]{2,1,0:T(8,128)(2,1)} %bitcast.2), calls=%async_computation.1 | async-start | bytes 1048576 | tf_op jit(solution)/shard_map/all_to_all | solution.py:157
  38.5 0.0 copy-done.6
  38.5 0.0 copy-done.7
  38.5 0.0 copy-done.8
  38.5 0.0 copy-done.9
  38.5 0.0 copy-done.10
  38.6 0.0 copy-done.5
  38.6 23.0 %all_gather.3.table = bf16[768,512]{1,0:T(8,128)(2,1)S(1)} all-gather(bf16[96,512]{1,0:T(8,128)(2,1)S(1)} %pad_maximum_fusion), channel_id=1, replica_groups={{0,3,6,9,12,15,18,21},{1,4,7,10,13,16,19,22},{2,5,8,11,14,17,20,23},{24..., dimensions={0}, use_global_device_ids=true | all-gather | bytes 884736 | tf_op jit(solution)/shard_map/all_gather | solution.py:159
  61.6 0.0 all-to-all-done.1
  61.6 0.0 copy-done.1
  61.6 0.0 copy-done.2
  61.6 0.0 copy-done.3
  61.6 0.0 copy-done.4
  61.6 3.7 %shard_map.157 = (bf16[256,512]{1,0:T(8,128)(2,1)}, bf16[256,1024]{1,0:T(8,128)(2,1)}, bf16[768,512]{1,0:T(8,128)(2,1)S(1)}) custom-call(bf16[768,512]{1,0:T(8,128)(2,1)S(1)} %all_gather.3.table, s32[1,256]{1,0:T(1,128)S(1)} %bitcast.14, bf16[256,1024]{1,0:T(8,128)(2,1)S(1)} %bitcast.13, s32[1,32]{1,0:T(1,128)S(1)} %copy-done.4, ...), custom_call_target="tpu_custom_call" | custom-call | flops 1073741824 | bytes 6291456 | tf_op jit(solution)/shard_map/pallas_call | solution.py:166
  65.3 21.3 %all_to_all.36 = bf16[8,96,512]{2,1,0:T(8,128)(2,1)S(1)} all-to-all(bf16[8,96,512]{2,1,0:T(8,128)(2,1)S(1)} %bitcast.12), channel_id=1, replica_groups={{0,3,6,9,12,15,18,21},{1,4,7,10,13,16,19,22},{2,5,8,11,14,17,20,23},{24..., dimensions={0} | all-to-all | bytes 1572864 | tf_op jit(solution)/shard_map/all_to_all | solution.py:192
  86.7 0.0 copy-start
  86.7 14.7 %all-to-all-start.2 = ((bf16[32,8,1024]{2,1,0:T(8,128)(2,1)}), bf16[32,8,1024]{2,1,0:T(8,128)(2,1)S(1)}, u32[]{:S(2)}, u32[]{:S(2)}) async-start(bf16[32,8,1024]{2,1,0:T(8,128)(2,1)} %bitcast.8), calls=%async_computation.2 | async-start | bytes 1048576 | tf_op jit(solution)/shard_map/all_to_all | solution.py:198
  101.4 0.1 convert_reduce_fusion.column_sum
  101.5 6.3 %collective-permute-start.3 = (bf16[32,512]{1,0:T(8,128)(2,1)S(1)}, bf16[32,512]{1,0:T(8,128)(2,1)S(1)}, u32[]{:S(2)}, u32[]{:S(2)}) collective-permute-start(bf16[32,512]{1,0:T(8,128)(2,1)S(1)} %get-tuple-element.20), channel_id=1, source_target_pairs={{0,1},{1,2},{2,0},{3,4},{4,5},{5,3},{6,7},{7,8},{8,6},{9,10},{10,1... | collective-permute-start | bytes 98312 | tf_op jit(solution)/shard_map/ppermute | solution.py:196
  107.8 3.2 %collective-permute-start.2 = (bf16[32,512]{1,0:T(8,128)(2,1)S(1)}, bf16[32,512]{1,0:T(8,128)(2,1)S(1)}, u32[]{:S(2)}, u32[]{:S(2)}) collective-permute-start(bf16[32,512]{1,0:T(8,128)(2,1)S(1)} %get-tuple-element.21), channel_id=1, source_target_pairs={{1,0},{2,1},{0,2},{4,3},{5,4},{3,5},{7,6},{8,7},{6,8},{10,9},{11,1... | collective-permute-start | bytes 98312 | tf_op jit(solution)/shard_map/ppermute | solution.py:195
  111.0 0.0 copy-done
  111.0 2.0 %fusion = bf16[256,512]{1,0:T(8,128)(2,1)} fusion(bf16[1536,512]{1,0:T(8,128)(2,1)S(1)} %copy-done, bf16[256,512]{1,0:T(8,128)(2,1)S(1)} %copy-done.3, bf16[256,1024]{1,0:T(8,128)(2,1)} %get-tuple-element.16), kind=kOutput, calls=%fused_computation.2 | convolution fusion | flops 134610944 | bytes 1310720 | tf_op jit(solution)/shard_map/dot_general | solution.py:18
  113.0 9.2 %collective-permute-done.3.to_above = bf16[32,512]{1,0:T(8,128)(2,1)S(1)} collective-permute-done((bf16[32,512]{1,0:T(8,128)(2,1)S(1)}, bf16[32,512]{1,0:T(8,128)(2,1)S(1)}, u32[]{:S(2)}, u32[]{:S(2)}) %collective-permute-start.3) | collective-permute-done | bytes 32800 | tf_op jit(solution)/shard_map/ppermute | solution.py:196
  122.2 0.0 collective-permute-done.2.to_below
  122.2 0.0 all-to-all-done.2
  122.2 1.3 %shard_map.158 = (bf16[32,512]{1,0:T(8,128)(2,1)}, bf16[32,512]{1,0:T(8,128)(2,1)}) custom-call(s32[32,1,8]{2,1,0:T(1,128)S(1)} %all-to-all-done.asked, bf16[256,1024]{1,0:T(8,128)(2,1)S(1)} %bitcast.11, f32[96,512]{1,0:T(8,128)S(1)} %convert_reduce_fusion.column_sum, bf16[32,512]{1,0:T(8,128)(2,1)S(1)} %collective-permute-done.2.to_below, ...), custom_call_target="tpu_custom_call" | custom-call | flops 50331648 | bytes 2097152 | tf_op jit(solution)/shard_map/pallas_call | solution.py:199
  (5 shorter events, 0.1 us)
Async XLA Ops:
  0.6 30.5 %collective-permute-start = (bf16[32,512]{1,0:T(8,128)(2,1)}, bf16[32,512]{1,0:T(8,128)(2,1)S(1)}, u32[]{:S(2)}, u32[]{:S(2)}) collective-permute-start(bf16[32,512]{1,0:T(8,128)(2,1)} %param.13), channel_id=1, source_target_pairs={{0,1},{1,2},{2,0},{3,4},{4,5},{5,3},{6,7},{7,8},{8,6},{9,10},{10,1... | collective-permute-start | bytes 98312 | tf_op jit(solution)/shard_map/ppermute | solution.py:143
  11.3 19.9 %collective-permute-start.1 = (bf16[32,512]{1,0:T(8,128)(2,1)}, bf16[32,512]{1,0:T(8,128)(2,1)S(1)}, u32[]{:S(2)}, u32[]{:S(2)}) collective-permute-start(bf16[32,512]{1,0:T(8,128)(2,1)} %param.13), channel_id=1, source_target_pairs={{1,0},{2,1},{0,2},{4,3},{5,4},{3,5},{7,6},{8,7},{6,8},{10,9},{11,1... | collective-permute-start | bytes 98312 | tf_op jit(solution)/shard_map/ppermute | solution.py:144
  17.3 12.6 %all-to-all-start = ((s32[32,1,8]{2,1,0:T(1,128)}), s32[32,1,8]{2,1,0:T(1,128)S(1)}, u32[]{:S(2)}, u32[]{:S(2)}) async-start(s32[32,1,8]{2,1,0:T(1,128)} %bitcast), calls=%async_computation | async-start | bytes 32768 | tf_op jit(solution)/shard_map/all_to_all | solution.py:145
  26.4 12.1 %copy-start.6 = (f32[512]{0:T(512)S(1)}, f32[512]{0:T(512)}, u32[]{:S(2)}) copy-start(f32[512]{0:T(512)} %param.23) | copy-start | bytes 6148
  26.4 12.1 %copy-start.7 = (f32[512]{0:T(512)S(1)}, f32[512]{0:T(512)}, u32[]{:S(2)}) copy-start(f32[512]{0:T(512)} %param.22) | copy-start | bytes 6148
  26.4 12.1 %copy-start.8 = (f32[512]{0:T(512)S(1)}, f32[512]{0:T(512)}, u32[]{:S(2)}) copy-start(f32[512]{0:T(512)} %param.21) | copy-start | bytes 6148
  26.4 12.1 %copy-start.9 = (f32[512]{0:T(512)S(1)}, f32[512]{0:T(512)}, u32[]{:S(2)}) copy-start(f32[512]{0:T(512)} %param.19) | copy-start | bytes 6148
  26.4 12.1 %copy-start.10 = (s32[256]{0:T(256)S(1)}, s32[256]{0:T(256)}, u32[]{:S(2)}) copy-start(s32[256]{0:T(256)} %param.15) | copy-start | bytes 3076
  26.4 12.2 %copy-start.5 = (bf16[32,512]{1,0:T(8,128)(2,1)S(1)}, bf16[32,512]{1,0:T(8,128)(2,1)}, u32[]{:S(2)}) copy-start(bf16[32,512]{1,0:T(8,128)(2,1)} %param.13) | copy-start | bytes 98308
  31.1 30.5 %copy-start.1 = (bf16[512,512]{1,0:T(8,128)(2,1)S(1)}, bf16[512,512]{1,0:T(8,128)(2,1)}, u32[]{:S(2)}) copy-start(bf16[512,512]{1,0:T(8,128)(2,1)} %w_out.1) | copy-start | bytes 1572868
  31.1 30.5 %copy-start.2 = (bf16[256,512]{1,0:T(8,128)(2,1)S(1)}, bf16[256,512]{1,0:T(8,128)(2,1)}, u32[]{:S(2)}) copy-start(bf16[256,512]{1,0:T(8,128)(2,1)} %edges_hbm.1) | copy-start | bytes 786436
  31.1 30.5 %copy-start.3 = (bf16[256,512]{1,0:T(8,128)(2,1)S(1)}, bf16[256,512]{1,0:T(8,128)(2,1)}, u32[]{:S(2)}) copy-start(bf16[256,512]{1,0:T(8,128)(2,1)} %cot_hbm.1) | copy-start | bytes 786436
  31.1 30.5 %copy-start.4 = (s32[1,32]{1,0:T(1,128)S(1)}, s32[1,32]{1,0:T(1,128)}, u32[]{:S(2)}) copy-start(s32[1,32]{1,0:T(1,128)} %counts.1) | copy-start | bytes 388
  31.1 30.5 %all-to-all-start.1 = ((bf16[32,8,1024]{2,1,0:T(8,128)(2,1)}), bf16[32,8,1024]{2,1,0:T(8,128)(2,1)S(1)}, u32[]{:S(2)}, u32[]{:S(2)}) async-start(bf16[32,8,1024]{2,1,0:T(8,128)(2,1)} %bitcast.2), calls=%async_computation.1 | async-start | bytes 1048576 | tf_op jit(solution)/shard_map/all_to_all | solution.py:157
  86.7 24.3 %copy-start = (bf16[1536,512]{1,0:T(8,128)(2,1)S(1)}, bf16[1536,512]{1,0:T(8,128)(2,1)}, u32[]{:S(2)}) copy-start(bf16[1536,512]{1,0:T(8,128)(2,1)} %w_in.1) | copy-start | bytes 4718596
  86.7 35.6 %all-to-all-start.2 = ((bf16[32,8,1024]{2,1,0:T(8,128)(2,1)}), bf16[32,8,1024]{2,1,0:T(8,128)(2,1)S(1)}, u32[]{:S(2)}, u32[]{:S(2)}) async-start(bf16[32,8,1024]{2,1,0:T(8,128)(2,1)} %bitcast.8), calls=%async_computation.2 | async-start | bytes 1048576 | tf_op jit(solution)/shard_map/all_to_all | solution.py:198
  101.5 20.7 %collective-permute-start.3 = (bf16[32,512]{1,0:T(8,128)(2,1)S(1)}, bf16[32,512]{1,0:T(8,128)(2,1)S(1)}, u32[]{:S(2)}, u32[]{:S(2)}) collective-permute-start(bf16[32,512]{1,0:T(8,128)(2,1)S(1)} %get-tuple-element.20), channel_id=1, source_target_pairs={{0,1},{1,2},{2,0},{3,4},{4,5},{5,3},{6,7},{7,8},{8,6},{9,10},{10,1... | collective-permute-start | bytes 98312 | tf_op jit(solution)/shard_map/ppermute | solution.py:196
  107.8 14.4 %collective-permute-start.2 = (bf16[32,512]{1,0:T(8,128)(2,1)S(1)}, bf16[32,512]{1,0:T(8,128)(2,1)S(1)}, u32[]{:S(2)}, u32[]{:S(2)}) collective-permute-start(bf16[32,512]{1,0:T(8,128)(2,1)S(1)} %get-tuple-element.21), channel_id=1, source_target_pairs={{1,0},{2,1},{0,2},{4,3},{5,4},{3,5},{7,6},{8,7},{6,8},{10,9},{11,1... | collective-permute-start | bytes 98312 | tf_op jit(solution)/shard_map/ppermute | solution.py:195

commit v6 on v5

--- a/solution.py
+++ b/solution.py
@@ -8,6 +8,8 @@
 from jax.sharding import PartitionSpec as P
 
 Z_HI = 3
+ROOM = 48
+NOTE = 16
 
 
 def dot(a, b):
@@ -32,13 +34,53 @@
     answer[...] = dot(onehot_of(asked, own.shape[0]), own[...]).astype(jnp.bfloat16)
 
 
+def column_of(row):
+    n = row.shape[1]
+    diagonal = lax.broadcasted_iota(jnp.int32, (n, n), 0) == lax.broadcasted_iota(jnp.int32, (n, n), 1)
+    return jnp.sum(jnp.where(diagonal, row, 0), axis=1, keepdims=True)
+
+
+def plan_kernel(room, height, nodes, cots, place, counts, own, note, target):
+    width = nodes.shape[1]
+    slots = place.shape[1]
+    per_block = slots // counts.shape[1]
+    own[:, :width] = nodes[...]
+    own[:, width:] = cots[...]
+    expand = (
+        lax.broadcasted_iota(jnp.int32, (counts.shape[1], slots), 0)
+        == lax.broadcasted_iota(jnp.int32, (counts.shape[1], slots), 1) // per_block
+    )
+    block_counts = column_of(counts[...])
+    count = jnp.sum(jnp.where(expand, block_counts, 0), axis=0, keepdims=True)
+    alive = lax.broadcasted_iota(jnp.int32, (1, slots), 1) % per_block < count
+    neighbour = jnp.where(alive, place[...] // height, -1)
+    inside = place[...] % height
+    earlier = lax.broadcasted_iota(jnp.int32, (slots, slots), 0) < lax.broadcasted_iota(
+        jnp.int32, (slots, slots), 1
+    )
+    same = (column_of(neighbour) == neighbour) & earlier
+    rank = jnp.sum(jnp.where(same, 1, 0), axis=0, keepdims=True)
+    fits = rank < room
+    target[...] = jnp.where(alive & fits, neighbour * room + rank, -1)
+    over = jnp.max(jnp.where(alive & jnp.logical_not(fits), 1.0, 0.0))
+    chosen = jnp.where(
+        target[...] == lax.broadcasted_iota(jnp.int32, (width, slots), 0), 1.0, 0.0
+    ).astype(jnp.bfloat16)
+    moved = dot_t(
+        jnp.broadcast_to(inside.astype(jnp.float32), (NOTE, slots)).astype(jnp.bfloat16), chosen
+    )
+    first = lax.broadcasted_iota(jnp.int32, (NOTE, width), 0) == 0
+    note[...] = jnp.where(first, over, moved).astype(jnp.bfloat16)
+
+
 def edge_kernel(
-    table, spread, recv, counts, w_out, vectors, w_hbm, edges_hbm, cot_hbm,
-    new_edges, packed, partial,
+    table, sender, target, recv, counts, w_out, vectors, w_hbm, edges_hbm, cot_hbm,
+    new_edges, packed, compact, overflow,
     w_in, edges, edge_cot, sems,
 ):
     slots, width = edges.shape
     group = table.shape[0]
+    sender_height = group // (compact.shape[0] // ROOM)
     per_block = slots // counts.shape[1]
     edges_copy = pltpu.make_async_copy(edges_hbm, edges, sems.at[0])
     cot_copy = pltpu.make_async_copy(cot_hbm, edge_cot, sems.at[1])
@@ -52,10 +94,7 @@
         copy.start()
     b_in, b_out = vectors[0:1, :], vectors[1:2, :]
     gain, bias = vectors[2:3, :], vectors[3:4, :]
-    diagonal = lax.broadcasted_iota(jnp.int32, (slots, slots), 0) == lax.broadcasted_iota(
-        jnp.int32, (slots, slots), 1
-    )
-    pick = jnp.sum(jnp.where(diagonal, spread[...], 0), axis=1, keepdims=True)
+    pick = column_of(sender[...])
     slot = lax.broadcasted_iota(jnp.int32, (slots, counts.shape[1]), 0)
     block = lax.broadcasted_iota(jnp.int32, (slots, counts.shape[1]), 1)
     count = jnp.sum(jnp.where(slot // per_block == block, counts[...], 0), axis=1, keepdims=True)
@@ -91,9 +130,45 @@
     d_hidden = dot_t(d_outer.astype(jnp.bfloat16), w_out[...])
     d_pre = (d_hidden * sigma * (1.0 + pre * (1.0 - sigma))).astype(jnp.bfloat16)
     packed[:, width:] = d_pre
-    row = lax.broadcasted_iota(jnp.int32, (group, slots), 0)
-    placed = jnp.where(spread[...] == row, 1.0, 0.0).astype(jnp.bfloat16)
-    partial[...] = dot(placed, d_pre).astype(jnp.bfloat16)
+    row = lax.broadcasted_iota(jnp.int32, (compact.shape[0], slots), 0)
+    chosen = jnp.where(target[...] == row, 1.0, 0.0).astype(jnp.bfloat16)
+    compact[...] = dot(chosen, d_pre).astype(jnp.bfloat16)
+    flags = sum(note[:, :128].astype(jnp.float32) for note in notes_of(table, sender_height))
+    first = lax.broadcasted_iota(jnp.int32, flags.shape, 0) == 0
+    overflow[0, 0] = (jnp.max(jnp.where(first, flags, 0.0)) > 0.5).astype(jnp.int32)
+
+
+def notes_of(table, height):
+    return [table[at + height - NOTE : at + height, :] for at in range(0, table.shape[0], height)]
+
+
+def dense_kernel(packed, place, partial):
+    width = partial.shape[1]
+    row = lax.broadcasted_iota(jnp.int32, (partial.shape[0], packed.shape[0]), 0)
+    placed = jnp.where(place[...] == row, 1.0, 0.0).astype(jnp.bfloat16)
+    partial[...] = dot(placed, packed[:, width:]).astype(jnp.bfloat16)
+
+
+def place_kernel(arrived, table, mine, column_sum):
+    height, width = column_sum.shape
+    notes = notes_of(table, height + NOTE)
+    room = arrived.shape[0] // len(notes)
+    shape = (NOTE, width)
+    second = lax.broadcasted_iota(jnp.int32, shape, 0) == 1
+    source = lax.broadcasted_iota(jnp.int32, shape, 0)
+    index = jnp.zeros(shape, jnp.float32)
+    for at, note in enumerate(notes):
+        line = jnp.sum(jnp.where(second, note.astype(jnp.float32), 0.0), axis=0, keepdims=True)
+        index = jnp.where(source == at, line, index)
+    lane = lax.broadcasted_iota(jnp.int32, (width, 128), 0) - mine[0, 0] * room
+    own_part = jnp.where(lane == lax.broadcasted_iota(jnp.int32, (width, 128), 1), 1.0, 0.0)
+    index = dot(index.astype(jnp.bfloat16), own_part.astype(jnp.bfloat16))
+    row = lax.broadcasted_iota(jnp.int32, (height, room), 0).astype(jnp.float32)
+    total = jnp.zeros(column_sum.shape, jnp.float32)
+    for at in range(len(notes)):
+        placed = jnp.where(index[at : at + 1, :room] == row, 1.0, 0.0).astype(jnp.bfloat16)
+        total += dot(placed, arrived[at * room : (at + 1) * room, :])
+    column_sum[...] = total
 
 
 def owner_kernel(asked, returned, column_sum, to_below, to_above, w_in, aggregated, grad_nodes):
@@ -139,7 +214,26 @@
     down = [(b, a) for a, b in up]
     my_h = lax.axis_index("col") % Z_HI
 
-    own = jnp.concatenate([node_latents, agg_cotangent], axis=1)
+    height = Z_HI * owned
+    device = edge_sender // owned
+    turn = (my_h - device % Z_HI + Z_HI) % Z_HI
+    place = (device // Z_HI) * height + turn * owned + edge_sender % owned
+    sender = (place + (device // Z_HI) * NOTE).reshape(1, slots)
+    place = place.reshape(1, slots)
+    own, note, target = pl.pallas_call(
+        functools.partial(plan_kernel, ROOM, height),
+        in_specs=[VMEM] * 4,
+        out_specs=[VMEM] * 3,
+        out_shape=[
+            jax.ShapeDtypeStruct((owned, 2 * width), jnp.bfloat16),
+            jax.ShapeDtypeStruct((NOTE, width), jnp.bfloat16),
+            jax.ShapeDtypeStruct((1, slots), jnp.int32),
+        ],
+        cost_estimate=pl.CostEstimate(
+            flops=2 * NOTE * slots * width, bytes_accessed=256 * 1024, transcendentals=0
+        ),
+        compiler_params=pltpu.CompilerParams(vmem_limit_bytes=16 * 1024 * 1024),
+    )(node_latents, agg_cotangent, place, edge_count)
     from_below = lax.ppermute(node_latents, "col", up)
     from_above = lax.ppermute(node_latents, "col", down)
     asked = lax.all_to_all(edge_receiver.reshape(rows, 1, per_block), "row", 0, 0, tiled=True)
@@ -155,22 +249,20 @@
     )(asked, own)
     answer, from_below, from_above = lax.optimization_barrier((answer, from_below, from_above))
     recv = lax.all_to_all(answer, "row", 0, 0, tiled=True)
-    column = jnp.concatenate([node_latents, from_below, from_above], axis=0)
+    column = jnp.concatenate([node_latents, from_below, from_above, note], axis=0)
     table = lax.all_gather(column, "col", axis=0, tiled=True, axis_index_groups=along_y)
 
-    device = edge_sender // owned
-    turn = (my_h - device % Z_HI + Z_HI) % Z_HI
-    place = ((device // Z_HI) * Z_HI + turn) * owned + edge_sender % owned
     vectors = jnp.stack([b_in, b_out, ln_gain, ln_bias])
 
-    new_edges, packed, partial = pl.pallas_call(
+    new_edges, packed, compact, overflow = pl.pallas_call(
         edge_kernel,
-        in_specs=[VMEM] * 6 + [ANY] * 3,
-        out_specs=[VMEM] * 3,
+        in_specs=[VMEM] * 7 + [ANY] * 3,
+        out_specs=[VMEM] * 3 + [pl.BlockSpec(memory_space=pltpu.SMEM)],
         out_shape=[
             jax.ShapeDtypeStruct((slots, width), jnp.bfloat16),
             jax.ShapeDtypeStruct((slots, 2 * width), jnp.bfloat16),
-            jax.ShapeDtypeStruct((cols * owned, width), jnp.bfloat16),
+            jax.ShapeDtypeStruct((tall * ROOM, width), jnp.bfloat16),
+            jax.ShapeDtypeStruct((1, 1), jnp.int32),
         ],
         scratch_shapes=[
             pltpu.VMEM((3 * width, width), jnp.bfloat16),
@@ -185,12 +277,33 @@
             transcendentals=slots * width,
         ),
     )(
-        table, place.reshape(1, slots), recv, edge_count, w_out, vectors,
+        table, sender, target, recv, edge_count, w_out, vectors,
         w_in, edge_latents, edge_cotangent,
     )
 
-    parts = lax.all_to_all(partial, "col", 0, 0, tiled=True, axis_index_groups=along_y)
-    column_sum = jnp.sum(parts.reshape(tall, Z_HI * owned, width).astype(jnp.float32), axis=0)
+    def short_way():
+        arrived = lax.all_to_all(compact, "col", 0, 0, tiled=True, axis_index_groups=along_y)
+        mine = (lax.axis_index("col") // Z_HI).astype(jnp.int32).reshape(1, 1)
+        return pl.pallas_call(
+            place_kernel,
+            in_specs=[VMEM] * 2 + [pl.BlockSpec(memory_space=pltpu.SMEM)],
+            out_specs=VMEM,
+            out_shape=jax.ShapeDtypeStruct((height, width), jnp.float32),
+            compiler_params=pltpu.CompilerParams(vmem_limit_bytes=16 * 1024 * 1024),
+        )(arrived, table, mine)
+
+    def long_way():
+        partial = pl.pallas_call(
+            dense_kernel,
+            in_specs=[VMEM] * 2,
+            out_specs=VMEM,
+            out_shape=jax.ShapeDtypeStruct((tall * height, width), jnp.bfloat16),
+            compiler_params=pltpu.CompilerParams(vmem_limit_bytes=16 * 1024 * 1024),
+        )(packed, place)
+        parts = lax.all_to_all(partial, "col", 0, 0, tiled=True, axis_index_groups=along_y)
+        return jnp.sum(parts.reshape(tall, height, width).astype(jnp.float32), axis=0)
+
+    column_sum = lax.cond(overflow[0, 0] > 0, long_way, short_way)
     away = column_sum.astype(jnp.bfloat16)
     to_below = lax.ppermute(away[owned : 2 * owned], "col", down)
     to_above = lax.ppermute(away[2 * owned :], "col", up)

time: 124 us -> 124 us (level)
  blocking collectives: 44.3 us -> 25.2 us
  waiting for transfers between devices: 12.7 us -> 22.1 us
  starting transfers between devices: 55 us -> 59.7 us
  Pallas kernels: 6.18 us -> 9.21 us
  local copies, waits for them, and re-layouts: 1.43 us -> 3.59 us
    all_to_all x1 -> x0, blocking collectives: 21.3 us -> none  [on_device(): lax.all_to_all(partial, 'col', 0, 0, tiled=True, axis_index_groups=along_y)]
    all_to_all x0 -> x1, waiting for transfers between devices: none -> 10.8 us  [short_way(): lax.all_to_all(compact, 'col', 0, 0, tiled=True, axis_index_groups=along_y)]
    all_to_all x0 -> x1, starting transfers between devices: none -> 5.09 us  [short_way(): lax.all_to_all(compact, 'col', 0, 0, tiled=True, axis_index_groups=along_y)]
    pallas_call x1 -> x3, Pallas kernels: 3.68 us -> 6.7 us  [the longest x1 4.56 us: on_device(): pl.pallas_call(edge_kernel, in_specs=[VMEM] * 7 + [ANY] * 3, out_specs=[V...]
    all_to_all x1, waiting for transfers between devices: 3.49 us -> 0.96 us  [on_device(): lax.all_to_all(edge_receiver.reshape(rows, 1, per_block), 'row', 0, 0, ti...]
    all_gather x1, blocking collectives: 23 us -> 25.2 us  [on_device(): lax.all_gather(column, 'col', axis=0, tiled=True, axis_index_groups=along_y)]
    unnamed x22 -> x28, local copies, waits for them, and re-layouts: 0.05 us -> 2.21 us
  transfers between devices with their start and end apart: 7 -> 8, of which waited for: 2 -> 3; matrix products, arithmetic and copies ran while one was open for 4% -> 3% of each run, Pallas kernels for 1% -> 1%
where the time goes in v6:
time: 124 us; the launch traced here: 123 us
  starting transfers between devices  59.7 us (48%)
  blocking collectives  25.2 us (20%)
  waiting for transfers between devices  22.1 us (18%)
  Pallas kernels  9.21 us (7%)
  local copies, waits for them, and re-layouts  3.59 us (3%)
  between operations  1.55 us (1%)
    all_gather x1, blocking collectives, on_device(): lax.all_gather(column, 'col', axis=0, tiled=True, axis_index_groups=along_y)  25.2 us
    all_to_all x1, starting transfers between devices, on_device(): returned = lax.all_to_all(packed, 'row', 0, 0, tiled=True)  14.2 us
    all_to_all x1, waiting for transfers between devices, short_way(): lax.all_to_all(compact, 'col', 0, 0, tiled=True, axis_index_groups=along_y)  10.8 us
    ppermute x1, starting transfers between devices, on_device(): from_below = lax.ppermute(node_latents, 'col', up)  10.6 us
    ppermute x1, waiting for transfers between devices, on_device(): to_above = lax.ppermute(away[2 * owned:], 'col', up)  10.3 us
    all_to_all x1, starting transfers between devices, on_device(): lax.all_to_all(edge_receiver.reshape(rows, 1, per_block), 'row', 0, 0, ti...  8.28 us
    all_to_all x1, starting transfers between devices, on_device(): recv = lax.all_to_all(answer, 'row', 0, 0, tiled=True)  7.3 us
    ppermute x1, starting transfers between devices, on_device(): to_above = lax.ppermute(away[2 * owned:], 'col', up)  6.32 us
  transfers between devices with their start and end apart: 8, of which 3 were waited for; matrix products, arithmetic and copies ran while one was open for 3% of the time, Pallas kernels for 1%

profile of v6, /device:TPU:69, one launch (start us, length us, event | category | flops | bytes accessed | tf_op | source)
XLA Modules:
  0.0 123.2 jit_solution(4985589433978193130)
XLA Ops:
  0.6 10.6 %collective-permute-start = (bf16[32,512]{1,0:T(8,128)(2,1)}, bf16[32,512]{1,0:T(8,128)(2,1)S(1)}, u32[]{:S(2)}, u32[]{:S(2)}) collective-permute-start(bf16[32,512]{1,0:T(8,128)(2,1)} %nodes.1), channel_id=1, source_target_pairs={{0,1},{1,2},{2,0},{3,4},{4,5},{5,3},{6,7},{7,8},{8,6},{9,10},{10,1... | collective-permute-start | bytes 98312 | tf_op jit(solution)/shard_map/ppermute | solution.py:237
  11.3 4.7 %collective-permute-start.1 = (bf16[32,512]{1,0:T(8,128)(2,1)}, bf16[32,512]{1,0:T(8,128)(2,1)S(1)}, u32[]{:S(2)}, u32[]{:S(2)}) collective-permute-start(bf16[32,512]{1,0:T(8,128)(2,1)} %nodes.1), channel_id=1, source_target_pairs={{1,0},{2,1},{0,2},{4,3},{5,4},{3,5},{7,6},{8,7},{6,8},{10,9},{11,1... | collective-permute-start | bytes 98312 | tf_op jit(solution)/shard_map/ppermute | solution.py:238
  15.9 1.4 %reshape.34 = s32[32,1,8]{2,0,1:T(8,128)} reshape(s32[256]{0:T(256)} %param.18) | data formatting | bytes 2048 | tf_op jit(solution)/shard_map/reshape | solution.py:239
  17.3 8.3 %all-to-all-start.2 = ((s32[32,1,8]{2,1,0:T(1,128)}), s32[32,1,8]{2,1,0:T(1,128)S(1)}, u32[]{:S(2)}, u32[]{:S(2)}) async-start(s32[32,1,8]{2,1,0:T(1,128)} %bitcast.4), calls=%async_computation.2 | async-start | bytes 32768 | tf_op jit(solution)/shard_map/all_to_all | solution.py:239
  25.6 0.7 multiply_add_fusion
  26.3 0.0 copy-start.4
  26.4 0.8 copy-done.4
  27.1 0.0 copy-start.6
  27.1 0.8 copy-done.6
  27.9 0.0 copy-start.7
  27.9 0.7 copy-done.7
  28.5 0.5 shard_map.156
  29.0 1.0 all-to-all-done.2.asked
  29.9 0.0 copy-start.10
  29.9 0.0 copy-start.5
  30.0 0.0 copy-start.2
  30.0 0.0 copy-start.3
  30.0 1.2 shard_map.157
  31.2 0.0 collective-permute-done
  31.2 0.0 collective-permute-done.1
  31.2 7.3 %all-to-all-start.3 = ((bf16[32,8,1024]{2,1,0:T(8,128)(2,1)}), bf16[32,8,1024]{2,1,0:T(8,128)(2,1)S(1)}, u32[]{:S(2)}, u32[]{:S(2)}) async-start(bf16[32,8,1024]{2,1,0:T(8,128)(2,1)} %bitcast.7), calls=%async_computation.3 | async-start | bytes 1048576 | tf_op jit(solution)/shard_map/all_to_all | solution.py:251
  38.5 0.0 copy-done.10
  38.5 0.0 copy-done.11
  38.5 0.0 copy-done.12
  38.5 0.0 copy-done.13
  38.6 0.0 copy-done.5
  38.6 25.2 %all_gather.3.table = bf16[896,512]{1,0:T(8,128)(2,1)} all-gather(bf16[112,512]{1,0:T(8,128)(2,1)S(1)} %pad_maximum_fusion), channel_id=1, replica_groups={{0,3,6,9,12,15,18,21},{1,4,7,10,13,16,19,22},{2,5,8,11,14,17,20,23},{24..., dimensions={0}, use_global_device_ids=true | all-gather | bytes 1032192 | tf_op jit(solution)/shard_map/all_gather | solution.py:253
  63.8 0.0 all-to-all-done.3
  63.8 0.0 copy-done.2
  63.8 0.0 copy-done.3
  63.8 0.0 copy-done
  63.8 0.0 copy-done.1
  63.9 0.0 copy-done.8
  63.9 4.6 %shard_map.158 = (bf16[256,512]{1,0:T(8,128)(2,1)}, bf16[256,1024]{1,0:T(8,128)(2,1)}, bf16[384,512]{1,0:T(8,128)(2,1)}, s32[1,1]{1,0:T(1,128)}) custom-call(bf16[896,512]{1,0:T(8,128)(2,1)} %all_gather.3.table, s32[1,256]{1,0:T(1,128)S(1)} %bitcast.20, s32[1,256]{1,0:T(1,128)S(1)} %get-tuple-element.35.target, bf16[256,1024]{1,0:T(8,128)(2,1)S(1)} %bitcast.18, ...), custom_call_target="tpu_custom_call" | custom-call | flops 1073741824 | bytes 6291456 | tf_op jit(solution)/shard_map/pallas_call | solution.py:257
  69.1 0.0 copy-start.9
  69.1 17.6 %conditional.1 = (f32[96,512]{1,0:T(8,128)S(1)}) conditional(s32[]{:T(128)} %bitcast.15, (bf16[384,512]{1,0:T(8,128)(2,1)}, bf16[896,512]{1,0:T(8,128)(2,1)}) %tuple.16, (bf16[256,1024]{1,0:T(8,128)(2,1)}, s32[1,256]{1,0:T(1,128)S(1)}) %tuple.23), branch_computations={%region_0.1_spmd, %region_1.3_spmd} | conditional | flops 737280 | bytes 2555912 | solution.py:306
  69.1 5.1 %all-to-all-start = ((bf16[8,48,512]{2,1,0:T(8,128)(2,1)}), bf16[8,48,512]{2,1,0:T(8,128)(2,1)S(1)}, u32[]{:S(2)}, u32[]{:S(2)}) async-start(bf16[8,48,512]{2,1,0:T(8,128)(2,1)} %bitcast.22), calls=%async_computation | async-start | bytes 786432 | tf_op jit(solution)/shard_map/cond/branch_0_fun/all_to_all | solution.py:285
  74.2 10.8 %all-to-all-done = bf16[8,48,512]{2,1,0:T(8,128)(2,1)S(1)} async-done(((bf16[8,48,512]{2,1,0:T(8,128)(2,1)}), bf16[8,48,512]{2,1,0:T(8,128)(2,1)S(1)}, u32[]{:S(2)}, u32[]{:S(2)}) %all-to-all-start) | async-done | bytes 393248 | tf_op jit(solution)/shard_map/cond/branch_0_fun/all_to_all | solution.py:285
  85.0 1.7 %branch_0_fun.1 = f32[96,512]{1,0:T(8,128)S(1)} custom-call(bf16[384,512]{1,0:T(8,128)(2,1)S(1)} %bitcast.19, bf16[896,512]{1,0:T(8,128)(2,1)} %get-tuple-element.12.table, s32[1,1]{1,0:T(1,128)} %bitcast.2.mine), custom_call_target="tpu_custom_call" | custom-call | tf_op jit(solution)/shard_map/cond/branch_0_fun/pallas_call | solution.py:287
  86.7 14.2 %all-to-all-start.4 = ((bf16[32,8,1024]{2,1,0:T(8,128)(2,1)}), bf16[32,8,1024]{2,1,0:T(8,128)(2,1)S(1)}, u32[]{:S(2)}, u32[]{:S(2)}) async-start(bf16[32,8,1024]{2,1,0:T(8,128)(2,1)} %bitcast.21), calls=%async_computation.4 | async-start | bytes 1048576 | tf_op jit(solution)/shard_map/all_to_all | solution.py:311
  101.0 6.3 %collective-permute-start.3 = (bf16[32,512]{1,0:T(8,128)(2,1)S(1)}, bf16[32,512]{1,0:T(8,128)(2,1)S(1)}, u32[]{:S(2)}, u32[]{:S(2)}) collective-permute-start(bf16[32,512]{1,0:T(8,128)(2,1)S(1)} %get-tuple-element.45), channel_id=1, source_target_pairs={{0,1},{1,2},{2,0},{3,4},{4,5},{5,3},{6,7},{7,8},{8,6},{9,10},{10,1... | collective-permute-start | bytes 98312 | tf_op jit(solution)/shard_map/ppermute | solution.py:309
  107.4 3.2 %collective-permute-start.2 = (bf16[32,512]{1,0:T(8,128)(2,1)S(1)}, bf16[32,512]{1,0:T(8,128)(2,1)S(1)}, u32[]{:S(2)}, u32[]{:S(2)}) collective-permute-start(bf16[32,512]{1,0:T(8,128)(2,1)S(1)} %get-tuple-element.46), channel_id=1, source_target_pairs={{1,0},{2,1},{0,2},{4,3},{5,4},{3,5},{7,6},{8,7},{6,8},{10,9},{11,1... | collective-permute-start | bytes 98312 | tf_op jit(solution)/shard_map/ppermute | solution.py:308
  110.5 0.0 copy-done.9
  110.5 1.0 fusion
  111.6 10.3 %collective-permute-done.3.to_above = bf16[32,512]{1,0:T(8,128)(2,1)S(1)} collective-permute-done((bf16[32,512]{1,0:T(8,128)(2,1)S(1)}, bf16[32,512]{1,0:T(8,128)(2,1)S(1)}, u32[]{:S(2)}, u32[]{:S(2)}) %collective-permute-start.3) | collective-permute-done | bytes 32800 | tf_op jit(solution)/shard_map/ppermute | solution.py:309
  121.8 0.0 collective-permute-done.2.to_below
  121.8 0.0 all-to-all-done.4
  121.8 1.3 %shard_map.159 = (bf16[32,512]{1,0:T(8,128)(2,1)}, bf16[32,512]{1,0:T(8,128)(2,1)}) custom-call(s32[32,1,8]{2,1,0:T(1,128)S(1)} %all-to-all-done.2.asked, bf16[256,1024]{1,0:T(8,128)(2,1)S(1)} %bitcast.17, f32[96,512]{1,0:T(8,128)S(1)} %get-tuple-element.47.column_sum, bf16[32,512]{1,0:T(8,128)(2,1)S(1)} %collective-permute-done.2.to_below, ...), custom_call_target="tpu_custom_call" | custom-call | flops 50331648 | bytes 2097152 | tf_op jit(solution)/shard_map/pallas_call | solution.py:312
  (10 shorter events, 0.1 us)
Async XLA Ops:
  0.6 30.5 %collective-permute-start = (bf16[32,512]{1,0:T(8,128)(2,1)}, bf16[32,512]{1,0:T(8,128)(2,1)S(1)}, u32[]{:S(2)}, u32[]{:S(2)}) collective-permute-start(bf16[32,512]{1,0:T(8,128)(2,1)} %nodes.1), channel_id=1, source_target_pairs={{0,1},{1,2},{2,0},{3,4},{4,5},{5,3},{6,7},{7,8},{8,6},{9,10},{10,1... | collective-permute-start | bytes 98312 | tf_op jit(solution)/shard_map/ppermute | solution.py:237
  11.3 19.9 %collective-permute-start.1 = (bf16[32,512]{1,0:T(8,128)(2,1)}, bf16[32,512]{1,0:T(8,128)(2,1)S(1)}, u32[]{:S(2)}, u32[]{:S(2)}) collective-permute-start(bf16[32,512]{1,0:T(8,128)(2,1)} %nodes.1), channel_id=1, source_target_pairs={{1,0},{2,1},{0,2},{4,3},{5,4},{3,5},{7,6},{8,7},{6,8},{10,9},{11,1... | collective-permute-start | bytes 98312 | tf_op jit(solution)/shard_map/ppermute | solution.py:238
  17.3 12.6 %all-to-all-start.2 = ((s32[32,1,8]{2,1,0:T(1,128)}), s32[32,1,8]{2,1,0:T(1,128)S(1)}, u32[]{:S(2)}, u32[]{:S(2)}) async-start(s32[32,1,8]{2,1,0:T(1,128)} %bitcast.4), calls=%async_computation.2 | async-start | bytes 32768 | tf_op jit(solution)/shard_map/all_to_all | solution.py:239
  26.3 0.8 copy-start.4
  27.1 0.8 copy-start.6
  27.9 0.7 copy-start.7
  29.9 8.6 %copy-start.10 = (f32[512]{0:T(512)S(1)}, f32[512]{0:T(512)}, u32[]{:S(2)}) copy-start(f32[512]{0:T(512)} %param.25) | copy-start | bytes 6148
  29.9 8.6 %copy-start.11 = (f32[512]{0:T(512)S(1)}, f32[512]{0:T(512)}, u32[]{:S(2)}) copy-start(f32[512]{0:T(512)} %param.24) | copy-start | bytes 6148
  29.9 8.6 %copy-start.12 = (f32[512]{0:T(512)S(1)}, f32[512]{0:T(512)}, u32[]{:S(2)}) copy-start(f32[512]{0:T(512)} %param.23) | copy-start | bytes 6148
  29.9 8.6 %copy-start.13 = (f32[512]{0:T(512)S(1)}, f32[512]{0:T(512)}, u32[]{:S(2)}) copy-start(f32[512]{0:T(512)} %param.21) | copy-start | bytes 6148
  29.9 8.6 %copy-start.5 = (bf16[32,512]{1,0:T(8,128)(2,1)S(1)}, bf16[32,512]{1,0:T(8,128)(2,1)}, u32[]{:S(2)}) copy-start(bf16[32,512]{1,0:T(8,128)(2,1)} %nodes.1) | copy-start | bytes 98308
  30.0 33.9 %copy-start.2 = (bf16[256,512]{1,0:T(8,128)(2,1)S(1)}, bf16[256,512]{1,0:T(8,128)(2,1)}, u32[]{:S(2)}) copy-start(bf16[256,512]{1,0:T(8,128)(2,1)} %edges_hbm.1) | copy-start | bytes 786436
  30.0 33.9 %copy-start.3 = (bf16[256,512]{1,0:T(8,128)(2,1)S(1)}, bf16[256,512]{1,0:T(8,128)(2,1)}, u32[]{:S(2)}) copy-start(bf16[256,512]{1,0:T(8,128)(2,1)} %cot_hbm.1) | copy-start | bytes 786436
  31.2 32.7 %copy-start = (bf16[1536,512]{1,0:T(8,128)(2,1)S(1)}, bf16[1536,512]{1,0:T(8,128)(2,1)}, u32[]{:S(2)}) copy-start(bf16[1536,512]{1,0:T(8,128)(2,1)} %w_in.1) | copy-start | bytes 4718596
  31.2 32.7 %copy-start.1 = (bf16[512,512]{1,0:T(8,128)(2,1)S(1)}, bf16[512,512]{1,0:T(8,128)(2,1)}, u32[]{:S(2)}) copy-start(bf16[512,512]{1,0:T(8,128)(2,1)} %w_out.1) | copy-start | bytes 1572868
  31.2 32.7 %copy-start.8 = (s32[1,32]{1,0:T(1,128)S(1)}, s32[1,32]{1,0:T(1,128)}, u32[]{:S(2)}) copy-start(s32[1,32]{1,0:T(1,128)} %counts.3) | copy-start | bytes 388
  31.2 32.6 %all-to-all-start.3 = ((bf16[32,8,1024]{2,1,0:T(8,128)(2,1)}), bf16[32,8,1024]{2,1,0:T(8,128)(2,1)S(1)}, u32[]{:S(2)}, u32[]{:S(2)}) async-start(bf16[32,8,1024]{2,1,0:T(8,128)(2,1)} %bitcast.7), calls=%async_computation.3 | async-start | bytes 1048576 | tf_op jit(solution)/shard_map/all_to_all | solution.py:251
  69.1 41.4 %copy-start.9 = (bf16[256,1024]{1,0:T(8,128)(2,1)S(1)}, bf16[256,1024]{1,0:T(8,128)(2,1)}, u32[]{:S(2)}) copy-start(bf16[256,1024]{1,0:T(8,128)(2,1)} %get-tuple-element.38) | copy-start | bytes 1572868
  69.1 15.9 %all-to-all-start = ((bf16[8,48,512]{2,1,0:T(8,128)(2,1)}), bf16[8,48,512]{2,1,0:T(8,128)(2,1)S(1)}, u32[]{:S(2)}, u32[]{:S(2)}) async-start(bf16[8,48,512]{2,1,0:T(8,128)(2,1)} %bitcast.22), calls=%async_computation | async-start | bytes 786432 | tf_op jit(solution)/shard_map/cond/branch_0_fun/all_to_all | solution.py:285
  86.7 35.1 %all-to-all-start.4 = ((bf16[32,8,1024]{2,1,0:T(8,128)(2,1)}), bf16[32,8,1024]{2,1,0:T(8,128)(2,1)S(1)}, u32[]{:S(2)}, u32[]{:S(2)}) async-start(bf16[32,8,1024]{2,1,0:T(8,128)(2,1)} %bitcast.21), calls=%async_computation.4 | async-start | bytes 1048576 | tf_op jit(solution)/shard_map/all_to_all | solution.py:311
  101.0 20.8 %collective-permute-start.3 = (bf16[32,512]{1,0:T(8,128)(2,1)S(1)}, bf16[32,512]{1,0:T(8,128)(2,1)S(1)}, u32[]{:S(2)}, u32[]{:S(2)}) collective-permute-start(bf16[32,512]{1,0:T(8,128)(2,1)S(1)} %get-tuple-element.45), channel_id=1, source_target_pairs={{0,1},{1,2},{2,0},{3,4},{4,5},{5,3},{6,7},{7,8},{8,6},{9,10},{10,1... | collective-permute-start | bytes 98312 | tf_op jit(solution)/shard_map/ppermute | solution.py:309
  107.4 14.5 %collective-permute-start.2 = (bf16[32,512]{1,0:T(8,128)(2,1)S(1)}, bf16[32,512]{1,0:T(8,128)(2,1)S(1)}, u32[]{:S(2)}, u32[]{:S(2)}) collective-permute-start(bf16[32,512]{1,0:T(8,128)(2,1)S(1)} %get-tuple-element.46), channel_id=1, source_target_pairs={{1,0},{2,1},{0,2},{4,3},{5,4},{3,5},{7,6},{8,7},{6,8},{10,9},{11,1... | collective-permute-start | bytes 98312 | tf_op jit(solution)/shard_map/ppermute | solution.py:308

commit v7 on v6

--- a/solution.py
+++ b/solution.py
@@ -9,7 +9,6 @@
 
 Z_HI = 3
 ROOM = 48
-NOTE = 16
 
 
 def dot(a, b):
@@ -20,18 +19,20 @@
     return lax.dot_general(a, b, (((1,), (1,)), ((), ())), preferred_element_type=jnp.float32)
 
 
-def onehot_of(asked, owned):
-    rows, _, per_block = asked.shape
-    spread = jnp.broadcast_to(asked[...], (rows, per_block, per_block)).reshape(rows * per_block, per_block)
-    slot = lax.broadcasted_iota(jnp.int32, spread.shape, 0) % per_block
-    lane = lax.broadcasted_iota(jnp.int32, spread.shape, 1)
-    index = jnp.sum(jnp.where(slot == lane, spread, 0), axis=1, keepdims=True)
+def onehot_of(asked, my_row, owned):
+    rows, _, slots = asked.shape
+    per_block = slots // rows
+    shape = (rows * per_block, slots)
+    spread = jnp.broadcast_to(asked[...], (rows, per_block, slots)).reshape(shape)
+    wanted = my_row[0, 0] * per_block + lax.broadcasted_iota(jnp.int32, shape, 0) % per_block
+    lane = lax.broadcasted_iota(jnp.int32, shape, 1)
+    index = jnp.sum(jnp.where(wanted == lane, spread, 0), axis=1, keepdims=True)
     node = lax.broadcasted_iota(jnp.int32, (rows * per_block, owned), 1)
     return jnp.where(index % owned == node, 1.0, 0.0).astype(jnp.bfloat16)
 
 
-def answer_kernel(asked, own, answer):
-    answer[...] = dot(onehot_of(asked, own.shape[0]), own[...]).astype(jnp.bfloat16)
+def answer_kernel(asked, my_row, own, answer):
+    answer[...] = dot(onehot_of(asked, my_row, own.shape[0]), own[...]).astype(jnp.bfloat16)
 
 
 def column_of(row):
@@ -40,7 +41,7 @@
     return jnp.sum(jnp.where(diagonal, row, 0), axis=1, keepdims=True)
 
 
-def plan_kernel(room, height, nodes, cots, place, counts, own, note, target):
+def plan_kernel(height, nodes, cots, place, counts, own, note, target, rest):
     width = nodes.shape[1]
     slots = place.shape[1]
     per_block = slots // counts.shape[1]
@@ -60,27 +61,30 @@
     )
     same = (column_of(neighbour) == neighbour) & earlier
     rank = jnp.sum(jnp.where(same, 1, 0), axis=0, keepdims=True)
-    fits = rank < room
-    target[...] = jnp.where(alive & fits, neighbour * room + rank, -1)
-    over = jnp.max(jnp.where(alive & jnp.logical_not(fits), 1.0, 0.0))
-    chosen = jnp.where(
-        target[...] == lax.broadcasted_iota(jnp.int32, (width, slots), 0), 1.0, 0.0
-    ).astype(jnp.bfloat16)
-    moved = dot_t(
-        jnp.broadcast_to(inside.astype(jnp.float32), (NOTE, slots)).astype(jnp.bfloat16), chosen
-    )
-    first = lax.broadcasted_iota(jnp.int32, (NOTE, width), 0) == 0
-    note[...] = jnp.where(first, over, moved).astype(jnp.bfloat16)
+    fits = alive & (rank < ROOM - 1)
+    left = alive & (rank >= ROOM - 1)
+    target[...] = jnp.where(fits, neighbour * ROOM + rank, -1)
+    rest[...] = jnp.where(left, place[...], -1)
+    over = jnp.max(jnp.where(left, 1.0, 0.0))
+    shape = note.shape
+    row = lax.broadcasted_iota(jnp.int32, (shape[0], slots), 0)
+    told = (row % ROOM == ROOM - 1) & (row // ROOM == neighbour) & fits
+    values = jnp.where(told, inside, 0).astype(jnp.float32).astype(jnp.bfloat16)
+    at = lax.broadcasted_iota(jnp.int32, (width, slots), 0) == rank
+    lines = dot_t(values, jnp.where(at, 1.0, 0.0).astype(jnp.bfloat16))
+    flag = (lax.broadcasted_iota(jnp.int32, shape, 0) % ROOM == ROOM - 1) & (
+        lax.broadcasted_iota(jnp.int32, shape, 1) == width - 1
+    )
+    note[...] = jnp.where(flag, over, lines).astype(jnp.bfloat16)
 
 
 def edge_kernel(
-    table, sender, target, recv, counts, w_out, vectors, w_hbm, edges_hbm, cot_hbm,
-    new_edges, packed, compact, overflow,
+    table, sender, target, note, recv, counts, w_out, vectors, w_hbm, edges_hbm, cot_hbm,
+    new_edges, packed, compact,
     w_in, edges, edge_cot, sems,
 ):
     slots, width = edges.shape
     group = table.shape[0]
-    sender_height = group // (compact.shape[0] // ROOM)
     per_block = slots // counts.shape[1]
     edges_copy = pltpu.make_async_copy(edges_hbm, edges, sems.at[0])
     cot_copy = pltpu.make_async_copy(cot_hbm, edge_cot, sems.at[1])
@@ -132,14 +136,7 @@
     packed[:, width:] = d_pre
     row = lax.broadcasted_iota(jnp.int32, (compact.shape[0], slots), 0)
     chosen = jnp.where(target[...] == row, 1.0, 0.0).astype(jnp.bfloat16)
-    compact[...] = dot(chosen, d_pre).astype(jnp.bfloat16)
-    flags = sum(note[:, :128].astype(jnp.float32) for note in notes_of(table, sender_height))
-    first = lax.broadcasted_iota(jnp.int32, flags.shape, 0) == 0
-    overflow[0, 0] = (jnp.max(jnp.where(first, flags, 0.0)) > 0.5).astype(jnp.int32)
-
-
-def notes_of(table, height):
-    return [table[at + height - NOTE : at + height, :] for at in range(0, table.shape[0], height)]
+    compact[...] = (dot(chosen, d_pre) + note[...].astype(jnp.float32)).astype(jnp.bfloat16)
 
 
 def dense_kernel(packed, place, partial):
@@ -149,31 +146,27 @@
     partial[...] = dot(placed, packed[:, width:]).astype(jnp.bfloat16)
 
 
-def place_kernel(arrived, table, mine, column_sum):
+def place_kernel(arrived, column_sum, overflow):
     height, width = column_sum.shape
-    notes = notes_of(table, height + NOTE)
-    room = arrived.shape[0] // len(notes)
-    shape = (NOTE, width)
-    second = lax.broadcasted_iota(jnp.int32, shape, 0) == 1
-    source = lax.broadcasted_iota(jnp.int32, shape, 0)
-    index = jnp.zeros(shape, jnp.float32)
-    for at, note in enumerate(notes):
-        line = jnp.sum(jnp.where(second, note.astype(jnp.float32), 0.0), axis=0, keepdims=True)
-        index = jnp.where(source == at, line, index)
-    lane = lax.broadcasted_iota(jnp.int32, (width, 128), 0) - mine[0, 0] * room
-    own_part = jnp.where(lane == lax.broadcasted_iota(jnp.int32, (width, 128), 1), 1.0, 0.0)
-    index = dot(index.astype(jnp.bfloat16), own_part.astype(jnp.bfloat16))
-    row = lax.broadcasted_iota(jnp.int32, (height, room), 0).astype(jnp.float32)
+    row = lax.broadcasted_iota(jnp.int32, (height, ROOM), 0).astype(jnp.float32)
+    data = lax.broadcasted_iota(jnp.int32, (height, ROOM), 1) < ROOM - 1
+    last = lax.broadcasted_iota(jnp.int32, (16, width), 0) == 15
     total = jnp.zeros(column_sum.shape, jnp.float32)
-    for at in range(len(notes)):
-        placed = jnp.where(index[at : at + 1, :room] == row, 1.0, 0.0).astype(jnp.bfloat16)
-        total += dot(placed, arrived[at * room : (at + 1) * room, :])
+    over = jnp.zeros((1, 128), jnp.float32)
+    for at in range(0, arrived.shape[0], ROOM):
+        note = arrived[at + ROOM - 16 : at + ROOM, :].astype(jnp.float32)
+        line = jnp.sum(jnp.where(last, note, 0.0), axis=0, keepdims=True)
+        placed = jnp.where((line[:, :ROOM] == row) & data, 1.0, 0.0).astype(jnp.bfloat16)
+        total += dot(placed, arrived[at : at + ROOM, :])
+        over = jnp.maximum(over, line[:, width - 128 :])
     column_sum[...] = total
-
-
-def owner_kernel(asked, returned, column_sum, to_below, to_above, w_in, aggregated, grad_nodes):
+    end = lax.broadcasted_iota(jnp.int32, over.shape, 1) == 127
+    overflow[0, 0] = (jnp.max(jnp.where(end, over, 0.0)) > 0.5).astype(jnp.int32)
+
+
+def owner_kernel(asked, my_row, returned, column_sum, to_below, to_above, w_in, aggregated, grad_nodes):
     owned, width = aggregated.shape
-    onehot = onehot_of(asked, owned)
+    onehot = onehot_of(asked, my_row, owned)
     summed = lax.dot_general(
         onehot, returned[...], (((0,), (0,)), ((), ())), preferred_element_type=jnp.float32
     )
@@ -186,6 +179,7 @@
 
 VMEM = pl.BlockSpec(memory_space=pltpu.VMEM)
 ANY = pl.BlockSpec(memory_space=pl.ANY)
+SMEM = pl.BlockSpec(memory_space=pltpu.SMEM)
 
 
 def on_device(
@@ -218,51 +212,52 @@
     device = edge_sender // owned
     turn = (my_h - device % Z_HI + Z_HI) % Z_HI
     place = (device // Z_HI) * height + turn * owned + edge_sender % owned
-    sender = (place + (device // Z_HI) * NOTE).reshape(1, slots)
     place = place.reshape(1, slots)
-    own, note, target = pl.pallas_call(
-        functools.partial(plan_kernel, ROOM, height),
+    own, note, target, rest = pl.pallas_call(
+        functools.partial(plan_kernel, height),
         in_specs=[VMEM] * 4,
-        out_specs=[VMEM] * 3,
+        out_specs=[VMEM] * 4,
         out_shape=[
             jax.ShapeDtypeStruct((owned, 2 * width), jnp.bfloat16),
-            jax.ShapeDtypeStruct((NOTE, width), jnp.bfloat16),
+            jax.ShapeDtypeStruct((tall * ROOM, width), jnp.bfloat16),
+            jax.ShapeDtypeStruct((1, slots), jnp.int32),
             jax.ShapeDtypeStruct((1, slots), jnp.int32),
         ],
         cost_estimate=pl.CostEstimate(
-            flops=2 * NOTE * slots * width, bytes_accessed=256 * 1024, transcendentals=0
+            flops=2 * tall * ROOM * slots * width, bytes_accessed=256 * 1024, transcendentals=0
         ),
         compiler_params=pltpu.CompilerParams(vmem_limit_bytes=16 * 1024 * 1024),
     )(node_latents, agg_cotangent, place, edge_count)
     from_below = lax.ppermute(node_latents, "col", up)
     from_above = lax.ppermute(node_latents, "col", down)
-    asked = lax.all_to_all(edge_receiver.reshape(rows, 1, per_block), "row", 0, 0, tiled=True)
+    my_row = lax.axis_index("row").astype(jnp.int32).reshape(1, 1)
+    indices = jnp.broadcast_to(edge_receiver.reshape(1, 1, slots), (rows, 1, slots))
+    asked = lax.all_to_all(indices, "row", 0, 0, tiled=True)
     answer = pl.pallas_call(
         answer_kernel,
-        in_specs=[VMEM] * 2,
+        in_specs=[VMEM, SMEM, VMEM],
         out_specs=VMEM,
         out_shape=jax.ShapeDtypeStruct((slots, 2 * width), jnp.bfloat16),
         cost_estimate=pl.CostEstimate(
             flops=4_000_000_000, bytes_accessed=640 * 1024, transcendentals=0
         ),
         compiler_params=pltpu.CompilerParams(vmem_limit_bytes=16 * 1024 * 1024),
-    )(asked, own)
+    )(asked, my_row, own)
     answer, from_below, from_above = lax.optimization_barrier((answer, from_below, from_above))
     recv = lax.all_to_all(answer, "row", 0, 0, tiled=True)
-    column = jnp.concatenate([node_latents, from_below, from_above, note], axis=0)
+    column = jnp.concatenate([node_latents, from_below, from_above], axis=0)
     table = lax.all_gather(column, "col", axis=0, tiled=True, axis_index_groups=along_y)
 
     vectors = jnp.stack([b_in, b_out, ln_gain, ln_bias])
 
-    new_edges, packed, compact, overflow = pl.pallas_call(
+    new_edges, packed, compact = pl.pallas_call(
         edge_kernel,
-        in_specs=[VMEM] * 7 + [ANY] * 3,
-        out_specs=[VMEM] * 3 + [pl.BlockSpec(memory_space=pltpu.SMEM)],
+        in_specs=[VMEM] * 8 + [ANY] * 3,
+        out_specs=[VMEM] * 3,
         out_shape=[
             jax.ShapeDtypeStruct((slots, width), jnp.bfloat16),
             jax.ShapeDtypeStruct((slots, 2 * width), jnp.bfloat16),
             jax.ShapeDtypeStruct((tall * ROOM, width), jnp.bfloat16),
-            jax.ShapeDtypeStruct((1, 1), jnp.int32),
         ],
         scratch_shapes=[
             pltpu.VMEM((3 * width, width), jnp.bfloat16),
@@ -277,33 +272,34 @@
             transcendentals=slots * width,
         ),
     )(
-        table, sender, target, recv, edge_count, w_out, vectors,
+        table, place, target, note, recv, edge_count, w_out, vectors,
         w_in, edge_latents, edge_cotangent,
     )
 
-    def short_way():
-        arrived = lax.all_to_all(compact, "col", 0, 0, tiled=True, axis_index_groups=along_y)
-        mine = (lax.axis_index("col") // Z_HI).astype(jnp.int32).reshape(1, 1)
-        return pl.pallas_call(
-            place_kernel,
-            in_specs=[VMEM] * 2 + [pl.BlockSpec(memory_space=pltpu.SMEM)],
-            out_specs=VMEM,
-            out_shape=jax.ShapeDtypeStruct((height, width), jnp.float32),
-            compiler_params=pltpu.CompilerParams(vmem_limit_bytes=16 * 1024 * 1024),
-        )(arrived, table, mine)
-
-    def long_way():
+    arrived = lax.all_to_all(compact, "col", 0, 0, tiled=True, axis_index_groups=along_y)
+    column_sum, overflow = pl.pallas_call(
+        place_kernel,
+        in_specs=[VMEM],
+        out_specs=[VMEM, SMEM],
+        out_shape=[
+            jax.ShapeDtypeStruct((height, width), jnp.float32),
+            jax.ShapeDtypeStruct((1, 1), jnp.int32),
+        ],
+        compiler_params=pltpu.CompilerParams(vmem_limit_bytes=16 * 1024 * 1024),
+    )(arrived)
+
+    def with_rest():
         partial = pl.pallas_call(
             dense_kernel,
             in_specs=[VMEM] * 2,
             out_specs=VMEM,
             out_shape=jax.ShapeDtypeStruct((tall * height, width), jnp.bfloat16),
             compiler_params=pltpu.CompilerParams(vmem_limit_bytes=16 * 1024 * 1024),
-        )(packed, place)
+        )(packed, rest)
         parts = lax.all_to_all(partial, "col", 0, 0, tiled=True, axis_index_groups=along_y)
-        return jnp.sum(parts.reshape(tall, height, width).astype(jnp.float32), axis=0)
-
-    column_sum = lax.cond(overflow[0, 0] > 0, long_way, short_way)
+        return column_sum + jnp.sum(parts.reshape(tall, height, width).astype(jnp.float32), axis=0)
+
+    column_sum = lax.cond(overflow[0, 0] > 0, with_rest, lambda: column_sum)
     away = column_sum.astype(jnp.bfloat16)
     to_below = lax.ppermute(away[owned : 2 * owned], "col", down)
     to_above = lax.ppermute(away[2 * owned :], "col", up)
@@ -311,14 +307,14 @@
     returned = lax.all_to_all(packed, "row", 0, 0, tiled=True)
     aggregated, grad_nodes = pl.pallas_call(
         owner_kernel,
-        in_specs=[VMEM] * 6,
+        in_specs=[VMEM, SMEM] + [VMEM] * 5,
         out_specs=[VMEM] * 2,
         out_shape=[jax.ShapeDtypeStruct((owned, width), jnp.bfloat16)] * 2,
         cost_estimate=pl.CostEstimate(
             flops=2 * owned * width * (2 * slots + 2 * width), bytes_accessed=2 * 1024 * 1024, transcendentals=0
         ),
         compiler_params=pltpu.CompilerParams(vmem_limit_bytes=16 * 1024 * 1024),
-    )(asked, returned, column_sum, to_below, to_above, w_in)
+    )(asked, my_row, returned, column_sum, to_below, to_above, w_in)
     d_edge = dot_t(packed[:, width:], w_in[:width])
     grad_edges = (edge_cotangent.astype(jnp.float32) + d_edge).astype(jnp.bfloat16)
     return (new_edges, aggregated, grad_nodes, grad_edges)

time: 124 us -> 120 us (0.968)
  blocking collectives: 25.2 us -> 38.6 us
  waiting for transfers between devices: 22.1 us -> 10.5 us
  starting transfers between devices: 59.7 us -> 54.3 us
  Pallas kernels: 9.21 us -> 7.53 us
    all_to_all x0 -> x1, blocking collectives: none -> 15.4 us  [on_device(): lax.all_to_all(compact, 'col', 0, 0, tiled=True, axis_index_groups=along_y)]
    all_to_all x2 -> x1, waiting for transfers between devices: 11.8 us -> 1.2 us  [on_device(): asked = lax.all_to_all(indices, 'row', 0, 0, tiled=True)]
    all_to_all x2 -> x1, starting transfers between devices: 13.4 us -> 8.28 us  [on_device(): asked = lax.all_to_all(indices, 'row', 0, 0, tiled=True)]
    all_gather x1, blocking collectives: 25.2 us -> 23.2 us  [on_device(): lax.all_gather(column, 'col', axis=0, tiled=True, axis_index_groups=along_y)]
    pallas_call x5, Pallas kernels: 9.21 us -> 7.53 us  [the longest x1 3.65 us: on_device(): pl.pallas_call(edge_kernel, in_specs=[VMEM] * 8 + [ANY] * 3, out_specs=[V...]
    reshape x1 -> x0, local copies, waits for them, and re-layouts: 1.37 us -> none  [on_device(): edge_receiver.reshape(rows, 1, per_block)]
    broadcast_in_dim x0 -> x1, local copies, waits for them, and re-layouts: none -> 1.31 us  [on_device(): jnp.broadcast_to(edge_receiver.reshape(1, 1, slots), (rows, 1, slots))]
  transfers between devices with their start and end apart: 8 -> 7, of which waited for: 3 -> 2; matrix products, arithmetic and copies ran while one was open for 3% -> 3% of each run, Pallas kernels for 1% -> 1%
where the time goes in v7:
time: 120 us; the launch traced here: 119 us
  starting transfers between devices  54.3 us (45%)
  blocking collectives  38.6 us (32%)
  waiting for transfers between devices  10.5 us (9%)
  Pallas kernels  7.53 us (6%)
  local copies, waits for them, and re-layouts  3.53 us (3%)
  matrix products  1.99 us (2%)
  between operations  1.55 us (1%)
    all_gather x1, blocking collectives, on_device(): lax.all_gather(column, 'col', axis=0, tiled=True, axis_index_groups=along_y)  23.2 us
    all_to_all x1, blocking collectives, on_device(): lax.all_to_all(compact, 'col', 0, 0, tiled=True, axis_index_groups=along_y)  15.4 us
    all_to_all x1, starting transfers between devices, on_device(): returned = lax.all_to_all(packed, 'row', 0, 0, tiled=True)  14.2 us
    ppermute x1, starting transfers between devices, on_device(): from_below = lax.ppermute(node_latents, 'col', up)  10.6 us
    ppermute x1, waiting for transfers between devices, on_device(): to_above = lax.ppermute(away[2 * owned:], 'col', up)  9.32 us
    all_to_all x1, starting transfers between devices, on_device(): asked = lax.all_to_all(indices, 'row', 0, 0, tiled=True)  8.28 us
    all_to_all x1, starting transfers between devices, on_device(): recv = lax.all_to_all(answer, 'row', 0, 0, tiled=True)  7.09 us
    ppermute x1, starting transfers between devices, on_device(): to_above = lax.ppermute(away[2 * owned:], 'col', up)  6.31 us
  transfers between devices with their start and end apart: 7, of which 2 were waited for; matrix products, arithmetic and copies ran while one was open for 3% of the time, Pallas kernels for 1%

profile of v7, /device:TPU:69, one launch (start us, length us, event | category | flops | bytes accessed | tf_op | source)
XLA Modules:
  0.0 118.8 jit_solution(10425381843563567662)
XLA Ops:
  0.6 10.6 %collective-permute-start = (bf16[32,512]{1,0:T(8,128)(2,1)}, bf16[32,512]{1,0:T(8,128)(2,1)S(1)}, u32[]{:S(2)}, u32[]{:S(2)}) collective-permute-start(bf16[32,512]{1,0:T(8,128)(2,1)} %nodes.1), channel_id=1, source_target_pairs={{0,1},{1,2},{2,0},{3,4},{4,5},{5,3},{6,7},{7,8},{8,6},{9,10},{10,1... | collective-permute-start | bytes 98312 | tf_op jit(solution)/shard_map/ppermute | solution.py:231
  11.3 4.7 %collective-permute-start.1 = (bf16[32,512]{1,0:T(8,128)(2,1)}, bf16[32,512]{1,0:T(8,128)(2,1)S(1)}, u32[]{:S(2)}, u32[]{:S(2)}) collective-permute-start(bf16[32,512]{1,0:T(8,128)(2,1)} %nodes.1), channel_id=1, source_target_pairs={{1,0},{2,1},{0,2},{4,3},{5,4},{3,5},{7,6},{8,7},{6,8},{10,9},{11,1... | collective-permute-start | bytes 98312 | tf_op jit(solution)/shard_map/ppermute | solution.py:232
  15.9 1.3 %broadcast_in_dim.2 = s32[32,1,256]{2,1,0:T(1,128)} broadcast(s32[256]{0:T(256)} %param.18), dimensions={2} | broadcast | bytes 33792 | tf_op jit(solution)/shard_map/broadcast_in_dim | solution.py:234
  17.3 8.3 %all-to-all-start.1 = ((s32[32,1,256]{2,1,0:T(1,128)}), s32[32,1,256]{2,1,0:T(1,128)S(1)}, u32[]{:S(2)}, u32[]{:S(2)}) async-start(s32[32,1,256]{2,1,0:T(1,128)} %broadcast_in_dim.2), calls=%async_computation.1 | async-start | bytes 65536 | tf_op jit(solution)/shard_map/all_to_all | solution.py:235
  25.6 0.7 fusion.6
  26.3 0.0 copy-start.4
  26.3 0.7 copy-done.4
  27.0 0.0 copy-start.6
  27.1 0.7 copy-done.6
  27.7 0.0 copy-start.8
  27.7 0.8 copy-done.8
  28.5 0.6 shard_map.156
  29.0 1.2 %all-to-all-done.1.asked = s32[32,1,256]{2,1,0:T(1,128)S(1)} async-done(((s32[32,1,256]{2,1,0:T(1,128)}), s32[32,1,256]{2,1,0:T(1,128)S(1)}, u32[]{:S(2)}, u32[]{:S(2)}) %all-to-all-start.1) | async-done | bytes 32800 | tf_op jit(solution)/shard_map/all_to_all | solution.py:235
  30.2 0.0 copy-start.9
  30.2 0.0 copy-start.11
  30.2 0.0 copy-start.12
  30.3 0.0 copy-start.5
  30.3 1.2 %shard_map.157 = bf16[256,1024]{1,0:T(8,128)(2,1)} custom-call(s32[32,1,256]{2,1,0:T(1,128)S(1)} %all-to-all-done.1.asked, s32[1,1]{1,0:T(1,128)} %bitcast.1.my_row, bf16[32,1024]{1,0:T(8,128)(2,1)S(1)} %get-tuple-element.31.own), custom_call_target="tpu_custom_call" | custom-call | flops 4000000000 | bytes 655360 | tf_op jit(solution)/shard_map/pallas_call | solution.py:236
  31.5 0.0 copy-start.1
  31.5 0.0 copy-start.2
  31.5 0.0 copy-start.7
  31.5 0.0 collective-permute-done
  31.5 0.0 collective-permute-done.1
  31.5 7.1 %all-to-all-start.2 = ((bf16[32,8,1024]{2,1,0:T(8,128)(2,1)}), bf16[32,8,1024]{2,1,0:T(8,128)(2,1)S(1)}, u32[]{:S(2)}, u32[]{:S(2)}) async-start(bf16[32,8,1024]{2,1,0:T(8,128)(2,1)} %bitcast.3), calls=%async_computation.2 | async-start | bytes 1048576 | tf_op jit(solution)/shard_map/all_to_all | solution.py:247
  38.6 0.0 copy-done.9
  38.6 0.0 copy-done.10
  38.6 0.0 copy-done.11
  38.6 0.0 copy-done.12
  38.6 0.0 copy-done.5
  38.7 23.2 %all_gather.3.table = bf16[768,512]{1,0:T(8,128)(2,1)S(1)} all-gather(bf16[96,512]{1,0:T(8,128)(2,1)S(1)} %pad_maximum_fusion), channel_id=1, replica_groups={{0,3,6,9,12,15,18,21},{1,4,7,10,13,16,19,22},{2,5,8,11,14,17,20,23},{24..., dimensions={0}, use_global_device_ids=true | all-gather | bytes 884736 | tf_op jit(solution)/shard_map/all_gather | solution.py:249
  61.8 0.0 all-to-all-done.2
  61.8 0.0 copy-done.1
  61.8 0.0 copy-done.2
  61.8 0.0 copy-done.3
  61.9 0.0 copy-done.7
  61.9 3.7 %shard_map.158 = (bf16[256,512]{1,0:T(8,128)(2,1)}, bf16[256,1024]{1,0:T(8,128)(2,1)}, bf16[384,512]{1,0:T(8,128)(2,1)S(1)}) custom-call(bf16[768,512]{1,0:T(8,128)(2,1)S(1)} %all_gather.3.table, s32[1,256]{1,0:T(1,128)S(1)} %bitcast.20, s32[1,256]{1,0:T(1,128)S(1)} %get-tuple-element.34.target, bf16[384,512]{1,0:T(8,128)(2,1)S(1)} %get-tuple-element.35.note, ...), custom_call_target="tpu_custom_call" | custom-call | flops 1073741824 | bytes 6291456 | tf_op jit(solution)/shard_map/pallas_call | solution.py:253
  65.5 15.4 %all_to_all.46 = bf16[8,48,512]{2,1,0:T(8,128)(2,1)S(1)} all-to-all(bf16[8,48,512]{2,1,0:T(8,128)(2,1)S(1)} %bitcast.18), channel_id=1, replica_groups={{0,3,6,9,12,15,18,21},{1,4,7,10,13,16,19,22},{2,5,8,11,14,17,20,23},{24..., dimensions={0} | all-to-all | bytes 786432 | tf_op jit(solution)/shard_map/all_to_all | solution.py:279
  80.9 0.8 shard_map.159
  82.4 0.0 copy-start
  82.4 14.2 %all-to-all-start.3 = ((bf16[32,8,1024]{2,1,0:T(8,128)(2,1)}), bf16[32,8,1024]{2,1,0:T(8,128)(2,1)S(1)}, u32[]{:S(2)}, u32[]{:S(2)}) async-start(bf16[32,8,1024]{2,1,0:T(8,128)(2,1)} %bitcast.9), calls=%async_computation.3 | async-start | bytes 1048576 | tf_op jit(solution)/shard_map/all_to_all | solution.py:307
  96.7 6.3 %collective-permute-start.3 = (bf16[32,512]{1,0:T(8,128)(2,1)S(1)}, bf16[32,512]{1,0:T(8,128)(2,1)S(1)}, u32[]{:S(2)}, u32[]{:S(2)}) collective-permute-start(bf16[32,512]{1,0:T(8,128)(2,1)S(1)} %get-tuple-element.45), channel_id=1, source_target_pairs={{0,1},{1,2},{2,0},{3,4},{4,5},{5,3},{6,7},{7,8},{8,6},{9,10},{10,1... | collective-permute-start | bytes 98312 | tf_op jit(solution)/shard_map/ppermute | solution.py:305
  103.0 3.2 %collective-permute-start.2 = (bf16[32,512]{1,0:T(8,128)(2,1)S(1)}, bf16[32,512]{1,0:T(8,128)(2,1)S(1)}, u32[]{:S(2)}, u32[]{:S(2)}) collective-permute-start(bf16[32,512]{1,0:T(8,128)(2,1)S(1)} %get-tuple-element.46), channel_id=1, source_target_pairs={{1,0},{2,1},{0,2},{4,3},{5,4},{3,5},{7,6},{8,7},{6,8},{10,9},{11,1... | collective-permute-start | bytes 98312 | tf_op jit(solution)/shard_map/ppermute | solution.py:304
  106.1 0.0 copy-done
  106.1 2.0 %fusion = bf16[256,512]{1,0:T(8,128)(2,1)} fusion(bf16[1536,512]{1,0:T(8,128)(2,1)S(1)} %copy-done, bf16[256,512]{1,0:T(8,128)(2,1)S(1)} %copy-done.3, bf16[256,1024]{1,0:T(8,128)(2,1)} %get-tuple-element.38), kind=kOutput, calls=%fused_computation.2 | convolution fusion | flops 134610944 | bytes 1310720 | tf_op jit(solution)/shard_map/dot_general | solution.py:19
  108.1 9.3 %collective-permute-done.3.to_above = bf16[32,512]{1,0:T(8,128)(2,1)S(1)} collective-permute-done((bf16[32,512]{1,0:T(8,128)(2,1)S(1)}, bf16[32,512]{1,0:T(8,128)(2,1)S(1)}, u32[]{:S(2)}, u32[]{:S(2)}) %collective-permute-start.3) | collective-permute-done | bytes 32800 | tf_op jit(solution)/shard_map/ppermute | solution.py:305
  117.5 0.0 collective-permute-done.2.to_below
  117.5 0.0 all-to-all-done.3
  117.5 1.3 %shard_map.160 = (bf16[32,512]{1,0:T(8,128)(2,1)}, bf16[32,512]{1,0:T(8,128)(2,1)}) custom-call(s32[32,1,256]{2,1,0:T(1,128)S(1)} %all-to-all-done.1.asked, s32[1,1]{1,0:T(1,128)} %bitcast.1.my_row, bf16[256,1024]{1,0:T(8,128)(2,1)S(1)} %bitcast.15, f32[96,512]{1,0:T(8,128)S(1)} %get-tuple-element.47.column_sum, ...), custom_call_target="tpu_custom_call" | custom-call | flops 50331648 | bytes 2097152 | tf_op jit(solution)/shard_map/pallas_call | solution.py:308
  (7 shorter events, 0.1 us)
Async XLA Ops:
  0.6 30.8 %collective-permute-start = (bf16[32,512]{1,0:T(8,128)(2,1)}, bf16[32,512]{1,0:T(8,128)(2,1)S(1)}, u32[]{:S(2)}, u32[]{:S(2)}) collective-permute-start(bf16[32,512]{1,0:T(8,128)(2,1)} %nodes.1), channel_id=1, source_target_pairs={{0,1},{1,2},{2,0},{3,4},{4,5},{5,3},{6,7},{7,8},{8,6},{9,10},{10,1... | collective-permute-start | bytes 98312 | tf_op jit(solution)/shard_map/ppermute | solution.py:231
  11.3 20.2 %collective-permute-start.1 = (bf16[32,512]{1,0:T(8,128)(2,1)}, bf16[32,512]{1,0:T(8,128)(2,1)S(1)}, u32[]{:S(2)}, u32[]{:S(2)}) collective-permute-start(bf16[32,512]{1,0:T(8,128)(2,1)} %nodes.1), channel_id=1, source_target_pairs={{1,0},{2,1},{0,2},{4,3},{5,4},{3,5},{7,6},{8,7},{6,8},{10,9},{11,1... | collective-permute-start | bytes 98312 | tf_op jit(solution)/shard_map/ppermute | solution.py:232
  17.3 13.0 %all-to-all-start.1 = ((s32[32,1,256]{2,1,0:T(1,128)}), s32[32,1,256]{2,1,0:T(1,128)S(1)}, u32[]{:S(2)}, u32[]{:S(2)}) async-start(s32[32,1,256]{2,1,0:T(1,128)} %broadcast_in_dim.2), calls=%async_computation.1 | async-start | bytes 65536 | tf_op jit(solution)/shard_map/all_to_all | solution.py:235
  26.3 0.8 copy-start.4
  27.0 0.7 copy-start.6
  27.7 0.8 copy-start.8
  30.2 8.3 %copy-start.9 = (f32[512]{0:T(512)S(1)}, f32[512]{0:T(512)}, u32[]{:S(2)}) copy-start(f32[512]{0:T(512)} %param.25) | copy-start | bytes 6148
  30.2 8.4 %copy-start.10 = (f32[512]{0:T(512)S(1)}, f32[512]{0:T(512)}, u32[]{:S(2)}) copy-start(f32[512]{0:T(512)} %param.24) | copy-start | bytes 6148
  30.2 8.4 %copy-start.11 = (f32[512]{0:T(512)S(1)}, f32[512]{0:T(512)}, u32[]{:S(2)}) copy-start(f32[512]{0:T(512)} %param.23) | copy-start | bytes 6148
  30.2 8.4 %copy-start.12 = (f32[512]{0:T(512)S(1)}, f32[512]{0:T(512)}, u32[]{:S(2)}) copy-start(f32[512]{0:T(512)} %param.21) | copy-start | bytes 6148
  30.3 8.4 %copy-start.5 = (bf16[32,512]{1,0:T(8,128)(2,1)S(1)}, bf16[32,512]{1,0:T(8,128)(2,1)}, u32[]{:S(2)}) copy-start(bf16[32,512]{1,0:T(8,128)(2,1)} %nodes.1) | copy-start | bytes 98308
  31.5 30.4 %copy-start.1 = (bf16[512,512]{1,0:T(8,128)(2,1)S(1)}, bf16[512,512]{1,0:T(8,128)(2,1)}, u32[]{:S(2)}) copy-start(bf16[512,512]{1,0:T(8,128)(2,1)} %w_out.1) | copy-start | bytes 1572868
  31.5 30.4 %copy-start.2 = (bf16[256,512]{1,0:T(8,128)(2,1)S(1)}, bf16[256,512]{1,0:T(8,128)(2,1)}, u32[]{:S(2)}) copy-start(bf16[256,512]{1,0:T(8,128)(2,1)} %edges_hbm.1) | copy-start | bytes 786436
  31.5 30.4 %copy-start.3 = (bf16[256,512]{1,0:T(8,128)(2,1)S(1)}, bf16[256,512]{1,0:T(8,128)(2,1)}, u32[]{:S(2)}) copy-start(bf16[256,512]{1,0:T(8,128)(2,1)} %cot_hbm.1) | copy-start | bytes 786436
  31.5 30.4 %copy-start.7 = (s32[1,32]{1,0:T(1,128)S(1)}, s32[1,32]{1,0:T(1,128)}, u32[]{:S(2)}) copy-start(s32[1,32]{1,0:T(1,128)} %counts.3) | copy-start | bytes 388
  31.5 30.3 %all-to-all-start.2 = ((bf16[32,8,1024]{2,1,0:T(8,128)(2,1)}), bf16[32,8,1024]{2,1,0:T(8,128)(2,1)S(1)}, u32[]{:S(2)}, u32[]{:S(2)}) async-start(bf16[32,8,1024]{2,1,0:T(8,128)(2,1)} %bitcast.3), calls=%async_computation.2 | async-start | bytes 1048576 | tf_op jit(solution)/shard_map/all_to_all | solution.py:247
  82.4 23.8 %copy-start = (bf16[1536,512]{1,0:T(8,128)(2,1)S(1)}, bf16[1536,512]{1,0:T(8,128)(2,1)}, u32[]{:S(2)}) copy-start(bf16[1536,512]{1,0:T(8,128)(2,1)} %w_in.1) | copy-start | bytes 4718596
  82.4 35.1 %all-to-all-start.3 = ((bf16[32,8,1024]{2,1,0:T(8,128)(2,1)}), bf16[32,8,1024]{2,1,0:T(8,128)(2,1)S(1)}, u32[]{:S(2)}, u32[]{:S(2)}) async-start(bf16[32,8,1024]{2,1,0:T(8,128)(2,1)} %bitcast.9), calls=%async_computation.3 | async-start | bytes 1048576 | tf_op jit(solution)/shard_map/all_to_all | solution.py:307
  96.7 20.8 %collective-permute-start.3 = (bf16[32,512]{1,0:T(8,128)(2,1)S(1)}, bf16[32,512]{1,0:T(8,128)(2,1)S(1)}, u32[]{:S(2)}, u32[]{:S(2)}) collective-permute-start(bf16[32,512]{1,0:T(8,128)(2,1)S(1)} %get-tuple-element.45), channel_id=1, source_target_pairs={{0,1},{1,2},{2,0},{3,4},{4,5},{5,3},{6,7},{7,8},{8,6},{9,10},{10,1... | collective-permute-start | bytes 98312 | tf_op jit(solution)/shard_map/ppermute | solution.py:305
  103.0 14.5 %collective-permute-start.2 = (bf16[32,512]{1,0:T(8,128)(2,1)S(1)}, bf16[32,512]{1,0:T(8,128)(2,1)S(1)}, u32[]{:S(2)}, u32[]{:S(2)}) collective-permute-start(bf16[32,512]{1,0:T(8,128)(2,1)S(1)} %get-tuple-element.46), channel_id=1, source_target_pairs={{1,0},{2,1},{0,2},{4,3},{5,4},{3,5},{7,6},{8,7},{6,8},{10,9},{11,1... | collective-permute-start | bytes 98312 | tf_op jit(solution)/shard_map/ppermute | solution.py:304

commit v8 on v7

--- a/solution.py
+++ b/solution.py
@@ -229,9 +229,10 @@
         compiler_params=pltpu.CompilerParams(vmem_limit_bytes=16 * 1024 * 1024),
     )(node_latents, agg_cotangent, place, edge_count)
     from_below = lax.ppermute(node_latents, "col", up)
-    from_above = lax.ppermute(node_latents, "col", down)
+    indices = jnp.broadcast_to(edge_receiver.reshape(1, 1, slots), (rows, 1, slots))
+    latents, indices = lax.optimization_barrier((node_latents, indices))
+    from_above = lax.ppermute(latents, "col", down)
     my_row = lax.axis_index("row").astype(jnp.int32).reshape(1, 1)
-    indices = jnp.broadcast_to(edge_receiver.reshape(1, 1, slots), (rows, 1, slots))
     asked = lax.all_to_all(indices, "row", 0, 0, tiled=True)
     answer = pl.pallas_call(
         answer_kernel,

time: 120 us -> 120 us (level)
  the two profiles are of different devices: /device:TPU:69 before, /device:TPU:1 now
where the time goes in v8:
time: 120 us; the launch traced here: 119 us
  starting transfers between devices  56.9 us (47%)
  blocking collectives  39 us (32%)
  waiting for transfers between devices  8.17 us (7%)
  Pallas kernels  7.54 us (6%)
  local copies, waits for them, and re-layouts  3.53 us (3%)
  matrix products  1.99 us (2%)
  between operations  1.55 us (1%)
    all_gather x1, blocking collectives, on_device(): lax.all_gather(column, 'col', axis=0, tiled=True, axis_index_groups=along_y)  23 us
    all_to_all x1, blocking collectives, on_device(): lax.all_to_all(compact, 'col', 0, 0, tiled=True, axis_index_groups=along_y)  16 us
    all_to_all x1, starting transfers between devices, on_device(): returned = lax.all_to_all(packed, 'row', 0, 0, tiled=True)  13.7 us
    ppermute x1, starting transfers between devices, on_device(): from_below = lax.ppermute(node_latents, 'col', up)  11.5 us
    all_to_all x1, starting transfers between devices, on_device(): asked = lax.all_to_all(indices, 'row', 0, 0, tiled=True)  10.5 us
    all_to_all x1, starting transfers between devices, on_device(): recv = lax.all_to_all(answer, 'row', 0, 0, tiled=True)  9.13 us
    ppermute x1, starting transfers between devices, on_device(): to_above = lax.ppermute(away[2 * owned:], 'col', up)  5.47 us
    ppermute x1, waiting for transfers between devices, on_device(): to_above = lax.ppermute(away[2 * owned:], 'col', up)  3.79 us
  transfers between devices with their start and end apart: 7, of which 3 were waited for; matrix products, arithmetic and copies ran while one was open for 3% of the time, Pallas kernels for 1%

profile of v8, /device:TPU:1, one launch (start us, length us, event | category | flops | bytes accessed | tf_op | source)
XLA Modules:
  0.0 119.5 jit_solution(11305150078555194166)
XLA Ops:
  0.6 11.5 %collective-permute-start = (bf16[32,512]{1,0:T(8,128)(2,1)}, bf16[32,512]{1,0:T(8,128)(2,1)S(1)}, u32[]{:S(2)}, u32[]{:S(2)}) collective-permute-start(bf16[32,512]{1,0:T(8,128)(2,1)} %nodes.1), channel_id=1, source_target_pairs={{0,1},{1,2},{2,0},{3,4},{4,5},{5,3},{6,7},{7,8},{8,6},{9,10},{10,1... | collective-permute-start | bytes 98312 | tf_op jit(solution)/shard_map/ppermute | solution.py:231
  12.1 1.3 %broadcast_in_dim.2 = s32[32,1,256]{2,1,0:T(1,128)} broadcast(s32[256]{0:T(256)} %param.18), dimensions={2} | broadcast | bytes 33792 | tf_op jit(solution)/shard_map/broadcast_in_dim | solution.py:232
  13.4 10.5 %all-to-all-start.1 = ((s32[32,1,256]{2,1,0:T(1,128)}), s32[32,1,256]{2,1,0:T(1,128)S(1)}, u32[]{:S(2)}, u32[]{:S(2)}) async-start(s32[32,1,256]{2,1,0:T(1,128)} %broadcast_in_dim.2), calls=%async_computation.1 | async-start | bytes 65536 | tf_op jit(solution)/shard_map/all_to_all | solution.py:236
  24.0 2.9 %collective-permute-start.1 = (bf16[32,512]{1,0:T(8,128)(2,1)}, bf16[32,512]{1,0:T(8,128)(2,1)S(1)}, u32[]{:S(2)}, u32[]{:S(2)}) collective-permute-start(bf16[32,512]{1,0:T(8,128)(2,1)} %nodes.1), channel_id=1, source_target_pairs={{1,0},{2,1},{0,2},{4,3},{5,4},{3,5},{7,6},{8,7},{6,8},{10,9},{11,1... | collective-permute-start | bytes 98312 | tf_op jit(solution)/shard_map/ppermute | solution.py:234
  26.9 0.7 fusion.6
  27.6 0.0 copy-start.4
  27.6 0.7 copy-done.4
  28.4 0.0 copy-start.6
  28.4 0.7 copy-done.6
  29.0 0.0 copy-start.8
  29.0 0.8 copy-done.8
  29.8 0.6 shard_map.156
  30.3 1.3 %all-to-all-done.1.asked = s32[32,1,256]{2,1,0:T(1,128)S(1)} async-done(((s32[32,1,256]{2,1,0:T(1,128)}), s32[32,1,256]{2,1,0:T(1,128)S(1)}, u32[]{:S(2)}, u32[]{:S(2)}) %all-to-all-start.1) | async-done | bytes 32800 | tf_op jit(solution)/shard_map/all_to_all | solution.py:236
  31.6 0.0 copy-start.9
  31.6 0.0 copy-start.10
  31.6 0.0 copy-start.11
  31.6 0.0 copy-start.12
  31.6 0.0 copy-start.5
  31.6 1.2 shard_map.157
  32.8 0.0 copy-start.1
  32.8 0.0 copy-start.3
  32.8 0.0 collective-permute-done.1
  32.8 0.0 collective-permute-done
  32.8 9.1 %all-to-all-start.2 = ((bf16[32,8,1024]{2,1,0:T(8,128)(2,1)}), bf16[32,8,1024]{2,1,0:T(8,128)(2,1)S(1)}, u32[]{:S(2)}, u32[]{:S(2)}) async-start(bf16[32,8,1024]{2,1,0:T(8,128)(2,1)} %bitcast.3), calls=%async_computation.2 | async-start | bytes 1048576 | tf_op jit(solution)/shard_map/all_to_all | solution.py:248
  42.0 0.0 copy-done.9
  42.0 0.0 copy-done.10
  42.0 0.0 copy-done.11
  42.0 0.0 copy-done.12
  42.1 0.0 copy-done.5
  42.1 23.0 %all_gather.3.table = bf16[768,512]{1,0:T(8,128)(2,1)S(1)} all-gather(bf16[96,512]{1,0:T(8,128)(2,1)S(1)} %pad_maximum_fusion), channel_id=1, replica_groups={{0,3,6,9,12,15,18,21},{1,4,7,10,13,16,19,22},{2,5,8,11,14,17,20,23},{24..., dimensions={0}, use_global_device_ids=true | all-gather | bytes 884736 | tf_op jit(solution)/shard_map/all_gather | solution.py:250
  65.1 0.0 all-to-all-done.2
  65.1 0.0 copy-done.1
  65.1 0.0 copy-done.2
  65.1 0.0 copy-done.3
  65.1 0.0 copy-done.7
  65.1 3.7 %shard_map.158 = (bf16[256,512]{1,0:T(8,128)(2,1)}, bf16[256,1024]{1,0:T(8,128)(2,1)}, bf16[384,512]{1,0:T(8,128)(2,1)S(1)}) custom-call(bf16[768,512]{1,0:T(8,128)(2,1)S(1)} %all_gather.3.table, s32[1,256]{1,0:T(1,128)S(1)} %bitcast.20, s32[1,256]{1,0:T(1,128)S(1)} %get-tuple-element.38.target, bf16[384,512]{1,0:T(8,128)(2,1)S(1)} %get-tuple-element.39.note, ...), custom_call_target="tpu_custom_call" | custom-call | flops 1073741824 | bytes 6291456 | tf_op jit(solution)/shard_map/pallas_call | solution.py:254
  68.8 16.0 %all_to_all.46 = bf16[8,48,512]{2,1,0:T(8,128)(2,1)S(1)} all-to-all(bf16[8,48,512]{2,1,0:T(8,128)(2,1)S(1)} %bitcast.18), channel_id=1, replica_groups={{0,3,6,9,12,15,18,21},{1,4,7,10,13,16,19,22},{2,5,8,11,14,17,20,23},{24..., dimensions={0} | all-to-all | bytes 786432 | tf_op jit(solution)/shard_map/all_to_all | solution.py:280
  84.8 0.8 shard_map.159
  86.2 0.0 copy-start
  86.3 13.7 %all-to-all-start.3 = ((bf16[32,8,1024]{2,1,0:T(8,128)(2,1)}), bf16[32,8,1024]{2,1,0:T(8,128)(2,1)S(1)}, u32[]{:S(2)}, u32[]{:S(2)}) async-start(bf16[32,8,1024]{2,1,0:T(8,128)(2,1)} %bitcast.9), calls=%async_computation.3 | async-start | bytes 1048576 | tf_op jit(solution)/shard_map/all_to_all | solution.py:308
  100.0 5.5 %collective-permute-start.3 = (bf16[32,512]{1,0:T(8,128)(2,1)S(1)}, bf16[32,512]{1,0:T(8,128)(2,1)S(1)}, u32[]{:S(2)}, u32[]{:S(2)}) collective-permute-start(bf16[32,512]{1,0:T(8,128)(2,1)S(1)} %get-tuple-element.49), channel_id=1, source_target_pairs={{0,1},{1,2},{2,0},{3,4},{4,5},{5,3},{6,7},{7,8},{8,6},{9,10},{10,1... | collective-permute-start | bytes 98312 | tf_op jit(solution)/shard_map/ppermute | solution.py:306
  105.5 3.7 %collective-permute-start.2 = (bf16[32,512]{1,0:T(8,128)(2,1)S(1)}, bf16[32,512]{1,0:T(8,128)(2,1)S(1)}, u32[]{:S(2)}, u32[]{:S(2)}) collective-permute-start(bf16[32,512]{1,0:T(8,128)(2,1)S(1)} %get-tuple-element.50), channel_id=1, source_target_pairs={{1,0},{2,1},{0,2},{4,3},{5,4},{3,5},{7,6},{8,7},{6,8},{10,9},{11,1... | collective-permute-start | bytes 98312 | tf_op jit(solution)/shard_map/ppermute | solution.py:305
  109.2 0.0 copy-done
  109.2 2.0 %fusion = bf16[256,512]{1,0:T(8,128)(2,1)} fusion(bf16[1536,512]{1,0:T(8,128)(2,1)S(1)} %copy-done, bf16[256,512]{1,0:T(8,128)(2,1)S(1)} %copy-done.3, bf16[256,1024]{1,0:T(8,128)(2,1)} %get-tuple-element.42), kind=kOutput, calls=%fused_computation.2 | convolution fusion | flops 134610944 | bytes 1310720 | tf_op jit(solution)/shard_map/dot_general | solution.py:19
  111.2 3.8 %collective-permute-done.3.to_above = bf16[32,512]{1,0:T(8,128)(2,1)S(1)} collective-permute-done((bf16[32,512]{1,0:T(8,128)(2,1)S(1)}, bf16[32,512]{1,0:T(8,128)(2,1)S(1)}, u32[]{:S(2)}, u32[]{:S(2)}) %collective-permute-start.3) | collective-permute-done | bytes 32800 | tf_op jit(solution)/shard_map/ppermute | solution.py:306
  115.0 0.0 collective-permute-done.2.to_below
  115.0 3.1 %all-to-all-done.3 = bf16[32,8,1024]{2,1,0:T(8,128)(2,1)S(1)} async-done(((bf16[32,8,1024]{2,1,0:T(8,128)(2,1)}), bf16[32,8,1024]{2,1,0:T(8,128)(2,1)S(1)}, u32[]{:S(2)}, u32[]{:S(2)}) %all-to-all-start.3) | async-done | bytes 524320 | tf_op jit(solution)/shard_map/all_to_all | solution.py:308
  118.1 1.3 %shard_map.160 = (bf16[32,512]{1,0:T(8,128)(2,1)}, bf16[32,512]{1,0:T(8,128)(2,1)}) custom-call(s32[32,1,256]{2,1,0:T(1,128)S(1)} %all-to-all-done.1.asked, s32[1,1]{1,0:T(1,128)} %bitcast.1.my_row, bf16[256,1024]{1,0:T(8,128)(2,1)S(1)} %bitcast.15, f32[96,512]{1,0:T(8,128)S(1)} %get-tuple-element.51.column_sum, ...), custom_call_target="tpu_custom_call" | custom-call | flops 50331648 | bytes 2097152 | tf_op jit(solution)/shard_map/pallas_call | solution.py:309
  (7 shorter events, 0.1 us)
Async XLA Ops:
  0.6 32.2 %collective-permute-start = (bf16[32,512]{1,0:T(8,128)(2,1)}, bf16[32,512]{1,0:T(8,128)(2,1)S(1)}, u32[]{:S(2)}, u32[]{:S(2)}) collective-permute-start(bf16[32,512]{1,0:T(8,128)(2,1)} %nodes.1), channel_id=1, source_target_pairs={{0,1},{1,2},{2,0},{3,4},{4,5},{5,3},{6,7},{7,8},{8,6},{9,10},{10,1... | collective-permute-start | bytes 98312 | tf_op jit(solution)/shard_map/ppermute | solution.py:231
  13.4 18.2 %all-to-all-start.1 = ((s32[32,1,256]{2,1,0:T(1,128)}), s32[32,1,256]{2,1,0:T(1,128)S(1)}, u32[]{:S(2)}, u32[]{:S(2)}) async-start(s32[32,1,256]{2,1,0:T(1,128)} %broadcast_in_dim.2), calls=%async_computation.1 | async-start | bytes 65536 | tf_op jit(solution)/shard_map/all_to_all | solution.py:236
  24.0 8.9 %collective-permute-start.1 = (bf16[32,512]{1,0:T(8,128)(2,1)}, bf16[32,512]{1,0:T(8,128)(2,1)S(1)}, u32[]{:S(2)}, u32[]{:S(2)}) collective-permute-start(bf16[32,512]{1,0:T(8,128)(2,1)} %nodes.1), channel_id=1, source_target_pairs={{1,0},{2,1},{0,2},{4,3},{5,4},{3,5},{7,6},{8,7},{6,8},{10,9},{11,1... | collective-permute-start | bytes 98312 | tf_op jit(solution)/shard_map/ppermute | solution.py:234
  27.6 0.8 copy-start.4
  28.4 0.7 copy-start.6
  29.0 0.8 copy-start.8
  31.6 10.4 %copy-start.9 = (f32[512]{0:T(512)S(1)}, f32[512]{0:T(512)}, u32[]{:S(2)}) copy-start(f32[512]{0:T(512)} %param.25) | copy-start | bytes 6148
  31.6 10.4 %copy-start.10 = (f32[512]{0:T(512)S(1)}, f32[512]{0:T(512)}, u32[]{:S(2)}) copy-start(f32[512]{0:T(512)} %param.24) | copy-start | bytes 6148
  31.6 10.4 %copy-start.11 = (f32[512]{0:T(512)S(1)}, f32[512]{0:T(512)}, u32[]{:S(2)}) copy-start(f32[512]{0:T(512)} %param.23) | copy-start | bytes 6148
  31.6 10.4 %copy-start.12 = (f32[512]{0:T(512)S(1)}, f32[512]{0:T(512)}, u32[]{:S(2)}) copy-start(f32[512]{0:T(512)} %param.21) | copy-start | bytes 6148
  31.6 10.4 %copy-start.5 = (bf16[32,512]{1,0:T(8,128)(2,1)S(1)}, bf16[32,512]{1,0:T(8,128)(2,1)}, u32[]{:S(2)}) copy-start(bf16[32,512]{1,0:T(8,128)(2,1)} %nodes.1) | copy-start | bytes 98308
  32.8 32.3 %copy-start.1 = (bf16[512,512]{1,0:T(8,128)(2,1)S(1)}, bf16[512,512]{1,0:T(8,128)(2,1)}, u32[]{:S(2)}) copy-start(bf16[512,512]{1,0:T(8,128)(2,1)} %w_out.1) | copy-start | bytes 1572868
  32.8 32.3 %copy-start.2 = (bf16[256,512]{1,0:T(8,128)(2,1)S(1)}, bf16[256,512]{1,0:T(8,128)(2,1)}, u32[]{:S(2)}) copy-start(bf16[256,512]{1,0:T(8,128)(2,1)} %edges_hbm.1) | copy-start | bytes 786436
  32.8 32.3 %copy-start.3 = (bf16[256,512]{1,0:T(8,128)(2,1)S(1)}, bf16[256,512]{1,0:T(8,128)(2,1)}, u32[]{:S(2)}) copy-start(bf16[256,512]{1,0:T(8,128)(2,1)} %cot_hbm.1) | copy-start | bytes 786436
  32.8 32.3 %copy-start.7 = (s32[1,32]{1,0:T(1,128)S(1)}, s32[1,32]{1,0:T(1,128)}, u32[]{:S(2)}) copy-start(s32[1,32]{1,0:T(1,128)} %counts.3) | copy-start | bytes 388
  32.8 32.2 %all-to-all-start.2 = ((bf16[32,8,1024]{2,1,0:T(8,128)(2,1)}), bf16[32,8,1024]{2,1,0:T(8,128)(2,1)S(1)}, u32[]{:S(2)}, u32[]{:S(2)}) async-start(bf16[32,8,1024]{2,1,0:T(8,128)(2,1)} %bitcast.3), calls=%async_computation.2 | async-start | bytes 1048576 | tf_op jit(solution)/shard_map/all_to_all | solution.py:248
  86.2 23.0 %copy-start = (bf16[1536,512]{1,0:T(8,128)(2,1)S(1)}, bf16[1536,512]{1,0:T(8,128)(2,1)}, u32[]{:S(2)}) copy-start(bf16[1536,512]{1,0:T(8,128)(2,1)} %w_in.1) | copy-start | bytes 4718596
  86.3 31.9 %all-to-all-start.3 = ((bf16[32,8,1024]{2,1,0:T(8,128)(2,1)}), bf16[32,8,1024]{2,1,0:T(8,128)(2,1)S(1)}, u32[]{:S(2)}, u32[]{:S(2)}) async-start(bf16[32,8,1024]{2,1,0:T(8,128)(2,1)} %bitcast.9), calls=%async_computation.3 | async-start | bytes 1048576 | tf_op jit(solution)/shard_map/all_to_all | solution.py:308
  100.0 15.0 %collective-permute-start.3 = (bf16[32,512]{1,0:T(8,128)(2,1)S(1)}, bf16[32,512]{1,0:T(8,128)(2,1)S(1)}, u32[]{:S(2)}, u32[]{:S(2)}) collective-permute-start(bf16[32,512]{1,0:T(8,128)(2,1)S(1)} %get-tuple-element.49), channel_id=1, source_target_pairs={{0,1},{1,2},{2,0},{3,4},{4,5},{5,3},{6,7},{7,8},{8,6},{9,10},{10,1... | collective-permute-start | bytes 98312 | tf_op jit(solution)/shard_map/ppermute | solution.py:306
  105.5 9.5 %collective-permute-start.2 = (bf16[32,512]{1,0:T(8,128)(2,1)S(1)}, bf16[32,512]{1,0:T(8,128)(2,1)S(1)}, u32[]{:S(2)}, u32[]{:S(2)}) collective-permute-start(bf16[32,512]{1,0:T(8,128)(2,1)S(1)} %get-tuple-element.50), channel_id=1, source_target_pairs={{1,0},{2,1},{0,2},{4,3},{5,4},{3,5},{7,6},{8,7},{6,8},{10,9},{11,1... | collective-permute-start | bytes 98312 | tf_op jit(solution)/shard_map/ppermute | solution.py:305

commit v9 on v7

--- a/solution.py
+++ b/solution.py
@@ -79,22 +79,20 @@
 
 
 def edge_kernel(
-    table, sender, target, note, recv, counts, w_out, vectors, w_hbm, edges_hbm, cot_hbm,
+    table, sender, target, note, recv, counts, w_out, vectors, edges, edge_cot, w_hbm,
     new_edges, packed, compact,
-    w_in, edges, edge_cot, sems,
+    w_in, sems,
 ):
     slots, width = edges.shape
     group = table.shape[0]
     per_block = slots // counts.shape[1]
-    edges_copy = pltpu.make_async_copy(edges_hbm, edges, sems.at[0])
-    cot_copy = pltpu.make_async_copy(cot_hbm, edge_cot, sems.at[1])
     w_copies = [
         pltpu.make_async_copy(
-            w_hbm.at[pl.ds(part * width, width), :], w_in.at[pl.ds(part * width, width), :], sems.at[2 + part]
+            w_hbm.at[pl.ds(part * width, width), :], w_in.at[pl.ds(part * width, width), :], sems.at[part]
         )
         for part in range(3)
     ]
-    for copy in (w_copies[1], w_copies[2], edges_copy, w_copies[0], cot_copy):
+    for copy in (w_copies[1], w_copies[2], w_copies[0]):
         copy.start()
     b_in, b_out = vectors[0:1, :], vectors[1:2, :]
     gain, bias = vectors[2:3, :], vectors[3:4, :]
@@ -106,11 +104,15 @@
     lane = lax.broadcasted_iota(jnp.int32, (slots, group), 1)
     chosen = jnp.where(pick == lane, 1.0, 0.0).astype(jnp.bfloat16)
     send_feat = dot(chosen, table[...]).astype(jnp.bfloat16)
+    cot = edge_cot[...].astype(jnp.float32) + recv[:, width:].astype(jnp.float32)
+    scaled = jnp.where(alive, cot, 0.0) * gain
+    scaled_mean = jnp.mean(scaled, axis=1, keepdims=True)
+    row = lax.broadcasted_iota(jnp.int32, (compact.shape[0], slots), 0)
+    returning = jnp.where(target[...] == row, 1.0, 0.0).astype(jnp.bfloat16)
     w_copies[1].wait()
     pre = dot(send_feat, w_in[width : 2 * width, :])
     w_copies[2].wait()
     pre += dot(recv[:, :width], w_in[2 * width :, :])
-    edges_copy.wait()
     w_copies[0].wait()
     pre += dot(edges[...], w_in[:width, :])
     pre += b_in
@@ -123,20 +125,15 @@
     message = jnp.where(alive, normed * gain + bias, 0.0).astype(jnp.bfloat16)
     packed[:, :width] = message
     new_edges[...] = (edges[...].astype(jnp.float32) + message.astype(jnp.float32)).astype(jnp.bfloat16)
-    cot_copy.wait()
-    cot = edge_cot[...].astype(jnp.float32) + recv[:, width:].astype(jnp.float32)
-    scaled = jnp.where(alive, cot, 0.0) * gain
     d_outer = inv_std * (
         scaled
-        - jnp.mean(scaled, axis=1, keepdims=True)
+        - scaled_mean
         - normed * jnp.mean(scaled * normed, axis=1, keepdims=True)
     )
     d_hidden = dot_t(d_outer.astype(jnp.bfloat16), w_out[...])
     d_pre = (d_hidden * sigma * (1.0 + pre * (1.0 - sigma))).astype(jnp.bfloat16)
     packed[:, width:] = d_pre
-    row = lax.broadcasted_iota(jnp.int32, (compact.shape[0], slots), 0)
-    chosen = jnp.where(target[...] == row, 1.0, 0.0).astype(jnp.bfloat16)
-    compact[...] = (dot(chosen, d_pre) + note[...].astype(jnp.float32)).astype(jnp.bfloat16)
+    compact[...] = (dot(returning, d_pre) + note[...].astype(jnp.float32)).astype(jnp.bfloat16)
 
 
 def dense_kernel(packed, place, partial):
@@ -252,7 +249,7 @@
 
     new_edges, packed, compact = pl.pallas_call(
         edge_kernel,
-        in_specs=[VMEM] * 8 + [ANY] * 3,
+        in_specs=[VMEM] * 10 + [ANY],
         out_specs=[VMEM] * 3,
         out_shape=[
             jax.ShapeDtypeStruct((slots, width), jnp.bfloat16),
@@ -261,9 +258,7 @@
         ],
         scratch_shapes=[
             pltpu.VMEM((3 * width, width), jnp.bfloat16),
-            pltpu.VMEM((slots, width), jnp.bfloat16),
-            pltpu.VMEM((slots, width), jnp.bfloat16),
-            pltpu.SemaphoreType.DMA((5,)),
+            pltpu.SemaphoreType.DMA((3,)),
         ],
         compiler_params=pltpu.CompilerParams(vmem_limit_bytes=50 * 1024 * 1024),
         cost_estimate=pl.CostEstimate(
@@ -273,7 +268,7 @@
         ),
     )(
         table, place, target, note, recv, edge_count, w_out, vectors,
-        w_in, edge_latents, edge_cotangent,
+        edge_latents, edge_cotangent, w_in,
     )
 
     arrived = lax.all_to_all(compact, "col", 0, 0, tiled=True, axis_index_groups=along_y)

time: 120 us -> 119 us (level)
  no operation moved by 1% of the time
where the time goes in v9:
time: 119 us
  starting transfers between devices  54.3 us (46%)
  blocking collectives  38.6 us (32%)
  waiting for transfers between devices  10.5 us (9%)
  Pallas kernels  7.48 us (6%)
  local copies, waits for them, and re-layouts  3.53 us (3%)
  matrix products  1.99 us (2%)
  between operations  1.55 us (1%)
    all_gather x1, blocking collectives, on_device(): lax.all_gather(column, 'col', axis=0, tiled=True, axis_index_groups=along_y)  23.2 us
    all_to_all x1, blocking collectives, on_device(): lax.all_to_all(compact, 'col', 0, 0, tiled=True, axis_index_groups=along_y)  15.4 us
    all_to_all x1, starting transfers between devices, on_device(): returned = lax.all_to_all(packed, 'row', 0, 0, tiled=True)  14.2 us
    ppermute x1, starting transfers between devices, on_device(): from_below = lax.ppermute(node_latents, 'col', up)  10.6 us
    ppermute x1, waiting for transfers between devices, on_device(): to_above = lax.ppermute(away[2 * owned:], 'col', up)  9.32 us
    all_to_all x1, starting transfers between devices, on_device(): asked = lax.all_to_all(indices, 'row', 0, 0, tiled=True)  8.28 us
    all_to_all x1, starting transfers between devices, on_device(): recv = lax.all_to_all(answer, 'row', 0, 0, tiled=True)  7.09 us
    ppermute x1, starting transfers between devices, on_device(): to_above = lax.ppermute(away[2 * owned:], 'col', up)  6.31 us
  transfers between devices with their start and end apart: 7, of which 2 were waited for; matrix products, arithmetic and copies ran while one was open for 3% of the time, Pallas kernels for 1%

profile of v9, /device:TPU:69, one launch (start us, length us, event | category | flops | bytes accessed | tf_op | source)
XLA Modules:
  0.0 118.7 jit_solution(17687364135988923137)
XLA Ops:
  0.6 10.6 %collective-permute-start = (bf16[32,512]{1,0:T(8,128)(2,1)}, bf16[32,512]{1,0:T(8,128)(2,1)S(1)}, u32[]{:S(2)}, u32[]{:S(2)}) collective-permute-start(bf16[32,512]{1,0:T(8,128)(2,1)} %nodes.1), channel_id=1, source_target_pairs={{0,1},{1,2},{2,0},{3,4},{4,5},{5,3},{6,7},{7,8},{8,6},{9,10},{10,1... | collective-permute-start | bytes 98312 | tf_op jit(solution)/shard_map/ppermute | solution.py:228
  11.3 4.7 %collective-permute-start.1 = (bf16[32,512]{1,0:T(8,128)(2,1)}, bf16[32,512]{1,0:T(8,128)(2,1)S(1)}, u32[]{:S(2)}, u32[]{:S(2)}) collective-permute-start(bf16[32,512]{1,0:T(8,128)(2,1)} %nodes.1), channel_id=1, source_target_pairs={{1,0},{2,1},{0,2},{4,3},{5,4},{3,5},{7,6},{8,7},{6,8},{10,9},{11,1... | collective-permute-start | bytes 98312 | tf_op jit(solution)/shard_map/ppermute | solution.py:229
  15.9 1.3 %broadcast_in_dim.2 = s32[32,1,256]{2,1,0:T(1,128)} broadcast(s32[256]{0:T(256)} %param.18), dimensions={2} | broadcast | bytes 33792 | tf_op jit(solution)/shard_map/broadcast_in_dim | solution.py:231
  17.3 8.3 %all-to-all-start.1 = ((s32[32,1,256]{2,1,0:T(1,128)}), s32[32,1,256]{2,1,0:T(1,128)S(1)}, u32[]{:S(2)}, u32[]{:S(2)}) async-start(s32[32,1,256]{2,1,0:T(1,128)} %broadcast_in_dim.2), calls=%async_computation.1 | async-start | bytes 65536 | tf_op jit(solution)/shard_map/all_to_all | solution.py:232
  25.6 0.7 fusion.6
  26.3 0.0 copy-start.4
  26.3 0.7 copy-done.4
  27.0 0.0 copy-start.6
  27.1 0.7 copy-done.6
  27.7 0.0 copy-start.8
  27.7 0.8 copy-done.8
  28.5 0.6 shard_map.156
  29.0 1.2 %all-to-all-done.1.asked = s32[32,1,256]{2,1,0:T(1,128)S(1)} async-done(((s32[32,1,256]{2,1,0:T(1,128)}), s32[32,1,256]{2,1,0:T(1,128)S(1)}, u32[]{:S(2)}, u32[]{:S(2)}) %all-to-all-start.1) | async-done | bytes 32800 | tf_op jit(solution)/shard_map/all_to_all | solution.py:232
  30.2 0.0 copy-start.9
  30.2 0.0 copy-start.10
  30.2 0.0 copy-start.11
  30.2 0.0 copy-start.12
  30.3 0.0 copy-start.5
  30.3 1.2 %shard_map.157 = bf16[256,1024]{1,0:T(8,128)(2,1)} custom-call(s32[32,1,256]{2,1,0:T(1,128)S(1)} %all-to-all-done.1.asked, s32[1,1]{1,0:T(1,128)} %bitcast.1.my_row, bf16[32,1024]{1,0:T(8,128)(2,1)S(1)} %get-tuple-element.31.own), custom_call_target="tpu_custom_call" | custom-call | flops 4000000000 | bytes 655360 | tf_op jit(solution)/shard_map/pallas_call | solution.py:233
  31.5 0.0 copy-start.1
  31.5 0.0 copy-start.2
  31.5 0.0 collective-permute-done
  31.5 0.0 collective-permute-done.1
  31.5 7.1 %all-to-all-start.2 = ((bf16[32,8,1024]{2,1,0:T(8,128)(2,1)}), bf16[32,8,1024]{2,1,0:T(8,128)(2,1)S(1)}, u32[]{:S(2)}, u32[]{:S(2)}) async-start(bf16[32,8,1024]{2,1,0:T(8,128)(2,1)} %bitcast.3), calls=%async_computation.2 | async-start | bytes 1048576 | tf_op jit(solution)/shard_map/all_to_all | solution.py:244
  38.6 0.0 copy-done.9
  38.6 0.0 copy-done.10
  38.6 0.0 copy-done.11
  38.6 0.0 copy-done.12
  38.6 0.0 copy-done.5
  38.7 23.2 %all_gather.3.table = bf16[768,512]{1,0:T(8,128)(2,1)S(1)} all-gather(bf16[96,512]{1,0:T(8,128)(2,1)S(1)} %pad_maximum_fusion), channel_id=1, replica_groups={{0,3,6,9,12,15,18,21},{1,4,7,10,13,16,19,22},{2,5,8,11,14,17,20,23},{24..., dimensions={0}, use_global_device_ids=true | all-gather | bytes 884736 | tf_op jit(solution)/shard_map/all_gather | solution.py:246
  61.8 0.0 all-to-all-done.2
  61.8 0.0 copy-done.1
  61.8 0.0 copy-done.2
  61.8 0.0 copy-done.3
  61.9 0.0 copy-done.7
  61.9 3.6 %shard_map.158 = (bf16[256,512]{1,0:T(8,128)(2,1)}, bf16[256,1024]{1,0:T(8,128)(2,1)}, bf16[384,512]{1,0:T(8,128)(2,1)S(1)}) custom-call(bf16[768,512]{1,0:T(8,128)(2,1)S(1)} %all_gather.3.table, s32[1,256]{1,0:T(1,128)S(1)} %bitcast.20, s32[1,256]{1,0:T(1,128)S(1)} %get-tuple-element.34.target, bf16[384,512]{1,0:T(8,128)(2,1)S(1)} %get-tuple-element.35.note, ...), custom_call_target="tpu_custom_call" | custom-call | flops 1073741824 | bytes 6291456 | tf_op jit(solution)/shard_map/pallas_call | solution.py:250
  65.5 15.4 %all_to_all.46 = bf16[8,48,512]{2,1,0:T(8,128)(2,1)S(1)} all-to-all(bf16[8,48,512]{2,1,0:T(8,128)(2,1)S(1)} %bitcast.18), channel_id=1, replica_groups={{0,3,6,9,12,15,18,21},{1,4,7,10,13,16,19,22},{2,5,8,11,14,17,20,23},{24..., dimensions={0} | all-to-all | bytes 786432 | tf_op jit(solution)/shard_map/all_to_all | solution.py:274
  80.9 0.8 shard_map.159
  82.3 0.0 copy-start
  82.3 14.2 %all-to-all-start.3 = ((bf16[32,8,1024]{2,1,0:T(8,128)(2,1)}), bf16[32,8,1024]{2,1,0:T(8,128)(2,1)S(1)}, u32[]{:S(2)}, u32[]{:S(2)}) async-start(bf16[32,8,1024]{2,1,0:T(8,128)(2,1)} %bitcast.9), calls=%async_computation.3 | async-start | bytes 1048576 | tf_op jit(solution)/shard_map/all_to_all | solution.py:302
  96.6 6.3 %collective-permute-start.3 = (bf16[32,512]{1,0:T(8,128)(2,1)S(1)}, bf16[32,512]{1,0:T(8,128)(2,1)S(1)}, u32[]{:S(2)}, u32[]{:S(2)}) collective-permute-start(bf16[32,512]{1,0:T(8,128)(2,1)S(1)} %get-tuple-element.45), channel_id=1, source_target_pairs={{0,1},{1,2},{2,0},{3,4},{4,5},{5,3},{6,7},{7,8},{8,6},{9,10},{10,1... | collective-permute-start | bytes 98312 | tf_op jit(solution)/shard_map/ppermute | solution.py:300
  102.9 3.2 %collective-permute-start.2 = (bf16[32,512]{1,0:T(8,128)(2,1)S(1)}, bf16[32,512]{1,0:T(8,128)(2,1)S(1)}, u32[]{:S(2)}, u32[]{:S(2)}) collective-permute-start(bf16[32,512]{1,0:T(8,128)(2,1)S(1)} %get-tuple-element.46), channel_id=1, source_target_pairs={{1,0},{2,1},{0,2},{4,3},{5,4},{3,5},{7,6},{8,7},{6,8},{10,9},{11,1... | collective-permute-start | bytes 98312 | tf_op jit(solution)/shard_map/ppermute | solution.py:299
  106.1 0.0 copy-done
  106.1 2.0 %fusion = bf16[256,512]{1,0:T(8,128)(2,1)} fusion(bf16[1536,512]{1,0:T(8,128)(2,1)S(1)} %copy-done, bf16[256,512]{1,0:T(8,128)(2,1)S(1)} %copy-done.3, bf16[256,1024]{1,0:T(8,128)(2,1)} %get-tuple-element.38), kind=kOutput, calls=%fused_computation.2 | convolution fusion | flops 134610944 | bytes 1310720 | tf_op jit(solution)/shard_map/dot_general | solution.py:19
  108.1 9.3 %collective-permute-done.3.to_above = bf16[32,512]{1,0:T(8,128)(2,1)S(1)} collective-permute-done((bf16[32,512]{1,0:T(8,128)(2,1)S(1)}, bf16[32,512]{1,0:T(8,128)(2,1)S(1)}, u32[]{:S(2)}, u32[]{:S(2)}) %collective-permute-start.3) | collective-permute-done | bytes 32800 | tf_op jit(solution)/shard_map/ppermute | solution.py:300
  117.4 0.0 collective-permute-done.2.to_below
  117.4 0.0 all-to-all-done.3
  117.4 1.3 %shard_map.160 = (bf16[32,512]{1,0:T(8,128)(2,1)}, bf16[32,512]{1,0:T(8,128)(2,1)}) custom-call(s32[32,1,256]{2,1,0:T(1,128)S(1)} %all-to-all-done.1.asked, s32[1,1]{1,0:T(1,128)} %bitcast.1.my_row, bf16[256,1024]{1,0:T(8,128)(2,1)S(1)} %bitcast.15, f32[96,512]{1,0:T(8,128)S(1)} %get-tuple-element.47.column_sum, ...), custom_call_target="tpu_custom_call" | custom-call | flops 50331648 | bytes 2097152 | tf_op jit(solution)/shard_map/pallas_call | solution.py:303
  (7 shorter events, 0.1 us)
Async XLA Ops:
  0.6 30.8 %collective-permute-start = (bf16[32,512]{1,0:T(8,128)(2,1)}, bf16[32,512]{1,0:T(8,128)(2,1)S(1)}, u32[]{:S(2)}, u32[]{:S(2)}) collective-permute-start(bf16[32,512]{1,0:T(8,128)(2,1)} %nodes.1), channel_id=1, source_target_pairs={{0,1},{1,2},{2,0},{3,4},{4,5},{5,3},{6,7},{7,8},{8,6},{9,10},{10,1... | collective-permute-start | bytes 98312 | tf_op jit(solution)/shard_map/ppermute | solution.py:228
  11.3 20.2 %collective-permute-start.1 = (bf16[32,512]{1,0:T(8,128)(2,1)}, bf16[32,512]{1,0:T(8,128)(2,1)S(1)}, u32[]{:S(2)}, u32[]{:S(2)}) collective-permute-start(bf16[32,512]{1,0:T(8,128)(2,1)} %nodes.1), channel_id=1, source_target_pairs={{1,0},{2,1},{0,2},{4,3},{5,4},{3,5},{7,6},{8,7},{6,8},{10,9},{11,1... | collective-permute-start | bytes 98312 | tf_op jit(solution)/shard_map/ppermute | solution.py:229
  17.3 13.0 %all-to-all-start.1 = ((s32[32,1,256]{2,1,0:T(1,128)}), s32[32,1,256]{2,1,0:T(1,128)S(1)}, u32[]{:S(2)}, u32[]{:S(2)}) async-start(s32[32,1,256]{2,1,0:T(1,128)} %broadcast_in_dim.2), calls=%async_computation.1 | async-start | bytes 65536 | tf_op jit(solution)/shard_map/all_to_all | solution.py:232
  26.3 0.8 copy-start.4
  27.0 0.7 copy-start.6
  27.7 0.8 copy-start.8
  30.2 8.3 %copy-start.9 = (f32[512]{0:T(512)S(1)}, f32[512]{0:T(512)}, u32[]{:S(2)}) copy-start(f32[512]{0:T(512)} %param.25) | copy-start | bytes 6148
  30.2 8.4 %copy-start.10 = (f32[512]{0:T(512)S(1)}, f32[512]{0:T(512)}, u32[]{:S(2)}) copy-start(f32[512]{0:T(512)} %param.24) | copy-start | bytes 6148
  30.2 8.4 %copy-start.11 = (f32[512]{0:T(512)S(1)}, f32[512]{0:T(512)}, u32[]{:S(2)}) copy-start(f32[512]{0:T(512)} %param.23) | copy-start | bytes 6148
  30.2 8.4 %copy-start.12 = (f32[512]{0:T(512)S(1)}, f32[512]{0:T(512)}, u32[]{:S(2)}) copy-start(f32[512]{0:T(512)} %param.21) | copy-start | bytes 6148
  30.3 8.4 %copy-start.5 = (bf16[32,512]{1,0:T(8,128)(2,1)S(1)}, bf16[32,512]{1,0:T(8,128)(2,1)}, u32[]{:S(2)}) copy-start(bf16[32,512]{1,0:T(8,128)(2,1)} %nodes.1) | copy-start | bytes 98308
  31.5 30.4 %copy-start.1 = (bf16[512,512]{1,0:T(8,128)(2,1)S(1)}, bf16[512,512]{1,0:T(8,128)(2,1)}, u32[]{:S(2)}) copy-start(bf16[512,512]{1,0:T(8,128)(2,1)} %w_out.1) | copy-start | bytes 1572868
  31.5 30.4 %copy-start.2 = (bf16[256,512]{1,0:T(8,128)(2,1)S(1)}, bf16[256,512]{1,0:T(8,128)(2,1)}, u32[]{:S(2)}) copy-start(bf16[256,512]{1,0:T(8,128)(2,1)} %edges.1) | copy-start | bytes 786436
  31.5 30.4 %copy-start.3 = (bf16[256,512]{1,0:T(8,128)(2,1)S(1)}, bf16[256,512]{1,0:T(8,128)(2,1)}, u32[]{:S(2)}) copy-start(bf16[256,512]{1,0:T(8,128)(2,1)} %edge_cot.1) | copy-start | bytes 786436
  31.5 30.4 %copy-start.7 = (s32[1,32]{1,0:T(1,128)S(1)}, s32[1,32]{1,0:T(1,128)}, u32[]{:S(2)}) copy-start(s32[1,32]{1,0:T(1,128)} %counts.3) | copy-start | bytes 388
  31.5 30.3 %all-to-all-start.2 = ((bf16[32,8,1024]{2,1,0:T(8,128)(2,1)}), bf16[32,8,1024]{2,1,0:T(8,128)(2,1)S(1)}, u32[]{:S(2)}, u32[]{:S(2)}) async-start(bf16[32,8,1024]{2,1,0:T(8,128)(2,1)} %bitcast.3), calls=%async_computation.2 | async-start | bytes 1048576 | tf_op jit(solution)/shard_map/all_to_all | solution.py:244
  82.3 23.8 %copy-start = (bf16[1536,512]{1,0:T(8,128)(2,1)S(1)}, bf16[1536,512]{1,0:T(8,128)(2,1)}, u32[]{:S(2)}) copy-start(bf16[1536,512]{1,0:T(8,128)(2,1)} %w_in.1) | copy-start | bytes 4718596
  82.3 35.1 %all-to-all-start.3 = ((bf16[32,8,1024]{2,1,0:T(8,128)(2,1)}), bf16[32,8,1024]{2,1,0:T(8,128)(2,1)S(1)}, u32[]{:S(2)}, u32[]{:S(2)}) async-start(bf16[32,8,1024]{2,1,0:T(8,128)(2,1)} %bitcast.9), calls=%async_computation.3 | async-start | bytes 1048576 | tf_op jit(solution)/shard_map/all_to_all | solution.py:302
  96.6 20.8 %collective-permute-start.3 = (bf16[32,512]{1,0:T(8,128)(2,1)S(1)}, bf16[32,512]{1,0:T(8,128)(2,1)S(1)}, u32[]{:S(2)}, u32[]{:S(2)}) collective-permute-start(bf16[32,512]{1,0:T(8,128)(2,1)S(1)} %get-tuple-element.45), channel_id=1, source_target_pairs={{0,1},{1,2},{2,0},{3,4},{4,5},{5,3},{6,7},{7,8},{8,6},{9,10},{10,1... | collective-permute-start | bytes 98312 | tf_op jit(solution)/shard_map/ppermute | solution.py:300
  102.9 14.5 %collective-permute-start.2 = (bf16[32,512]{1,0:T(8,128)(2,1)S(1)}, bf16[32,512]{1,0:T(8,128)(2,1)S(1)}, u32[]{:S(2)}, u32[]{:S(2)}) collective-permute-start(bf16[32,512]{1,0:T(8,128)(2,1)S(1)} %get-tuple-element.46), channel_id=1, source_target_pairs={{1,0},{2,1},{0,2},{4,3},{5,4},{3,5},{7,6},{8,7},{6,8},{10,9},{11,1... | collective-permute-start | bytes 98312 | tf_op jit(solution)/shard_map/ppermute | solution.py:299
